TPU v7x, 128 devices: a whole 4x4x4 slice. The times are simulated.
128 devices in a mesh: sample: 8 (over x_lo, z), head: 16 (over x_hi, y, core).
Axes of the slice: x: 4 (x_hi: 2, x_lo: 2; x = x_hi * 2 + x_lo), y: 4, z: 4, core: 2. Of those that a mesh axis runs over, the one named last changes fastest.
Arguments:
- queries: bfloat16 [8, 2048, 8192], P('sample', 'head'), may hold values from -200 to 200
- image_tokens: bfloat16 [8, 1664, 7680], P('sample', None, 'head'), may hold values from -6 to 6
- kv_weight: bfloat16 [7680, 8, 2, 128], P('head', 'sample'), may hold values from -0.0625 to 0.0625
- attn_gate: float32 [1], replicated, may hold values from 0.3 to 1.5
- image_counts: int32 [8], P('sample'), may hold values from 832 to 1664, as said below
- response_lengths: int32 [8], P('sample'), may hold values from 512 to 2048, as said below
Outputs:
- gated: bfloat16 [8, 2048, 8192], P('sample', 'head')
Inputs may be any that keep to these rules, and one draw needn't show every extreme that they name: `image_counts`: in every draw at least one sample has all 1664 slots filled. `response_lengths`: in every draw at least one sample has all 2048 tokens.
All inputs are finite; a program needn't handle non-finite values.
Results may differ from a plain program's by a relative error of at most 0.01.
Values may be sent and summed in bfloat16 or wider, within the bound.
No kernel may reach another device: no remote copies, remote signals or barrier semaphores. Data moves between devices by JAX's collectives and lax.ppermute only.
A program may use at most 128 MiB of HBM per device.

v0:
```python
import jax
import jax.numpy as jnp
from jax import lax
from jax.sharding import PartitionSpec as P


def from_partner(value, axis, apart):
    return lax.ppermute(value, axis, [(i, i ^ 1 << apart) for i in range(lax.axis_size(axis))])


def attend(query_rows, key_cols, value_cols, keep_keys):
    total_rows = query_rows.shape[0]
    head_size = query_rows.shape[1]
    block_size = 1024
    scale_factor = head_size ** (-0.5)

    def one_block(block_rows):
        scores = jnp.dot(block_rows, key_cols, preferred_element_type=jnp.float32) * scale_factor
        scores = jnp.where(keep_keys[None, :], scores, -1e30)
        top_score = jnp.max(scores, axis=1, keepdims=True)
        exponent = jnp.exp(scores - top_score)
        denominator = jnp.sum(exponent, axis=1, keepdims=True)
        weights = exponent.astype(jnp.bfloat16)
        mixed_rows = lax.dot_general(
            weights, value_cols, (((1,), (1,)), ((), ())), preferred_element_type=jnp.float32
        )
        return mixed_rows / denominator

    blocked = query_rows.reshape(total_rows // block_size, block_size, head_size)
    return lax.map(one_block, blocked).reshape(total_rows, head_size)


def on_device(queries, image_tokens, kv_weight, attn_gate, image_counts, response_lengths):
    sample_count = queries.shape[0]
    local_rows = queries.shape[1]
    image_len = image_tokens.shape[1]
    part_width = image_tokens.shape[2]
    head_dim = kv_weight.shape[3]
    gathered = lax.all_gather(kv_weight, "sample", axis=1, tiled=True)
    kv_heads = gathered.shape[1]
    kv_width = kv_heads * 2 * head_dim
    flat_weight = gathered.reshape(part_width, kv_width)
    flat_image = image_tokens.reshape(sample_count * image_len, part_width)
    keep_keys = jnp.arange(image_len, dtype=jnp.int32)[None, :] < image_counts[:, None]
    positions = lax.axis_index("head") * local_rows + jnp.arange(local_rows, dtype=jnp.int32)
    live_rows = positions[None, :] < response_lengths[:, None]
    own_share = lax.psum_scatter(
        lax.dot_general(
            flat_weight, flat_image, (((0,), (1,)), ((), ())), preferred_element_type=jnp.float32
        ),
        "head",
        scatter_dimension=0,
        tiled=True,
    ).astype(jnp.bfloat16)
    partner = from_partner(own_share, "head", 0)
    is_even = lax.axis_index("head") % 2 == 0
    key_all = jnp.where(is_even, own_share, partner)
    value_all = jnp.where(is_even, partner, own_share)
    local_q = lax.all_to_all(queries, "head", split_axis=2, concat_axis=1, tiled=True)
    seq_len = local_q.shape[1]
    per_device = local_q.shape[2] // head_dim

    def one_sample(sample_index):
        query_rows = lax.dynamic_index_in_dim(local_q, sample_index, 0, keepdims=False).reshape(
            seq_len * per_device, head_dim
        )
        keep_now = lax.dynamic_index_in_dim(keep_keys, sample_index, 0, keepdims=False)
        result_rows = attend(query_rows, key_all, value_all, keep_now)
        return result_rows.astype(jnp.bfloat16).reshape(seq_len, per_device * head_dim)

    local_out = lax.map(one_sample, jnp.arange(sample_count, dtype=jnp.int32))
    attention = lax.all_to_all(local_out, "head", split_axis=1, concat_axis=2, tiled=True)
    gate_value = jnp.tanh(attn_gate[0])
    gated_rows = jnp.where(live_rows[:, :, None], gate_value * attention.astype(jnp.float32), 0.0)
    return gated_rows.astype(jnp.bfloat16)


def solution(mesh):
    placed = (
        P("sample", "head", None),
        P("sample", None, "head"),
        P("head", "sample", None, None),
        P(),
        P("sample"),
        P("sample"),
    )
    return jax.shard_map(
        on_device, mesh=mesh, in_specs=placed, out_specs=P("sample", "head", None), check_vma=False
    )
```

profile of v0, /device:TPU:1, one launch (start us, length us, event | category | flops | bytes accessed | tf_op | source)
XLA Modules:
  0.0 412.2 jit_solution(5897830298923233646)
XLA Ops:
  7.3 60.4 %all-gather.2.cloned.1.call-done = bf16[480,8,2,128]{3,2,1,0:T(2,128)(2,1)} async-done(((bf16[480,1,2,128]{3,2,1,0:T(2,128)(2,1)}), bf16[480,8,2,128]{3,2,1,0:T(2,128)(2,1)}) %all-gather.2.cloned.1.call-update) | async-done | bytes 1966096 | tf_op jit(solution)/shard_map/all_gather | solution.py:39
  67.7 5.5 %reshape.100 = bf16[480,2048]{1,0:T(8,128)(2,1)} reshape(bf16[480,8,2,128]{3,2,1,0:T(2,128)(2,1)} %all-gather.2.cloned.1.call-done) | data formatting | bytes 3932160 | tf_op jit(solution)/shard_map/reshape | solution.py:42
  73.3 9.0 %fusion.24 = f32[2048,1664]{1,0:T(8,128)} fusion(bf16[480,2048]{1,0:T(8,128)(2,1)} %reshape.100, bf16[1,1664,480]{1,2,0:T(8,128)(2,1)S(1)} %copy-done), kind=kOutput, calls=%fused_computation.21 | convolution fusion | flops 3271557120 | bytes 17195008 | tf_op jit(solution)/shard_map/dot_general | solution.py:48
  82.3 9.5 %copy.22 = bf16[1,128,8192]{1,0,2:T(2,128)(2,1)} copy(bf16[1,128,8192]{2,1,0:T(8,128)(2,1)} %param.8) | data formatting | bytes 4194304 | tf_op args[0]
  92.4 46.5 %reduce = bf16[8192,128]{1,0:T(8,128)(2,1)} reduce(bf16[8192,1,128]{2,1,0:T(2,128)(2,1)} %bitcast.43, bf16[]{:T(256)} %broadcast.78), dimensions={1}, to_apply=%bitcast.25.reduce_sub_computation | reduce | bytes 4194306
  138.8 4.0 reshape.102
  142.8 8.9 %all-to-all-start = ((bf16[16,2,32768]{2,1,0:T(2,128)(2,1)}), bf16[16,2,32768]{2,1,0:T(2,128)(2,1)}, u32[]{:S(2)}, u32[]{:S(2)}) async-start(bf16[16,2,32768]{2,1,0:T(2,128)(2,1)} %reshape.102), calls=%async_computation | async-start | bytes 4194304 | tf_op jit(solution)/shard_map/all_to_all | solution.py:59
  151.7 79.8 %reduce-scatter.2.cloned.1.call-done = f32[128,1664]{1,0:T(8,128)} async-done(((f32[2048,1664]{1,0:T(8,128)}), f32[128,1664]{1,0:T(8,128)}) %reduce-scatter.2.cloned.1.call-update) | async-done | bytes 851984 | tf_op jit(solution)/shard_map/reduce_scatter | solution.py:47
  232.7 1.6 collective-permute-start
  234.3 10.4 %reshape.103 = bf16[8192,1,128]{2,1,0:T(2,128)(2,1)} reshape(bf16[16,2,32768]{2,1,0:T(2,128)(2,1)} %all-to-all-done) | data formatting | bytes 4194304
  244.8 3.8 copy.28
  248.5 3.9 copy.23
  252.4 4.4 %reshape.99 = bf16[8,1024,128]{2,1,0:T(8,128)(2,1)} reshape(bf16[1,16,128,512]{3,2,1,0:T(8,128)(2,1)} %copy.23) | data formatting | bytes 4194304 | tf_op jit(solution)/shard_map/while/body/eval_jaxpr/reshape;while/body/eval_jaxpr/reshape | solution.py:29
  257.0 57.2 %while.18 = (s32[]{:T(128)}, bf16[8,1024,128]{2,1,0:T(8,128)(2,1)}, bf16[8,1024,128]{2,1,0:T(8,128)(2,1)}, bf16[128,1664]{1,0:T(8,128)(2,1)S(1)}, bf16[128,1664]{1,0:T(8,128)(2,1)S(1)}, /*index=5*/s32[]{:T(128)}, s32[]{:T(128)}) while((s32[]{:T(128)}, bf16[8,1024,128]{2,1,0:T(8,128)(2,1)}, bf16[8,1024,128]{2,1,0:T(8,128)(2,1)}, ...), condition=%wide.region_4.5_spmd.clone, body=%wide.region_1.4_spmd.clone.sunk | while | flops 891289216 | bytes 22113872 | solution.py:30
  257.7 2.3 fusion.38
  260.0 1.5 fusion.39
  261.4 2.7 fusion.40
  264.8 2.3 fusion.38
  267.1 1.5 fusion.39
  268.6 2.7 fusion.40
  272.0 2.3 fusion.38
  274.3 1.5 fusion.39
  275.7 2.7 fusion.40
  279.1 2.3 fusion.38
  281.4 1.5 fusion.39
  282.9 2.7 fusion.40
  286.3 2.3 fusion.38
  288.6 1.5 fusion.39
  290.0 2.7 fusion.40
  293.4 2.3 fusion.38
  295.7 1.5 fusion.39
  297.2 2.7 fusion.40
  300.6 2.3 fusion.38
  302.9 1.5 fusion.39
  304.4 2.7 fusion.40
  307.7 2.3 fusion.38
  310.0 1.5 fusion.39
  311.5 2.7 fusion.40
  314.2 12.5 %convert_element_type.51 = bf16[1,2048,512]{2,0,1:T(2,128)(2,1)} reshape(bf16[8,1024,128]{2,1,0:T(8,128)(2,1)} %get-tuple-element.55) | data formatting | bytes 4194304 | tf_op jit(solution)/shard_map/while/body/eval_jaxpr/convert_element_type | solution.py:69
  326.7 15.4 %reduce.1 = bf16[2048,512]{1,0:T(8,128)(2,1)} reduce(bf16[2048,1,512]{2,1,0:T(2,128)(2,1)} %bitcast.44, bf16[]{:T(256)} %broadcast.78), dimensions={1}, to_apply=%bitcast.27.reduce_sub_computation | reduce | bytes 4194306
  342.1 4.5 %reshape.104 = bf16[16,2,32768]{2,1,0:T(2,128)(2,1)} reshape(bf16[2048,512]{1,0:T(8,128)(2,1)} %reduce.1) | data formatting | bytes 4194304
  346.6 4.3 %all-to-all-start.1 = ((bf16[16,2,32768]{2,1,0:T(2,128)(2,1)}), bf16[16,2,32768]{2,1,0:T(2,128)(2,1)}, u32[]{:S(2)}, u32[]{:S(2)}) async-start(bf16[16,2,32768]{2,1,0:T(2,128)(2,1)} %reshape.104), calls=%async_computation.2 | async-start | bytes 4194304 | tf_op jit(solution)/shard_map/all_to_all | solution.py:72
  352.3 27.2 %all-to-all-done.1 = bf16[16,2,32768]{2,1,0:T(2,128)(2,1)} async-done(((bf16[16,2,32768]{2,1,0:T(2,128)(2,1)}), bf16[16,2,32768]{2,1,0:T(2,128)(2,1)}, u32[]{:S(2)}, u32[]{:S(2)}) %all-to-all-start.1) | async-done | bytes 2097184 | tf_op jit(solution)/shard_map/all_to_all | solution.py:72
  379.5 10.4 %reshape.105 = bf16[2048,1,512]{2,1,0:T(2,128)(2,1)} reshape(bf16[16,2,32768]{2,1,0:T(2,128)(2,1)} %all-to-all-done.1) | data formatting | bytes 4194304
  389.9 4.1 convert_multiply_fusion
  394.0 3.9 copy.26
  397.9 3.4 fusion.23
  401.3 4.1 copy.27
  (25 shorter events, 7.8 us)
Async XLA Ops:
  6.5 66.7 %copy-start = (bf16[1,1664,480]{1,2,0:T(8,128)(2,1)S(1)}, bf16[1,1664,480]{1,2,0:T(8,128)(2,1)}, u32[]{:S(2)}) copy-start(bf16[1,1664,480]{1,2,0:T(8,128)(2,1)} %param.9) | copy-start | bytes 4792324
  6.5 61.2 %all-gather.2.cloned.1.call-start = ((), (), s32[]{:S(2)}) async-start(), calls=%async_computation.3 | async-start | bytes 2211840 | tf_op jit(solution)/shard_map/all_gather | solution.py:39
  7.3 224.3 %reduce-scatter.2.cloned.1.call-start = ((), (), s32[]{:S(2)}) async-start(), calls=%async_computation.4 | async-start | bytes 14483456 | tf_op jit(solution)/shard_map/reduce_scatter | solution.py:47
  142.8 91.5 %all-to-all-start = ((bf16[16,2,32768]{2,1,0:T(2,128)(2,1)}), bf16[16,2,32768]{2,1,0:T(2,128)(2,1)}, u32[]{:S(2)}, u32[]{:S(2)}) async-start(bf16[16,2,32768]{2,1,0:T(2,128)(2,1)} %reshape.102), calls=%async_computation | async-start | bytes 4194304 | tf_op jit(solution)/shard_map/all_to_all | solution.py:59
  232.7 24.1 %collective-permute-start = (bf16[128,1664]{1,0:T(8,128)(2,1)S(1)}, bf16[128,1664]{1,0:T(8,128)(2,1)S(1)}, u32[]{:S(2)}, u32[]{:S(2)}) collective-permute-start(bf16[128,1664]{1,0:T(8,128)(2,1)S(1)} %convert_element_type.45), channel_id=1, source_target_pairs={{0,1},{1,0},{2,3},{3,2},{4,5},{5,4},{6,7},{7,6},{8,9},{9,8},{10,11... | collective-permute-start | bytes 1277960 | tf_op jit(solution)/shard_map/ppermute | solution.py:8
  252.4 4.4 %copy-start.2 = (f32[128,1664]{1,0:T(8,128)S(1)}, f32[128,1664]{1,0:T(8,128)}, u32[]{:S(2)}) copy-start(f32[128,1664]{1,0:T(8,128)} %reduce-scatter.2.cloned.1.call-done) | copy-start | bytes 2555908
  346.6 32.9 %all-to-all-start.1 = ((bf16[16,2,32768]{2,1,0:T(2,128)(2,1)}), bf16[16,2,32768]{2,1,0:T(2,128)(2,1)}, u32[]{:S(2)}, u32[]{:S(2)}) async-start(bf16[16,2,32768]{2,1,0:T(2,128)(2,1)} %reshape.104), calls=%async_computation.2 | async-start | bytes 4194304 | tf_op jit(solution)/shard_map/all_to_all | solution.py:72
  397.9 7.5 %copy-start.1 = (bf16[1,1664,480]{1,2,0:T(8,128)(2,1)S(1)}, bf16[1,1664,480]{1,2,0:T(8,128)(2,1)}, u32[]{:S(2)}) copy-start(bf16[1,1664,480]{1,2,0:T(8,128)(2,1)} %param.9) | copy-start | bytes 4792324
Sparse Core Ops, SparseCore 0:
  8.9 58.7 all-gather.1
  82.5 148.9 reduce-scatter.1
where the time goes:
time: 415 us; the launch traced here: 412 us
  waiting for transfers between devices  168 us (40%)
  other arithmetic  87.6 us (21%)
  local copies, waits for them, and re-layouts  77.4 us (19%)
  matrix products  49.3 us (12%)
  starting transfers between devices  14.9 us (4%)
  between operations  14.8 us (4%)
    reduce_scatter x1, waiting for transfers between devices, on_device(): lax.psum_scatter(lax.dot_general(flat_weight, flat_image, (((0,), (1,)),...  79.8 us
    unnamed x2, other arithmetic  61.9 us
    all_gather x1, waiting for transfers between devices, on_device(): gathered = lax.all_gather(kv_weight, 'sample', axis=1, tiled=True)  60.4 us
    unnamed x13, local copies, waits for them, and re-layouts  43.1 us
    all_to_all x1, waiting for transfers between devices, on_device(): lax.all_to_all(local_out, 'head', split_axis=1, concat_axis=2, tiled=True)  27.2 us
    dot_general x8, matrix products, one_block(): lax.dot_general(weights, value_cols, (((1,), (1,)), ((), ())), preferred_...  21.8 us
    dot_general x8, matrix products, one_block(): jnp.dot(block_rows, key_cols, preferred_element_type=jnp.float32)  18.5 us
    convert_element_type x1, local copies, waits for them, and re-layouts, one_sample(): result_rows.astype(jnp.bfloat16).reshape(seq_len, per_device * head_dim)  12.5 us
  transfers between devices with their start and end apart: 5, of which 3 were waited for; matrix products, arithmetic and copies ran while one was open for 20% of the time, Pallas kernels for 0%

commit v1 on v0

v1 whole, which is shorter than its diff:
```python
import functools

import jax
import jax.numpy as jnp
from jax import lax
from jax.experimental import pallas as pl
from jax.experimental.pallas import tpu as pltpu
from jax.sharding import Mesh
from jax.sharding import PartitionSpec as P

XL, Z, XH, Y, C = "xl", "z", "xh", "y", "c"
CHIPS = (XH, Y)
N_CHIPS = 8
VMEM_LIMIT = 48 * 1024 * 1024


def params():
    return pltpu.CompilerParams(vmem_limit_bytes=VMEM_LIMIT)


def weight_round(flip):
    pairs = []
    for xl in range(2):
        for z in range(4):
            for b in range(2):
                pairs.append(((xl * 4 + z) * 2 + b, ((b ^ flip) * 4 + z) * 2 + xl))
    return pairs


def ring(size, step):
    return [(i, (i + step) % size) for i in range(size)]


def project_kernel(n_heads, *refs):
    w_refs, (own_ref, other_ref), out_ref = refs[:n_heads], refs[n_heads : n_heads + 2], refs[-1]
    for h in range(n_heads):
        acc = jnp.dot(w_refs[h][0], own_ref[...], preferred_element_type=jnp.float32)
        acc += jnp.dot(w_refs[h][1], other_ref[...], preferred_element_type=jnp.float32)
        out_ref[:, h] = acc.astype(jnp.bfloat16).reshape(out_ref.shape[0], out_ref.shape[2], out_ref.shape[3])


def project(weights, own_image, other_image):
    n_heads = len(weights)
    rows = weights[0].shape[1] // N_CHIPS
    tokens = own_image.shape[1]
    flops = 2 * n_heads * weights[0].shape[1] * tokens * own_image.shape[0] * 2
    return pl.pallas_call(
        functools.partial(project_kernel, n_heads),
        out_shape=jax.ShapeDtypeStruct((N_CHIPS, n_heads, rows, tokens), jnp.bfloat16),
        compiler_params=params(),
        cost_estimate=pl.CostEstimate(flops=flops, bytes_accessed=6 << 20, transcendentals=0),
        name="project",
    )(*weights, own_image, other_image)


def sum_kernel(info_ref, parts_ref, out_ref):
    total = parts_ref[0].astype(jnp.float32)
    for d in range(1, N_CHIPS):
        total += parts_ref[d].astype(jnp.float32)
    first = jnp.where(info_ref[1] == 1, total[..., :1], 0.0)
    slot = lax.broadcasted_iota(jnp.int32, total.shape, 2)
    total = jnp.where(slot < info_ref[0], total, first).astype(jnp.bfloat16)
    for d in range(N_CHIPS):
        out_ref[d] = total


def sum_parts(info, parts):
    return pl.pallas_call(
        sum_kernel,
        out_shape=jax.ShapeDtypeStruct(parts.shape, jnp.bfloat16),
        in_specs=[pl.BlockSpec(memory_space=pltpu.SMEM), pl.BlockSpec(memory_space=pltpu.VMEM)],
        compiler_params=params(),
        cost_estimate=pl.CostEstimate(flops=1 << 20, bytes_accessed=4 << 20, transcendentals=0),
        name="sum_parts",
    )(info, parts)


def attend_kernel(head_dim, scalars, gate_ref, kv_ref, q_own, q_other, held, out_own, out_other):
    del held
    rows = q_own.shape[0]
    tokens = kv_ref.shape[2]
    keys = kv_ref[:4].reshape(head_dim, tokens)
    slot = lax.broadcasted_iota(jnp.int32, (head_dim, tokens), 1)
    row = lax.broadcasted_iota(jnp.int32, (head_dim, tokens), 0)
    counted = ((slot < scalars[2]) & (row == 0)).astype(jnp.float32).astype(jnp.bfloat16)
    values = jnp.concatenate([kv_ref[4:].reshape(head_dim, tokens), counted], axis=0)
    gate = gate_ref[0]
    log2e = 1.4426950408889634
    factor = head_dim**-0.5 * log2e
    live = []
    for first in (scalars[3], scalars[4]):
        live.append(first + lax.broadcasted_iota(jnp.int32, (rows, head_dim), 0) < scalars[5])
    live = jnp.concatenate(live, axis=0)
    for h in range(q_own.shape[1] // head_dim):
        cols = slice(h * head_dim, (h + 1) * head_dim)
        q = jnp.concatenate([q_own[:, cols], q_other[:, cols]], axis=0)
        scores = jnp.dot(q, keys, preferred_element_type=jnp.float32)
        top = jnp.max(scores, axis=1, keepdims=True) * factor
        weights = jnp.exp2(scores * factor - top).astype(jnp.bfloat16)
        mixed = lax.dot_general(weights, values, (((1,), (1,)), ((), ())), preferred_element_type=jnp.float32)
        attention = (mixed[:, :head_dim] / mixed[:, head_dim : head_dim + 1]).astype(jnp.bfloat16)
        gated = jnp.where(live, gate * attention.astype(jnp.float32), 0.0).astype(jnp.bfloat16)
        out_own[:, cols] = gated[:rows]
        out_other[:, cols] = gated[rows:]


def attend(scalars, gate, kv, head, q_own, q_other, held, head_dim):
    rows = q_own.shape[0]
    width = q_other.shape[1] // 4
    tokens = kv.shape[-1]
    n_heads = kv.shape[1]
    aliases = {} if held is None else {6: 0}
    if held is None:
        held = jnp.zeros((8, 128), jnp.bfloat16)
    grid_spec = pltpu.PrefetchScalarGridSpec(
        num_scalar_prefetch=1,
        grid=(1,),
        in_specs=[
            pl.BlockSpec(memory_space=pltpu.SMEM),
            pl.BlockSpec((N_CHIPS, pl.Squeezed(), kv.shape[2], tokens), lambda i, s: (0, head, 0, 0)),
            pl.BlockSpec((rows, width), lambda i, s: (0, s[0])),
            pl.BlockSpec((rows, width), lambda i, s: (0, s[1])),
            pl.BlockSpec(memory_space=pl.ANY),
        ],
        out_specs=[
            pl.BlockSpec((rows, width), lambda i, s: (0, s[0])),
            pl.BlockSpec((rows, width), lambda i, s: (0, 0)),
        ],
    )
    n_q = 2 * rows * width // head_dim
    return pl.pallas_call(
        functools.partial(attend_kernel, head_dim),
        out_shape=[
            jax.ShapeDtypeStruct(q_own.shape, jnp.bfloat16),
            jax.ShapeDtypeStruct((rows, width), jnp.bfloat16),
        ],
        grid_spec=grid_spec,
        input_output_aliases=({5: 0} if aliases else {}),
        compiler_params=params(),
        cost_estimate=pl.CostEstimate(
            flops=4 * n_q * tokens * head_dim * 2, bytes_accessed=4 << 20, transcendentals=n_q * tokens
        ),
        name="attend",
    )(scalars, gate, kv, q_own, q_other, held)


def place_kernel(scalars, received, held, out):
    del held
    out[...] = received[...]


def place(scalars, received, held):
    rows, width = received.shape
    return pl.pallas_call(
        place_kernel,
        out_shape=jax.ShapeDtypeStruct(held.shape, held.dtype),
        grid_spec=pltpu.PrefetchScalarGridSpec(
            num_scalar_prefetch=1,
            grid=(1,),
            in_specs=[
                pl.BlockSpec((rows, width), lambda i, s: (0, 0)),
                pl.BlockSpec(memory_space=pl.ANY),
            ],
            out_specs=pl.BlockSpec((rows, width), lambda i, s: (0, s[6])),
        ),
        input_output_aliases={2: 0},
        compiler_params=params(),
        name="place",
    )(scalars, received, held)


def on_device(queries, image_tokens, kv_weight, attn_gate, image_counts, response_lengths):
    rows = queries.shape[1]
    head_dim = kv_weight.shape[3]
    half = queries.shape[2] // 2
    xl, z, xh, y, c = (lax.axis_index(a) for a in (XL, Z, XH, Y, C))
    q = queries[0]
    image = image_tokens[0].T
    w_own = kv_weight[:, 0].transpose(1, 2, 0).reshape(2 * head_dim, -1)

    firsts = [lax.ppermute(w_own, (XL, Z, C), weight_round(flip)) for flip in range(2)]
    swapped = (xl ^ c) == 1
    stack = jnp.stack([jnp.where(swapped, firsts[1], firsts[0]), jnp.where(swapped, firsts[0], firsts[1])])
    image_other = lax.ppermute(image, C, ring(2, 1))
    w_next = lax.ppermute(stack, Z, ring(4, -1))
    w_prev = lax.ppermute(stack, Z, ring(4, 1))
    w_far = lax.ppermute(stack, Z, ring(4, 2))
    q_give = lax.dynamic_slice_in_dim(q, (1 - c) * half, half, axis=1)
    q_other = lax.ppermute(q_give, C, ring(2, 1))

    chip = xh * 4 + y
    count = image_counts[0]
    sum_info = jnp.stack([count, (chip < 4).astype(jnp.int32)])
    gate = jnp.tanh(attn_gate)
    mine = (chip * 2 + c) * rows
    theirs = (chip * 2 + 1 - c) * rows

    out = None
    pending = []
    chunks = [([stack], [0]), ([w_next, w_prev], [1, 3]), ([w_far], [2])]
    gathered = []
    for weights, steps in chunks:
        parts = project(weights, image, image_other)
        n_heads, part_rows, tokens = parts.shape[1:]
        flat = (N_CHIPS, n_heads * part_rows, tokens)
        parts = lax.all_to_all(parts.reshape(flat), CHIPS, 0, 0, tiled=True)
        summed = sum_parts(sum_info, parts.reshape(N_CHIPS, n_heads, part_rows, tokens))
        kv = lax.all_to_all(summed.reshape(flat), CHIPS, 0, 0, tiled=True)
        gathered.append(kv.reshape(N_CHIPS, n_heads, part_rows, tokens))
    for (weights, steps), kv in zip(chunks, gathered):
        for i, step in enumerate(steps):
            head = (z + step) % 4
            scalars = jnp.stack(
                [c * 4 + head, head, count, mine, theirs, response_lengths[0], (1 - c) * 4 + head]
            ).astype(jnp.int32)
            out, give = attend(scalars, gate, kv, i, q, q_other, out, head_dim)
            pending.append((scalars, lax.ppermute(give, C, ring(2, 1))))
    for scalars, received in pending:
        out = place(scalars, received, out)
    return out[None]


def solution(mesh):
    fine = Mesh(mesh.devices.reshape(2, 4, 2, 4, 2), (XL, Z, XH, Y, C))
    sample, head = (XL, Z), (XH, Y, C)
    placed = (
        P(sample, head, None),
        P(sample, None, head),
        P(head, sample, None, None),
        P(),
        P(sample),
        P(sample),
    )
    return jax.shard_map(
        on_device, mesh=fine, in_specs=placed, out_specs=P(sample, head, None), check_vma=False
    )
```

time: 415 us -> 186 us (0.45)
  waiting for transfers between devices: 168 us -> 74 us
  other arithmetic: 87.6 us -> 1.2 us
  local copies, waits for them, and re-layouts: 77.4 us -> 9.89 us
  matrix products: 49.3 us -> 0 us
  Pallas kernels: 0 us -> 47.1 us
  starting transfers between devices: 14.9 us -> 50.7 us
  between operations: 14.8 us -> 2.15 us
    reduce_scatter x1 -> x0, waiting for transfers between devices: 79.8 us -> none  [on_device(): lax.psum_scatter(lax.dot_general(flat_weight, flat_image, (((0,), (1,)),...]
    unnamed x2 -> x0, other arithmetic: 61.9 us -> none
    all_gather x1 -> x0, waiting for transfers between devices: 60.4 us -> none  [on_device(): gathered = lax.all_gather(kv_weight, 'sample', axis=1, tiled=True)]
    dot_general x17 -> x0, matrix products: 49.3 us -> none  [the longest x8 21.8 us: one_block(): lax.dot_general(weights, value_cols, (((1,), (1,)), ((), ())), preferred_...]
    pallas_call x0 -> x14, Pallas kernels: none -> 47.1 us  [the longest x4 31.1 us: attend(): pl.pallas_call(functools.partial(attend_kernel, head_dim), out_shape=[jax...]
    unnamed x13 -> x14, local copies, waits for them, and re-layouts: 43.1 us -> 6.17 us
    ppermute x1 -> x11, waiting for transfers between devices: 0.01 us -> 30.7 us  [the longest x1 11.8 us: on_device(): w_prev = lax.ppermute(stack, Z, ring(4, 1))]
    all_to_all x2 -> x6, starting transfers between devices: 13.3 us -> 36.8 us  [the longest x3 20 us: on_device(): parts = lax.all_to_all(parts.reshape(flat), CHIPS, 0, 0, tiled=True)]
  transfers between devices with their start and end apart: 5 -> 17, of which waited for: 3 -> 7; matrix products, arithmetic and copies ran while one was open for 20% -> 3% of each run, Pallas kernels for 0% -> 24%
where the time goes in v1:
time: 186 us; the launch traced here: 185 us
  waiting for transfers between devices  74 us (40%)
  starting transfers between devices  50.7 us (27%)
  Pallas kernels  47.1 us (25%)
  local copies, waits for them, and re-layouts  9.89 us (5%)
  between operations  2.15 us (1%)
    pallas_call x4, Pallas kernels, attend(): pl.pallas_call(functools.partial(attend_kernel, head_dim), out_shape=[jax...  31.1 us
    all_to_all x3, waiting for transfers between devices, on_device(): kv = lax.all_to_all(summed.reshape(flat), CHIPS, 0, 0, tiled=True)  25.1 us
    all_to_all x3, starting transfers between devices, on_device(): parts = lax.all_to_all(parts.reshape(flat), CHIPS, 0, 0, tiled=True)  20 us
    all_to_all x3, waiting for transfers between devices, on_device(): parts = lax.all_to_all(parts.reshape(flat), CHIPS, 0, 0, tiled=True)  18.2 us
    all_to_all x3, starting transfers between devices, on_device(): kv = lax.all_to_all(summed.reshape(flat), CHIPS, 0, 0, tiled=True)  16.8 us
    ppermute x1, waiting for transfers between devices, on_device(): w_prev = lax.ppermute(stack, Z, ring(4, 1))  11.8 us
    ppermute x1, waiting for transfers between devices, on_device(): w_far = lax.ppermute(stack, Z, ring(4, 2))  11.6 us
    ppermute x2, waiting for transfers between devices, on_device(): lax.ppermute(w_own, (XL, Z, C), weight_round(flip))  7.28 us
  transfers between devices with their start and end apart: 17, of which 7 were waited for; matrix products, arithmetic and copies ran while one was open for 3% of the time, Pallas kernels for 24%

profile of v1, /device:TPU:1, one launch (start us, length us, event | category | flops | bytes accessed | tf_op | source)
XLA Modules:
  0.0 185.1 jit_solution(7254537429573560953)
XLA Ops:
  0.0 1.4 collective-permute-start.3
  1.4 1.1 copy.14
  2.5 3.2 %collective-permute-start.1 = (bf16[256,480]{1,0:T(8,128)(2,1)S(1)}, bf16[256,480]{1,0:T(8,128)(2,1)}, u32[]{:S(2)}, u32[]{:S(2)}) collective-permute-start(bf16[256,480]{1,0:T(8,128)(2,1)S(1)} %bitcast.58), channel_id=1, source_target_pairs={{0,0},{1,64},{16,16},{17,80},{32,32},{33,96},{48,48},{49,112},{64,... | collective-permute-start | bytes 737288 | tf_op jit(solution)/shard_map/ppermute | solution.py:181
  5.8 0.1 collective-permute-start
  5.9 6.5 %collective-permute-done.1 = bf16[256,480]{1,0:T(8,128)(2,1)} collective-permute-done((bf16[256,480]{1,0:T(8,128)(2,1)S(1)}, bf16[256,480]{1,0:T(8,128)(2,1)}, u32[]{:S(2)}, u32[]{:S(2)}) %collective-permute-start.1) | collective-permute-done | bytes 245792 | tf_op jit(solution)/shard_map/ppermute | solution.py:181
  12.3 0.8 collective-permute-done
  13.1 1.1 select_bitcast_fusion.1
  14.3 1.1 project.5
  15.4 0.9 copy-done.2
  16.3 6.7 %all-to-all-start.4 = ((bf16[8,32,1664]{2,1,0:T(8,128)(2,1)}), bf16[8,32,1664]{2,1,0:T(8,128)(2,1)}, u32[]{:S(2)}, u32[]{:S(2)}) async-start(bf16[8,32,1664]{2,1,0:T(8,128)(2,1)} %bitcast.48), calls=%async_computation.4 | async-start | bytes 1703936 | tf_op jit(solution)/shard_map/all_to_all | solution.py:206
  23.1 3.6 %collective-permute-start.2 = (bf16[2,256,480]{2,1,0:T(8,128)(2,1)}, bf16[2,256,480]{2,1,0:T(8,128)(2,1)S(1)}, u32[]{:S(2)}, u32[]{:S(2)}) collective-permute-start(bf16[2,256,480]{2,1,0:T(8,128)(2,1)} %copy-done.3), channel_id=1, source_target_pairs={{0,32},{16,48},{32,0},{48,16},{1,33},{17,49},{33,1},{49,17},{2,34}... | collective-permute-start | bytes 1474568 | tf_op jit(solution)/shard_map/ppermute | solution.py:187
  26.7 11.6 %collective-permute-done.2.refs_0_ = bf16[2,256,480]{2,1,0:T(8,128)(2,1)S(1)} collective-permute-done((bf16[2,256,480]{2,1,0:T(8,128)(2,1)}, bf16[2,256,480]{2,1,0:T(8,128)(2,1)S(1)}, u32[]{:S(2)}, u32[]{:S(2)}) %collective-permute-start.2) | collective-permute-done | bytes 491552 | tf_op jit(solution)/shard_map/ppermute | solution.py:187
  38.3 1.1 project.3
  39.4 0.9 copy-done.1
  40.3 6.9 %all-to-all-start = ((bf16[8,32,1664]{2,1,0:T(8,128)(2,1)}), bf16[8,32,1664]{2,1,0:T(8,128)(2,1)}, u32[]{:S(2)}, u32[]{:S(2)}) async-start(bf16[8,32,1664]{2,1,0:T(8,128)(2,1)} %bitcast.47), calls=%async_computation | async-start | bytes 1703936 | tf_op jit(solution)/shard_map/all_to_all | solution.py:206
  47.2 1.3 collective-permute-start.6
  48.6 2.2 %collective-permute-start.5 = (bf16[2,256,480]{2,1,0:T(8,128)(2,1)}, bf16[2,256,480]{2,1,0:T(8,128)(2,1)S(1)}, u32[]{:S(2)}, u32[]{:S(2)}) collective-permute-start(bf16[2,256,480]{2,1,0:T(8,128)(2,1)} %copy-done.3), channel_id=1, source_target_pairs={{0,48},{16,0},{32,16},{48,32},{1,49},{17,1},{33,17},{49,33},{2,50}... | collective-permute-start | bytes 1474568 | tf_op jit(solution)/shard_map/ppermute | solution.py:185
  50.7 11.8 %collective-permute-done.6.refs_1_ = bf16[2,256,480]{2,1,0:T(8,128)(2,1)S(1)} collective-permute-done((bf16[2,256,480]{2,1,0:T(8,128)(2,1)}, bf16[2,256,480]{2,1,0:T(8,128)(2,1)S(1)}, u32[]{:S(2)}, u32[]{:S(2)}) %collective-permute-start.6) | collective-permute-done | bytes 491552 | tf_op jit(solution)/shard_map/ppermute | solution.py:186
  62.5 2.1 %project.4 = bf16[8,2,32,1664]{3,2,1,0:T(8,128)(2,1)S(1)} custom-call(bf16[2,256,480]{2,1,0:T(8,128)(2,1)S(1)} %collective-permute-done.5.refs_0_, bf16[2,256,480]{2,1,0:T(8,128)(2,1)S(1)} %collective-permute-done.6.refs_1_, bf16[480,1664]{1,0:T(8,128)(2,1)S(1)} %bitcast.46, bf16[480,1664]{1,0:T(8,128)(2,1)S(1)} %collective-permute-done.3.refs_2_.refs_3_), custom_call_target="tpu_custom_call" | custom-call | flops 1635778560 | bytes 6291456 | tf_op jit(solution)/shard_map/project/pallas_call | solution.py:47
  64.6 1.2 copy-done.4
  65.8 6.3 %all-to-all-start.2 = ((bf16[8,64,1664]{2,1,0:T(8,128)(2,1)}), bf16[8,64,1664]{2,1,0:T(8,128)(2,1)S(1)}, u32[]{:S(2)}, u32[]{:S(2)}) async-start(bf16[8,64,1664]{2,1,0:T(8,128)(2,1)} %bitcast.51), calls=%async_computation.2 | async-start | bytes 3407872 | tf_op jit(solution)/shard_map/all_to_all | solution.py:206
  72.8 2.3 %sum_parts.5 = bf16[8,1,32,1664]{3,2,1,0:T(8,128)(2,1)} custom-call(s32[2]{0:T(128)S(1)} %pad_add_fusion.info_ref, bf16[8,1,32,1664]{3,2,1,0:T(8,128)(2,1)} %bitcast.34.parts_ref), custom_call_target="tpu_custom_call" | custom-call | flops 1048576 | bytes 4194304 | tf_op jit(solution)/shard_map/sum_parts/pallas_call | solution.py:68
  75.1 18.2 %all-to-all-done.2 = bf16[8,64,1664]{2,1,0:T(8,128)(2,1)S(1)} async-done(((bf16[8,64,1664]{2,1,0:T(8,128)(2,1)}), bf16[8,64,1664]{2,1,0:T(8,128)(2,1)S(1)}, u32[]{:S(2)}, u32[]{:S(2)}) %all-to-all-start.2) | async-done | bytes 1703968 | tf_op jit(solution)/shard_map/all_to_all | solution.py:206
  93.3 5.9 %all-to-all-start.5 = ((bf16[8,32,1664]{2,1,0:T(8,128)(2,1)}), bf16[8,32,1664]{2,1,0:T(8,128)(2,1)S(1)}, u32[]{:S(2)}, u32[]{:S(2)}) async-start(bf16[8,32,1664]{2,1,0:T(8,128)(2,1)} %bitcast.35), calls=%async_computation.5 | async-start | bytes 1703936 | tf_op jit(solution)/shard_map/all_to_all | solution.py:208
  99.3 2.1 %sum_parts.4 = bf16[8,2,32,1664]{3,2,1,0:T(8,128)(2,1)} custom-call(s32[2]{0:T(128)S(1)} %pad_add_fusion.info_ref, bf16[8,2,32,1664]{3,2,1,0:T(8,128)(2,1)S(1)} %bitcast.42), custom_call_target="tpu_custom_call" | custom-call | flops 1048576 | bytes 4194304 | tf_op jit(solution)/shard_map/sum_parts/pallas_call | solution.py:68
  101.4 10.1 %all-to-all-done.5 = bf16[8,32,1664]{2,1,0:T(8,128)(2,1)S(1)} async-done(((bf16[8,32,1664]{2,1,0:T(8,128)(2,1)}), bf16[8,32,1664]{2,1,0:T(8,128)(2,1)S(1)}, u32[]{:S(2)}, u32[]{:S(2)}) %all-to-all-start.5) | async-done | bytes 852000 | tf_op jit(solution)/shard_map/all_to_all | solution.py:208
  111.5 5.7 %all-to-all-start.3 = ((bf16[8,64,1664]{2,1,0:T(8,128)(2,1)}), bf16[8,64,1664]{2,1,0:T(8,128)(2,1)S(1)}, u32[]{:S(2)}, u32[]{:S(2)}) async-start(bf16[8,64,1664]{2,1,0:T(8,128)(2,1)} %bitcast.25), calls=%async_computation.3 | async-start | bytes 3407872 | tf_op jit(solution)/shard_map/all_to_all | solution.py:208
  117.3 2.3 %dynamic-slice_bitcast_fusion = bf16[128,4096]{1,0:T(8,128)(2,1)} fusion(bf16[1,128,8192]{2,1,0:T(8,128)(2,1)} %param.6, s32[]{:T(128)S(6)} %select_n.38), kind=kLoop, calls=%fused_computation | loop fusion | bytes 2097156 | tf_op jit(solution)/shard_map/dynamic_slice | solution.py:188
  119.6 0.8 collective-permute-start.4
  121.7 0.1 stack.93.scalars
  121.8 0.1 stack.83.scalars
  121.8 0.1 stack.101.scalars
  121.9 0.1 stack.97.scalars
  122.0 2.3 %sum_parts.3 = bf16[8,1,32,1664]{3,2,1,0:T(8,128)(2,1)} custom-call(s32[2]{0:T(128)S(1)} %pad_add_fusion.info_ref, bf16[8,1,32,1664]{3,2,1,0:T(8,128)(2,1)} %bitcast.15.parts_ref), custom_call_target="tpu_custom_call" | custom-call | flops 1048576 | bytes 4194304 | tf_op jit(solution)/shard_map/sum_parts/pallas_call | solution.py:68
  124.3 14.9 %all-to-all-done.3 = bf16[8,64,1664]{2,1,0:T(8,128)(2,1)S(1)} async-done(((bf16[8,64,1664]{2,1,0:T(8,128)(2,1)}), bf16[8,64,1664]{2,1,0:T(8,128)(2,1)S(1)}, u32[]{:S(2)}, u32[]{:S(2)}) %all-to-all-start.3) | async-done | bytes 1703968 | tf_op jit(solution)/shard_map/all_to_all | solution.py:208
  139.2 5.2 %all-to-all-start.1 = ((bf16[8,32,1664]{2,1,0:T(8,128)(2,1)}), bf16[8,32,1664]{2,1,0:T(8,128)(2,1)S(1)}, u32[]{:S(2)}, u32[]{:S(2)}) async-start(bf16[8,32,1664]{2,1,0:T(8,128)(2,1)} %bitcast.16), calls=%async_computation.1 | async-start | bytes 1703936 | tf_op jit(solution)/shard_map/all_to_all | solution.py:208
  144.5 1.6 copy-done.5
  146.0 7.8 %attend.4 = (bf16[128,8192]{1,0:T(8,128)(2,1)}, bf16[128,1024]{1,0:T(8,128)(2,1)}) custom-call(s32[7]{0:T(128)S(1)} %stack.101.scalars, f32[1]{0:T(128)S(6)} %tanh.3.gate_ref, bf16[8,1,32,1664]{3,2,1,0:T(8,128)(2,1)S(1)} %bitcast.52, bf16[128,8192]{1,0:T(8,128)(2,1)S(1)} %bitcast.54, bf16[128,4096]{1,0:T(8,128)(2,1)} %collective-permute-done.4.q_other, ...), custom_call_target="tpu_custom_call" | custom-call | flops 3489660928 | bytes 4194304 | tf_op jit(solution)/shard_map/attend/pallas_call | solution.py:131
  153.8 0.8 collective-permute-start.10
  154.6 7.8 %attend.5 = (bf16[128,8192]{1,0:T(8,128)(2,1)}, bf16[128,1024]{1,0:T(8,128)(2,1)}) custom-call(s32[7]{0:T(128)S(1)} %stack.97.scalars, f32[1]{0:T(128)S(6)} %tanh.3.gate_ref, bf16[8,2,32,1664]{3,2,1,0:T(8,128)(2,1)S(1)} %bitcast.49, bf16[128,8192]{1,0:T(8,128)(2,1)S(1)} %bitcast.55, ...), custom_call_target="tpu_custom_call", output_to_operand_aliasing={{0}: (5, {})} | custom-call | flops 3489660928 | bytes 4194304 | tf_op jit(solution)/shard_map/attend/pallas_call | solution.py:131
  162.4 7.8 %attend.6 = (bf16[128,8192]{1,0:T(8,128)(2,1)}, bf16[128,1024]{1,0:T(8,128)(2,1)S(1)}) custom-call(s32[7]{0:T(128)S(1)} %stack.93.scalars, f32[1]{0:T(128)S(6)} %tanh.3.gate_ref, bf16[8,2,32,1664]{3,2,1,0:T(8,128)(2,1)S(1)} %bitcast.50, bf16[128,8192]{1,0:T(8,128)(2,1)S(1)} %bitcast.56, ...), custom_call_target="tpu_custom_call", output_to_operand_aliasing={{0}: (5, {})} | custom-call | flops 3489660928 | bytes 4194304 | tf_op jit(solution)/shard_map/attend/pallas_call | solution.py:131
  170.2 0.5 collective-permute-start.9
  170.7 1.6 copy-done.6
  172.3 7.7 %attend.7 = (bf16[128,8192]{1,0:T(8,128)(2,1)}, bf16[128,1024]{1,0:T(8,128)(2,1)S(1)}) custom-call(s32[7]{0:T(128)S(1)} %stack.83.scalars, f32[1]{0:T(128)S(6)} %tanh.3.gate_ref, bf16[8,1,32,1664]{3,2,1,0:T(8,128)(2,1)S(1)} %bitcast.53, bf16[128,8192]{1,0:T(8,128)(2,1)S(1)} %bitcast.57, ...), custom_call_target="tpu_custom_call", output_to_operand_aliasing={{0}: (5, {})} | custom-call | flops 3489660928 | bytes 4194304 | tf_op jit(solution)/shard_map/attend/pallas_call | solution.py:131
  180.0 1.3 place.4.held
  181.3 1.3 place.5.held
  182.5 1.3 place.6.held
  183.8 1.3 place.7
  (24 shorter events, 0.2 us)
Async XLA Ops:
  0.0 14.3 %copy-start = (bf16[1,1664,480]{1,2,0:T(8,128)(2,1)S(1)}, bf16[1,1664,480]{1,2,0:T(8,128)(2,1)}, u32[]{:S(2)}) copy-start(bf16[1,1664,480]{1,2,0:T(8,128)(2,1)} %param.7) | copy-start | bytes 4792324
  0.0 14.3 %collective-permute-start.3 = (bf16[480,1664]{1,0:T(8,128)(2,1)}, bf16[480,1664]{1,0:T(8,128)(2,1)S(1)}, u32[]{:S(2)}, u32[]{:S(2)}) collective-permute-start(bf16[480,1664]{1,0:T(8,128)(2,1)} %bitcast.43), channel_id=1, source_target_pairs={{0,1},{1,0},{2,3},{3,2},{4,5},{5,4},{6,7},{7,6},{8,9},{9,8},{10,11... | collective-permute-start | bytes 4792328 | tf_op jit(solution)/shard_map/ppermute | solution.py:184
  2.5 9.8 %collective-permute-start.1 = (bf16[256,480]{1,0:T(8,128)(2,1)S(1)}, bf16[256,480]{1,0:T(8,128)(2,1)}, u32[]{:S(2)}, u32[]{:S(2)}) collective-permute-start(bf16[256,480]{1,0:T(8,128)(2,1)S(1)} %bitcast.58), channel_id=1, source_target_pairs={{0,0},{1,64},{16,16},{17,80},{32,32},{33,96},{48,48},{49,112},{64,... | collective-permute-start | bytes 737288 | tf_op jit(solution)/shard_map/ppermute | solution.py:181
  5.8 7.4 %collective-permute-start = (bf16[256,480]{1,0:T(8,128)(2,1)S(1)}, bf16[256,480]{1,0:T(8,128)(2,1)}, u32[]{:S(2)}, u32[]{:S(2)}) collective-permute-start(bf16[256,480]{1,0:T(8,128)(2,1)S(1)} %bitcast.59), channel_id=1, source_target_pairs={{0,64},{1,0},{16,80},{17,16},{32,96},{33,32},{48,112},{49,48},{64,... | collective-permute-start | bytes 737288 | tf_op jit(solution)/shard_map/ppermute | solution.py:181
  14.3 1.1 copy-start.3
  15.4 0.9 copy-start.2
  16.3 24.0 %all-to-all-start.4 = ((bf16[8,32,1664]{2,1,0:T(8,128)(2,1)}), bf16[8,32,1664]{2,1,0:T(8,128)(2,1)}, u32[]{:S(2)}, u32[]{:S(2)}) async-start(bf16[8,32,1664]{2,1,0:T(8,128)(2,1)} %bitcast.48), calls=%async_computation.4 | async-start | bytes 1703936 | tf_op jit(solution)/shard_map/all_to_all | solution.py:206
  23.1 15.2 %collective-permute-start.2 = (bf16[2,256,480]{2,1,0:T(8,128)(2,1)}, bf16[2,256,480]{2,1,0:T(8,128)(2,1)S(1)}, u32[]{:S(2)}, u32[]{:S(2)}) collective-permute-start(bf16[2,256,480]{2,1,0:T(8,128)(2,1)} %copy-done.3), channel_id=1, source_target_pairs={{0,32},{16,48},{32,0},{48,16},{1,33},{17,49},{33,1},{49,17},{2,34}... | collective-permute-start | bytes 1474568 | tf_op jit(solution)/shard_map/ppermute | solution.py:187
  39.4 0.9 copy-start.1
  40.3 25.5 %all-to-all-start = ((bf16[8,32,1664]{2,1,0:T(8,128)(2,1)}), bf16[8,32,1664]{2,1,0:T(8,128)(2,1)}, u32[]{:S(2)}, u32[]{:S(2)}) async-start(bf16[8,32,1664]{2,1,0:T(8,128)(2,1)} %bitcast.47), calls=%async_computation | async-start | bytes 1703936 | tf_op jit(solution)/shard_map/all_to_all | solution.py:206
  47.2 15.3 %collective-permute-start.6 = (bf16[2,256,480]{2,1,0:T(8,128)(2,1)}, bf16[2,256,480]{2,1,0:T(8,128)(2,1)S(1)}, u32[]{:S(2)}, u32[]{:S(2)}) collective-permute-start(bf16[2,256,480]{2,1,0:T(8,128)(2,1)} %copy-done.3), channel_id=1, source_target_pairs={{0,16},{16,32},{32,48},{48,0},{1,17},{17,33},{33,49},{49,1},{2,18}... | collective-permute-start | bytes 1474568 | tf_op jit(solution)/shard_map/ppermute | solution.py:186
  48.6 14.0 %collective-permute-start.5 = (bf16[2,256,480]{2,1,0:T(8,128)(2,1)}, bf16[2,256,480]{2,1,0:T(8,128)(2,1)S(1)}, u32[]{:S(2)}, u32[]{:S(2)}) collective-permute-start(bf16[2,256,480]{2,1,0:T(8,128)(2,1)} %copy-done.3), channel_id=1, source_target_pairs={{0,48},{16,0},{32,16},{48,32},{1,49},{17,1},{33,17},{49,33},{2,50}... | collective-permute-start | bytes 1474568 | tf_op jit(solution)/shard_map/ppermute | solution.py:185
  64.6 1.2 copy-start.4
  65.8 27.5 %all-to-all-start.2 = ((bf16[8,64,1664]{2,1,0:T(8,128)(2,1)}), bf16[8,64,1664]{2,1,0:T(8,128)(2,1)S(1)}, u32[]{:S(2)}, u32[]{:S(2)}) async-start(bf16[8,64,1664]{2,1,0:T(8,128)(2,1)} %bitcast.51), calls=%async_computation.2 | async-start | bytes 3407872 | tf_op jit(solution)/shard_map/all_to_all | solution.py:206
  93.3 18.2 %all-to-all-start.5 = ((bf16[8,32,1664]{2,1,0:T(8,128)(2,1)}), bf16[8,32,1664]{2,1,0:T(8,128)(2,1)S(1)}, u32[]{:S(2)}, u32[]{:S(2)}) async-start(bf16[8,32,1664]{2,1,0:T(8,128)(2,1)} %bitcast.35), calls=%async_computation.5 | async-start | bytes 1703936 | tf_op jit(solution)/shard_map/all_to_all | solution.py:208
  111.5 27.7 %all-to-all-start.3 = ((bf16[8,64,1664]{2,1,0:T(8,128)(2,1)}), bf16[8,64,1664]{2,1,0:T(8,128)(2,1)S(1)}, u32[]{:S(2)}, u32[]{:S(2)}) async-start(bf16[8,64,1664]{2,1,0:T(8,128)(2,1)} %bitcast.25), calls=%async_computation.3 | async-start | bytes 3407872 | tf_op jit(solution)/shard_map/all_to_all | solution.py:208
  119.6 24.9 %collective-permute-start.4 = (bf16[128,4096]{1,0:T(8,128)(2,1)}, bf16[128,4096]{1,0:T(8,128)(2,1)}, u32[]{:S(2)}, u32[]{:S(2)}) collective-permute-start(bf16[128,4096]{1,0:T(8,128)(2,1)} %dynamic-slice_bitcast_fusion), channel_id=1, source_target_pairs={{0,1},{1,0},{2,3},{3,2},{4,5},{5,4},{6,7},{7,6},{8,9},{9,8},{10,11... | collective-permute-start | bytes 3145736 | tf_op jit(solution)/shard_map/ppermute | solution.py:189
  139.2 31.5 %all-to-all-start.1 = ((bf16[8,32,1664]{2,1,0:T(8,128)(2,1)}), bf16[8,32,1664]{2,1,0:T(8,128)(2,1)S(1)}, u32[]{:S(2)}, u32[]{:S(2)}) async-start(bf16[8,32,1664]{2,1,0:T(8,128)(2,1)} %bitcast.16), calls=%async_computation.1 | async-start | bytes 1703936 | tf_op jit(solution)/shard_map/all_to_all | solution.py:208
  144.4 1.6 copy-start.5
  153.8 26.2 %collective-permute-start.10 = (bf16[128,1024]{1,0:T(8,128)(2,1)}, bf16[128,1024]{1,0:T(8,128)(2,1)S(1)}, u32[]{:S(2)}, u32[]{:S(2)}) collective-permute-start(bf16[128,1024]{1,0:T(8,128)(2,1)} %get-tuple-element.19), channel_id=1, source_target_pairs={{0,1},{1,0},{2,3},{3,2},{4,5},{5,4},{6,7},{7,6},{8,9},{9,8},{10,11... | collective-permute-start | bytes 786440 | tf_op jit(solution)/shard_map/ppermute | solution.py:217
  170.2 12.4 %collective-permute-start.8 = (bf16[128,1024]{1,0:T(8,128)(2,1)S(1)}, bf16[128,1024]{1,0:T(8,128)(2,1)S(1)}, u32[]{:S(2)}, u32[]{:S(2)}) collective-permute-start(bf16[128,1024]{1,0:T(8,128)(2,1)S(1)} %get-tuple-element.17), channel_id=1, source_target_pairs={{0,1},{1,0},{2,3},{3,2},{4,5},{5,4},{6,7},{7,6},{8,9},{9,8},{10,11... | collective-permute-start | bytes 786440 | tf_op jit(solution)/shard_map/ppermute | solution.py:217
  170.2 11.1 %collective-permute-start.9 = (bf16[128,1024]{1,0:T(8,128)(2,1)}, bf16[128,1024]{1,0:T(8,128)(2,1)S(1)}, u32[]{:S(2)}, u32[]{:S(2)}) collective-permute-start(bf16[128,1024]{1,0:T(8,128)(2,1)} %get-tuple-element.18), channel_id=1, source_target_pairs={{0,1},{1,0},{2,3},{3,2},{4,5},{5,4},{6,7},{7,6},{8,9},{9,8},{10,11... | collective-permute-start | bytes 786440 | tf_op jit(solution)/shard_map/ppermute | solution.py:217
  170.7 1.6 copy-start.6
  180.0 3.8 %collective-permute-start.7 = (bf16[128,1024]{1,0:T(8,128)(2,1)S(1)}, bf16[128,1024]{1,0:T(8,128)(2,1)S(1)}, u32[]{:S(2)}, u32[]{:S(2)}) collective-permute-start(bf16[128,1024]{1,0:T(8,128)(2,1)S(1)} %get-tuple-element.16), channel_id=1, source_target_pairs={{0,1},{1,0},{2,3},{3,2},{4,5},{5,4},{6,7},{7,6},{8,9},{9,8},{10,11... | collective-permute-start | bytes 786440 | tf_op jit(solution)/shard_map/ppermute | solution.py:217

commit v2 on v1

v2 whole, which is shorter than its diff:
```python
import functools

import jax
import jax.numpy as jnp
from jax import lax
from jax.experimental import pallas as pl
from jax.experimental.pallas import tpu as pltpu
from jax.sharding import Mesh
from jax.sharding import PartitionSpec as P

XL, Z, XH, Y, C = "xl", "z", "xh", "y", "c"
CHIPS = (XH, Y)
N_CHIPS = 8
MIB = 1024 * 1024


def params(mib):
    return pltpu.CompilerParams(vmem_limit_bytes=mib * MIB)


def weight_round(flip):
    pairs = []
    for xl in range(2):
        for z in range(4):
            for b in range(2):
                pairs.append(((xl * 4 + z) * 2 + b, ((b ^ flip) * 4 + z) * 2 + xl))
    return pairs


def ring(size, step):
    return [(i, (i + step) % size) for i in range(size)]


def project_kernel(w_ref, own_ref, other_ref, held, out_ref):
    del held
    acc = jnp.dot(w_ref[0], own_ref[...], preferred_element_type=jnp.float32)
    acc += jnp.dot(w_ref[1], other_ref[...], preferred_element_type=jnp.float32)
    out_ref[...] = acc.astype(jnp.bfloat16).reshape(out_ref.shape)


def project(weight, own_image, other_image, side, held):
    kv_rows = weight.shape[1]
    tokens = own_image.shape[1]
    groups = N_CHIPS // 2
    shape = (N_CHIPS, kv_rows // groups, tokens)
    whole = pl.BlockSpec(memory_space=pltpu.VMEM)
    return pl.pallas_call(
        project_kernel,
        out_shape=jax.ShapeDtypeStruct(shape, jnp.bfloat16),
        grid=(1,),
        in_specs=[whole, whole, whole, pl.BlockSpec(memory_space=pl.ANY)],
        out_specs=pl.BlockSpec((groups,) + shape[1:], lambda i: (side, 0, 0)),
        input_output_aliases={3: 0} if held.shape == shape else {},
        compiler_params=params(20),
        cost_estimate=pl.CostEstimate(
            flops=2 * kv_rows * tokens * own_image.shape[0] * 2, bytes_accessed=5 * MIB, transcendentals=0
        ),
        name="project",
    )(weight, own_image, other_image, held)


def sum_kernel(info_ref, parts_ref, out_ref):
    total = parts_ref[0].astype(jnp.float32)
    for d in range(1, N_CHIPS):
        total += parts_ref[d].astype(jnp.float32)
    first = jnp.where(info_ref[1] == 1, total[:, :1], 0.0)
    slot = lax.broadcasted_iota(jnp.int32, total.shape, 1)
    total = jnp.where(slot < info_ref[0], total, first).astype(jnp.bfloat16)
    for d in range(out_ref.shape[0]):
        out_ref[d] = total


def sum_parts(info, parts):
    return pl.pallas_call(
        sum_kernel,
        out_shape=jax.ShapeDtypeStruct((parts.shape[0] // 2,) + parts.shape[1:], jnp.bfloat16),
        in_specs=[pl.BlockSpec(memory_space=pltpu.SMEM), pl.BlockSpec(memory_space=pltpu.VMEM)],
        compiler_params=params(16),
        cost_estimate=pl.CostEstimate(flops=1 << 20, bytes_accessed=4 << 20, transcendentals=0),
        name="sum_parts",
    )(info, parts)


def attend_kernel(head_dim, scalars, gate_ref, kv_ref, q_0, q_1, held, out_0, out_1):
    del held
    rows = q_0.shape[0]
    tokens = kv_ref.shape[2]
    keys = kv_ref[:2].reshape(head_dim, tokens)
    slot = lax.broadcasted_iota(jnp.int32, (head_dim, tokens), 1)
    row = lax.broadcasted_iota(jnp.int32, (head_dim, tokens), 0)
    counted = ((slot < scalars[1]) & (row == 0)).astype(jnp.float32).astype(jnp.bfloat16)
    values = jnp.concatenate([kv_ref[2:].reshape(head_dim, tokens), counted], axis=0)
    gate = gate_ref[0]
    factor = head_dim**-0.5 * 1.4426950408889634
    live = []
    for first in (scalars[2], scalars[3]):
        live.append(first + lax.broadcasted_iota(jnp.int32, (rows, head_dim), 0) < scalars[4])
    live = jnp.concatenate(live + live, axis=0)
    for h in range(0, q_0.shape[1] // head_dim, 2):
        cols = [slice(k * head_dim, (k + 1) * head_dim) for k in (h, h + 1)]
        q = jnp.concatenate([ref[:, k] for k in cols for ref in (q_0, q_1)], axis=0)
        scores = jnp.dot(q, keys, preferred_element_type=jnp.float32)
        top = jnp.max(scores, axis=1, keepdims=True) * factor
        weights = jnp.exp2(scores * factor - top).astype(jnp.bfloat16)
        mixed = lax.dot_general(weights, values, (((1,), (1,)), ((), ())), preferred_element_type=jnp.float32)
        attention = (mixed[:, :head_dim] / mixed[:, head_dim : head_dim + 1]).astype(jnp.bfloat16)
        gated = jnp.where(live, gate * attention.astype(jnp.float32), 0.0).astype(jnp.bfloat16)
        for i, k in enumerate(cols):
            out_0[:, k] = gated[2 * i * rows : (2 * i + 1) * rows]
            out_1[:, k] = gated[(2 * i + 1) * rows : (2 * i + 2) * rows]


def attend(scalars, gate, kv, q_0, q_1, held, head_dim, whole, chunk):
    rows, width = q_1.shape[1:]
    tokens = kv.shape[-1]
    piece = pl.BlockSpec((rows, width), lambda i, s: (0, 0))
    q_piece = pl.BlockSpec((pl.Squeezed(), rows, width), lambda i, s: (chunk, 0, 0))
    column = pl.BlockSpec((rows, width), lambda i, s: (0, s[0]))
    grid_spec = pltpu.PrefetchScalarGridSpec(
        num_scalar_prefetch=1,
        grid=(1,),
        in_specs=[
            pl.BlockSpec(memory_space=pltpu.SMEM),
            pl.BlockSpec(kv.shape, lambda i, s: (0, 0, 0)),
            column if whole else q_piece,
            q_piece,
            pl.BlockSpec(memory_space=pl.ANY),
        ],
        out_specs=[column if whole else piece, piece],
    )
    n_q = 2 * rows * width // head_dim
    return pl.pallas_call(
        functools.partial(attend_kernel, head_dim),
        out_shape=[
            jax.ShapeDtypeStruct(q_0.shape if whole else (rows, width), jnp.bfloat16),
            jax.ShapeDtypeStruct((rows, width), jnp.bfloat16),
        ],
        grid_spec=grid_spec,
        input_output_aliases={5: 0} if whole == 2 else {},
        compiler_params=params(28),
        cost_estimate=pl.CostEstimate(
            flops=4 * n_q * tokens * head_dim, bytes_accessed=4 << 20, transcendentals=n_q * tokens
        ),
        name="attend",
    )(scalars, gate, kv, q_0, q_1, held)


def place_kernel(scalars, *refs):
    n = len(refs) - 3
    received, out, sems = refs[:n], refs[n + 1], refs[n + 2]
    width = received[0].shape[1]
    copies = []
    for i in range(n):
        cols = pl.ds(pl.multiple_of(scalars[i] * width, width), width)
        copies.append(pltpu.make_async_copy(received[i], out.at[:, cols], sems.at[i]))
    for copy in copies:
        copy.start()
    for copy in copies:
        copy.wait()


def place(columns, received, held):
    n = len(received)
    return pl.pallas_call(
        place_kernel,
        out_shape=jax.ShapeDtypeStruct(held.shape, held.dtype),
        in_specs=[pl.BlockSpec(memory_space=pltpu.SMEM)]
        + [pl.BlockSpec(memory_space=pltpu.VMEM)] * n
        + [pl.BlockSpec(memory_space=pl.ANY)],
        out_specs=pl.BlockSpec(memory_space=pl.ANY),
        scratch_shapes=[pltpu.SemaphoreType.DMA((n,))],
        input_output_aliases={n + 1: 0},
        compiler_params=params(8),
        cost_estimate=pl.CostEstimate(flops=0, bytes_accessed=1 << 20, transcendentals=0),
        name="place",
    )(jnp.stack(columns).astype(jnp.int32), *received, held)


def on_device(queries, image_tokens, kv_weight, attn_gate, image_counts, response_lengths):
    rows = queries.shape[1]
    head_dim = kv_weight.shape[3]
    width = queries.shape[2] // 8
    z, xh, y, c = (lax.axis_index(a) for a in (Z, XH, Y, C))
    xl = lax.axis_index(XL)
    q = queries[0]
    image = image_tokens[0].T
    w_own = kv_weight[:, 0].transpose(1, 2, 0).reshape(2 * head_dim, -1)

    others = ((1, 0), (1, 1), (0, 1))

    def to_other(value, dx, dc):
        return lax.ppermute(value, (XH, C), [(i, i ^ (dx * 2 + dc)) for i in range(4)])

    def column_of(dx, dc, chunk):
        step = jnp.where((xh ^ dx) == 0, chunk, 3 - chunk)
        return (c ^ dc) * 4 + (z + step) % 4

    def position_of(dx, dc):
        return (((xh ^ dx) * 4 + y) * 2 + (c ^ dc)) * rows

    def query_slice(dx, dc):
        cut = [lax.dynamic_slice_in_dim(q, column_of(dx, dc, chunk) * width, width, axis=1) for chunk in (0, 1)]
        return jnp.stack(cut)

    def exchange(values):
        return [to_other(value, dx, dc) for value, (dx, dc) in zip(values, others)]

    firsts = [lax.ppermute(w_own, (XL, Z, C), weight_round(flip)) for flip in range(2)]
    image_other = lax.ppermute(image, C, ring(2, 1))
    swapped = (xl ^ c) == 1
    stack = jnp.stack([jnp.where(swapped, firsts[1], firsts[0]), jnp.where(swapped, firsts[0], firsts[1])])
    w_prev = lax.ppermute(stack, Z, ring(4, 1))
    w_next = lax.ppermute(stack, Z, ring(4, -1))
    w_far = lax.ppermute(stack, Z, ring(4, 2))
    q_got = exchange([query_slice(dx, dc) for dx, dc in others])

    count = image_counts[0]
    sum_info = jnp.stack([count, (y < 2).astype(jnp.int32)])
    gate = jnp.tanh(attn_gate)

    parts_0 = project(stack, image, image_other, 0, w_own)
    parts_0 = project(w_prev, image, image_other, 1, parts_0)
    parts_0, w_next, q_got = lax.optimization_barrier((parts_0, w_next, q_got))
    parts_0 = lax.all_to_all(parts_0, CHIPS, 0, 0, tiled=True)
    parts_1 = project(w_next, image, image_other, 0, w_own)
    parts_1 = project(w_far, image, image_other, 1, parts_1)
    parts_1, parts_0 = lax.optimization_barrier((parts_1, parts_0))
    parts_1 = lax.all_to_all(parts_1, CHIPS, 0, 0, tiled=True)
    sum_0 = sum_parts(sum_info, parts_0)
    sum_0, parts_1 = lax.optimization_barrier((sum_0, parts_1))
    kv_0 = lax.all_to_all(sum_0, Y, 0, 0, tiled=True)
    sum_1 = sum_parts(sum_info, parts_1)
    kv_1 = lax.all_to_all(sum_1, Y, 0, 0, tiled=True)

    def scalars_of(chunk, groups):
        values = [column_of(0, 0, chunk), count] + [position_of(*g) for g in groups] + [response_lengths[0]]
        return jnp.stack(values).astype(jnp.int32)

    out = None
    for chunk, kv in enumerate((kv_0, kv_1)):
        far, far_other, near = q_got
        scalars = scalars_of(chunk, others[:2])
        give = attend(scalars, gate, kv, far, far_other, near if out is None else out, head_dim, 0, chunk)
        held = give[0] if out is None else out
        scalars = scalars_of(chunk, ((0, 0), (0, 1)))
        out, give_near = attend(scalars, gate, kv, q, near, held, head_dim, 1 if out is None else 2, chunk)
        got = exchange([give[0], give[1], give_near])
        out = place([column_of(dx, dc, chunk) for dx, dc in others], got, out)
    return out[None]


def solution(mesh):
    fine = Mesh(mesh.devices.reshape(2, 4, 2, 4, 2), (XL, Z, XH, Y, C))
    sample, head = (XL, Z), (XH, Y, C)
    placed = (
        P(sample, head, None),
        P(sample, None, head),
        P(head, sample, None, None),
        P(),
        P(sample),
        P(sample),
    )
    return jax.shard_map(
        on_device, mesh=fine, in_specs=placed, out_specs=P(sample, head, None), check_vma=False
    )
```

time: 186 us -> 166 us (0.89)
  Pallas kernels: 47.1 us -> 36.7 us
  starting transfers between devices: 50.7 us -> 43 us
  waiting for transfers between devices: 74 us -> 67.1 us
  other arithmetic: 1.2 us -> 4.08 us
  local copies, waits for them, and re-layouts: 9.89 us -> 12.5 us
    all_to_all x6 -> x4, starting transfers between devices: 36.8 us -> 16.8 us  [the longest x1 4.85 us: on_device(): parts_0 = lax.all_to_all(parts_0, CHIPS, 0, 0, tiled=True)]
    ppermute x5 -> x9, waiting for transfers between devices: 0.01 us -> 15.2 us  [to_other(): lax.ppermute(value, (XH, C), [(i, i ^ dx * 2 + dc) for i in range(4)])]
    ppermute x5 -> x9, starting transfers between devices: 2.07 us -> 14.1 us  [to_other(): lax.ppermute(value, (XH, C), [(i, i ^ dx * 2 + dc) for i in range(4)])]
    all_to_all x6 -> x4, waiting for transfers between devices: 43.3 us -> 31.7 us  [the longest x1 18.5 us: on_device(): parts_1 = lax.all_to_all(parts_1, CHIPS, 0, 0, tiled=True)]
    ppermute x2, waiting for transfers between devices: 7.28 us -> 0.01 us  [on_device(): lax.ppermute(w_own, (XL, Z, C), weight_round(flip))]
    pallas_call x4, Pallas kernels: 31.1 us -> 24.8 us  [attend(): pl.pallas_call(functools.partial(attend_kernel, head_dim), out_shape=[jax...]
    another operation x1 -> x6, other arithmetic: 0.08 us -> 2.91 us  [the longest x3 2.68 us: query_slice(): return jnp.stack(cut)]
    unnamed x14 -> x32, local copies, waits for them, and re-layouts: 6.17 us -> 8.72 us
  transfers between devices with their start and end apart: 17 -> 19, of which waited for: 7 -> 9; matrix products, arithmetic and copies ran while one was open for 3% -> 5% of each run, Pallas kernels for 24% -> 17%
where the time goes in v2:
time: 166 us
  waiting for transfers between devices  67.1 us (40%)
  starting transfers between devices  43 us (26%)
  Pallas kernels  36.7 us (22%)
  local copies, waits for them, and re-layouts  12.5 us (8%)
  other arithmetic  4.08 us (2%)
  between operations  2.47 us (1%)
    pallas_call x4, Pallas kernels, attend(): pl.pallas_call(functools.partial(attend_kernel, head_dim), out_shape=[jax...  24.8 us
    all_to_all x1, waiting for transfers between devices, on_device(): parts_1 = lax.all_to_all(parts_1, CHIPS, 0, 0, tiled=True)  18.5 us
    ppermute x9, waiting for transfers between devices, to_other(): lax.ppermute(value, (XH, C), [(i, i ^ dx * 2 + dc) for i in range(4)])  15.2 us
    ppermute x9, starting transfers between devices, to_other(): lax.ppermute(value, (XH, C), [(i, i ^ dx * 2 + dc) for i in range(4)])  14.1 us
    ppermute x1, waiting for transfers between devices, on_device(): w_far = lax.ppermute(stack, Z, ring(4, 2))  10.1 us
    ppermute x1, waiting for transfers between devices, on_device(): w_prev = lax.ppermute(stack, Z, ring(4, 1))  9.99 us
    all_to_all x1, waiting for transfers between devices, on_device(): kv_0 = lax.all_to_all(sum_0, Y, 0, 0, tiled=True)  9.04 us
    unnamed x32, local copies, waits for them, and re-layouts  8.72 us
  transfers between devices with their start and end apart: 19, of which 9 were waited for; matrix products, arithmetic and copies ran while one was open for 5% of the time, Pallas kernels for 17%

profile of v2, /device:TPU:1, one launch (start us, length us, event | category | flops | bytes accessed | tf_op | source)
XLA Modules:
  0.0 165.8 jit_solution(317971638835306752)
XLA Ops:
  0.0 1.4 collective-permute-start.3
  1.4 1.1 copy.12
  2.5 3.1 %collective-permute-start.1 = (bf16[256,480]{1,0:T(8,128)(2,1)S(1)}, bf16[256,480]{1,0:T(8,128)(2,1)}, u32[]{:S(2)}, u32[]{:S(2)}) collective-permute-start(bf16[256,480]{1,0:T(8,128)(2,1)S(1)} %bitcast.31), channel_id=1, source_target_pairs={{0,0},{1,64},{16,16},{17,80},{32,32},{33,96},{48,48},{49,112},{64,... | collective-permute-start | bytes 737288 | tf_op jit(solution)/shard_map/ppermute | solution.py:208
  5.8 2.3 %constant_dynamic-slice_fusion.1 = (bf16[1,128,1024]{2,1,0:T(8,128)(2,1)}, bf16[1,128,1024]{2,1,0:T(8,128)(2,1)S(1)}, bf16[1,128,1024]{2,1,0:T(8,128)(2,1)S(1)},...) fusion(bf16[1,128,8192]{2,1,0:T(8,128)(2,1)} %param.6, ...), kind=kLoop, calls=%fused_computation.7 | loop fusion | bytes 3145752 | tf_op jit(solution)/shard_map/dynamic_slice | solution.py:202
  8.1 0.8 pad_maximum_fusion.1
  9.0 2.5 %collective-permute-start.6 = (bf16[2,128,1024]{2,1,0:T(8,128)(2,1)}, bf16[2,128,1024]{2,1,0:T(8,128)(2,1)}, u32[]{:S(2)}, u32[]{:S(2)}) collective-permute-start(bf16[2,128,1024]{2,1,0:T(8,128)(2,1)} %pad_maximum_fusion.1), channel_id=1, source_target_pairs={{0,8},{1,9},{8,0},{9,1},{2,10},{3,11},{10,2},{11,3},{4,12},{5,13},... | collective-permute-start | bytes 1572872 | tf_op jit(solution)/shard_map/ppermute | solution.py:192
  11.4 0.8 pad_maximum_fusion.2
  12.3 1.5 collective-permute-start.7
  13.8 1.1 select_bitcast_fusion.1
  15.0 1.8 %collective-permute-start.4 = (bf16[2,256,480]{2,1,0:T(8,128)(2,1)S(1)}, bf16[2,256,480]{2,1,0:T(8,128)(2,1)S(1)}, u32[]{:S(2)}, u32[]{:S(2)}) collective-permute-start(bf16[2,256,480]{2,1,0:T(8,128)(2,1)S(1)} %pad_maximum_fusion.w_ref), channel_id=1, source_target_pairs={{0,16},{16,32},{32,48},{48,0},{1,17},{17,33},{33,49},{49,1},{2,18}... | collective-permute-start | bytes 1474568 | tf_op jit(solution)/shard_map/ppermute | solution.py:212
  16.8 1.0 pad_maximum_fusion.3
  18.2 2.1 %collective-permute-start.5 = (bf16[2,256,480]{2,1,0:T(8,128)(2,1)S(1)}, bf16[2,256,480]{2,1,0:T(8,128)(2,1)S(1)}, u32[]{:S(2)}, u32[]{:S(2)}) collective-permute-start(bf16[2,256,480]{2,1,0:T(8,128)(2,1)S(1)} %pad_maximum_fusion.w_ref), channel_id=1, source_target_pairs={{0,48},{16,0},{32,16},{48,32},{1,49},{17,1},{33,17},{49,33},{2,50}... | collective-permute-start | bytes 1474568 | tf_op jit(solution)/shard_map/ppermute | solution.py:213
  20.2 1.1 project.4.held
  21.3 10.0 %collective-permute-done.4.w_ref = bf16[2,256,480]{2,1,0:T(8,128)(2,1)S(1)} collective-permute-done((bf16[2,256,480]{2,1,0:T(8,128)(2,1)S(1)}, bf16[2,256,480]{2,1,0:T(8,128)(2,1)S(1)}, u32[]{:S(2)}, u32[]{:S(2)}) %collective-permute-start.4) | collective-permute-done | bytes 491552 | tf_op jit(solution)/shard_map/ppermute | solution.py:212
  31.3 1.1 project.5
  32.5 1.2 copy-done.2
  33.7 3.5 %collective-permute-done.7.q_1 = bf16[2,128,1024]{2,1,0:T(8,128)(2,1)} collective-permute-done((bf16[2,128,1024]{2,1,0:T(8,128)(2,1)}, bf16[2,128,1024]{2,1,0:T(8,128)(2,1)}, u32[]{:S(2)}, u32[]{:S(2)}) %collective-permute-start.7) | collective-permute-done | bytes 524320 | tf_op jit(solution)/shard_map/ppermute | solution.py:192
  37.2 0.8 copy-done.11
  38.0 0.8 copy-done.9
  38.8 4.9 %all-to-all-start = ((bf16[8,64,1664]{2,1,0:T(8,128)(2,1)}), bf16[8,64,1664]{2,1,0:T(8,128)(2,1)}, u32[]{:S(2)}, u32[]{:S(2)}) async-start(bf16[8,64,1664]{2,1,0:T(8,128)(2,1)} %copy-done.2), calls=%async_computation | async-start | bytes 3407872 | tf_op jit(solution)/shard_map/all_to_all | solution.py:224
  43.7 3.6 %collective-permute-start.2 = (bf16[2,256,480]{2,1,0:T(8,128)(2,1)}, bf16[2,256,480]{2,1,0:T(8,128)(2,1)S(1)}, u32[]{:S(2)}, u32[]{:S(2)}) collective-permute-start(bf16[2,256,480]{2,1,0:T(8,128)(2,1)} %copy-done.4), channel_id=1, source_target_pairs={{0,32},{16,48},{32,0},{48,16},{1,33},{17,49},{33,1},{49,17},{2,34}... | collective-permute-start | bytes 1474568 | tf_op jit(solution)/shard_map/ppermute | solution.py:214
  47.3 1.0 copy-done.10
  48.3 1.1 project.6.held
  49.4 10.1 %collective-permute-done.2.w_ref = bf16[2,256,480]{2,1,0:T(8,128)(2,1)S(1)} collective-permute-done((bf16[2,256,480]{2,1,0:T(8,128)(2,1)}, bf16[2,256,480]{2,1,0:T(8,128)(2,1)S(1)}, u32[]{:S(2)}, u32[]{:S(2)}) %collective-permute-start.2) | collective-permute-done | bytes 491552 | tf_op jit(solution)/shard_map/ppermute | solution.py:214
  59.5 1.1 project.7
  60.7 1.2 copy-done.1
  61.8 4.2 %all-to-all-done.parts_ref = bf16[8,64,1664]{2,1,0:T(8,128)(2,1)} async-done(((bf16[8,64,1664]{2,1,0:T(8,128)(2,1)}), bf16[8,64,1664]{2,1,0:T(8,128)(2,1)}, u32[]{:S(2)}, u32[]{:S(2)}) %all-to-all-start) | async-done | bytes 1703968 | tf_op jit(solution)/shard_map/all_to_all | solution.py:224
  66.0 4.7 %all-to-all-start.1 = ((bf16[8,64,1664]{2,1,0:T(8,128)(2,1)}), bf16[8,64,1664]{2,1,0:T(8,128)(2,1)S(1)}, u32[]{:S(2)}, u32[]{:S(2)}) async-start(bf16[8,64,1664]{2,1,0:T(8,128)(2,1)} %copy-done.1), calls=%async_computation.1 | async-start | bytes 3407872 | tf_op jit(solution)/shard_map/all_to_all | solution.py:228
  71.5 2.7 %sum_parts.2 = bf16[4,64,1664]{2,1,0:T(8,128)(2,1)} custom-call(s32[2]{0:T(128)S(1)} %pad_add_fusion.1.info_ref, bf16[8,64,1664]{2,1,0:T(8,128)(2,1)} %all-to-all-done.parts_ref), custom_call_target="tpu_custom_call" | custom-call | flops 1048576 | bytes 4194304 | tf_op jit(solution)/shard_map/sum_parts/pallas_call | solution.py:74
  74.2 18.5 %all-to-all-done.1.parts_ref = bf16[8,64,1664]{2,1,0:T(8,128)(2,1)S(1)} async-done(((bf16[8,64,1664]{2,1,0:T(8,128)(2,1)}), bf16[8,64,1664]{2,1,0:T(8,128)(2,1)S(1)}, u32[]{:S(2)}, u32[]{:S(2)}) %all-to-all-start.1) | async-done | bytes 1703968 | tf_op jit(solution)/shard_map/all_to_all | solution.py:228
  92.7 3.5 %all-to-all-start.3 = ((bf16[4,64,1664]{2,1,0:T(8,128)(2,1)}), bf16[4,64,1664]{2,1,0:T(8,128)(2,1)S(1)}, u32[]{:S(2)}, u32[]{:S(2)}) async-start(bf16[4,64,1664]{2,1,0:T(8,128)(2,1)} %sum_parts.2), calls=%async_computation.3 | async-start | bytes 1703936 | tf_op jit(solution)/shard_map/all_to_all | solution.py:231
  96.3 1.8 %sum_parts.3 = bf16[4,64,1664]{2,1,0:T(8,128)(2,1)} custom-call(s32[2]{0:T(128)S(1)} %pad_add_fusion.1.info_ref, bf16[8,64,1664]{2,1,0:T(8,128)(2,1)S(1)} %all-to-all-done.1.parts_ref), custom_call_target="tpu_custom_call" | custom-call | flops 1048576 | bytes 4194304 | tf_op jit(solution)/shard_map/sum_parts/pallas_call | solution.py:74
  98.1 9.0 %all-to-all-done.3.kv_ref = bf16[4,64,1664]{2,1,0:T(8,128)(2,1)S(1)} async-done(((bf16[4,64,1664]{2,1,0:T(8,128)(2,1)}), bf16[4,64,1664]{2,1,0:T(8,128)(2,1)S(1)}, u32[]{:S(2)}, u32[]{:S(2)}) %all-to-all-start.3) | async-done | bytes 852000 | tf_op jit(solution)/shard_map/all_to_all | solution.py:231
  107.1 0.9 copy-done.7
  108.0 3.7 %all-to-all-start.2 = ((bf16[4,64,1664]{2,1,0:T(8,128)(2,1)}), bf16[4,64,1664]{2,1,0:T(8,128)(2,1)S(1)}, u32[]{:S(2)}, u32[]{:S(2)}) async-start(bf16[4,64,1664]{2,1,0:T(8,128)(2,1)} %sum_parts.3), calls=%async_computation.2 | async-start | bytes 1703936 | tf_op jit(solution)/shard_map/all_to_all | solution.py:233
  113.2 1.2 copy-done.8
  114.4 6.5 %attend.4 = (bf16[128,1024]{1,0:T(8,128)(2,1)S(1)}, bf16[128,1024]{1,0:T(8,128)(2,1)S(1)}) custom-call(s32[5]{0:T(128)S(1)} %stack.115.scalars, f32[1]{0:T(128)S(6)} %tanh.3.gate_ref, bf16[4,64,1664]{2,1,0:T(8,128)(2,1)S(1)} %copy-done.8, bf16[2,128,1024]{2,1,0:T(8,128)(2,1)} %collective-permute-done.6.q_0, ...), custom_call_target="tpu_custom_call" | custom-call | flops 1744830464 | bytes 4194304 | tf_op jit(solution)/shard_map/attend/pallas_call | solution.py:132
  120.9 5.7 %collective-permute-start.10 = (bf16[128,1024]{1,0:T(8,128)(2,1)S(1)}, bf16[128,1024]{1,0:T(8,128)(2,1)S(1)}, u32[]{:S(2)}, u32[]{:S(2)}) collective-permute-start(bf16[128,1024]{1,0:T(8,128)(2,1)S(1)} %get-tuple-element.32), channel_id=1, source_target_pairs={{0,9},{1,8},{8,1},{9,0},{2,11},{3,10},{10,3},{11,2},{4,13},{5,12},... | collective-permute-start | bytes 786440 | tf_op jit(solution)/shard_map/ppermute | solution.py:192
  126.9 5.9 %attend.5 = (bf16[128,8192]{1,0:T(8,128)(2,1)}, bf16[128,1024]{1,0:T(8,128)(2,1)S(1)}) custom-call(s32[5]{0:T(128)S(1)} %stack.118.scalars, f32[1]{0:T(128)S(6)} %tanh.3.gate_ref, bf16[4,64,1664]{2,1,0:T(8,128)(2,1)S(1)} %copy-done.8, bf16[128,8192]{1,0:T(8,128)(2,1)S(1)} %bitcast.35, bf16[2,128,1024]{2,1,0:T(8,128)(2,1)S(1)} %copy-done.13, ...), custom_call_target="tpu_custom_call" | custom-call | flops 1744830464 | bytes 4194304 | tf_op jit(solution)/shard_map/attend/pallas_call | solution.py:132
  133.7 5.6 %collective-permute-done.9.refs_0_ = bf16[128,1024]{1,0:T(8,128)(2,1)S(1)} collective-permute-done((bf16[128,1024]{1,0:T(8,128)(2,1)S(1)}, bf16[128,1024]{1,0:T(8,128)(2,1)S(1)}, u32[]{:S(2)}, u32[]{:S(2)}) %collective-permute-start.9) | collective-permute-done | bytes 262176 | tf_op jit(solution)/shard_map/ppermute | solution.py:192
  139.3 1.4 place.2.held
  140.8 1.6 copy-done.3
  142.4 6.5 %attend.6 = (bf16[128,1024]{1,0:T(8,128)(2,1)S(1)}, bf16[128,1024]{1,0:T(8,128)(2,1)S(1)}) custom-call(s32[5]{0:T(128)S(1)} %stack.100.scalars, f32[1]{0:T(128)S(6)} %tanh.3.gate_ref, bf16[4,64,1664]{2,1,0:T(8,128)(2,1)S(1)} %all-to-all-done.2.kv_ref, bf16[2,128,1024]{2,1,0:T(8,128)(2,1)} %collective-permute-done.6.q_0, ...), custom_call_target="tpu_custom_call" | custom-call | flops 1744830464 | bytes 4194304 | tf_op jit(solution)/shard_map/attend/pallas_call | solution.py:132
  148.9 1.5 collective-permute-start.12
  150.4 2.1 %collective-permute-start.13 = (bf16[128,1024]{1,0:T(8,128)(2,1)S(1)}, bf16[128,1024]{1,0:T(8,128)(2,1)S(1)}, u32[]{:S(2)}, u32[]{:S(2)}) collective-permute-start(bf16[128,1024]{1,0:T(8,128)(2,1)S(1)} %get-tuple-element.36), channel_id=1, source_target_pairs={{0,9},{1,8},{8,1},{9,0},{2,11},{3,10},{10,3},{11,2},{4,13},{5,12},... | collective-permute-start | bytes 786440 | tf_op jit(solution)/shard_map/ppermute | solution.py:192
  152.5 5.9 %attend.7 = (bf16[128,8192]{1,0:T(8,128)(2,1)}, bf16[128,1024]{1,0:T(8,128)(2,1)S(1)}) custom-call(s32[5]{0:T(128)S(1)} %stack.119.scalars, f32[1]{0:T(128)S(6)} %tanh.3.gate_ref, bf16[4,64,1664]{2,1,0:T(8,128)(2,1)S(1)} %all-to-all-done.2.kv_ref, bf16[128,8192]{1,0:T(8,128)(2,1)S(1)} %bitcast.36, ...), custom_call_target="tpu_custom_call", output_to_operand_aliasing={{0}: (5, {})} | custom-call | flops 1744830464 | bytes 4194304 | tf_op jit(solution)/shard_map/attend/pallas_call | solution.py:132
  158.5 5.6 %collective-permute-done.13.refs_1_ = bf16[128,1024]{1,0:T(8,128)(2,1)S(1)} collective-permute-done((bf16[128,1024]{1,0:T(8,128)(2,1)S(1)}, bf16[128,1024]{1,0:T(8,128)(2,1)S(1)}, u32[]{:S(2)}, u32[]{:S(2)}) %collective-permute-start.13) | collective-permute-done | bytes 262176 | tf_op jit(solution)/shard_map/ppermute | solution.py:192
  164.1 1.4 place.3
  (48 shorter events, 2.1 us)
Async XLA Ops:
  0.0 18.2 %collective-permute-start.3 = (bf16[480,1664]{1,0:T(8,128)(2,1)}, bf16[480,1664]{1,0:T(8,128)(2,1)S(1)}, u32[]{:S(2)}, u32[]{:S(2)}) collective-permute-start(bf16[480,1664]{1,0:T(8,128)(2,1)} %bitcast.26), channel_id=1, source_target_pairs={{0,1},{1,0},{2,3},{3,2},{4,5},{5,4},{6,7},{7,6},{8,9},{9,8},{10,11... | collective-permute-start | bytes 4792328 | tf_op jit(solution)/shard_map/ppermute | solution.py:209
  2.5 11.3 %collective-permute-start.1 = (bf16[256,480]{1,0:T(8,128)(2,1)S(1)}, bf16[256,480]{1,0:T(8,128)(2,1)}, u32[]{:S(2)}, u32[]{:S(2)}) collective-permute-start(bf16[256,480]{1,0:T(8,128)(2,1)S(1)} %bitcast.31), channel_id=1, source_target_pairs={{0,0},{1,64},{16,16},{17,80},{32,32},{33,96},{48,48},{49,112},{64,... | collective-permute-start | bytes 737288 | tf_op jit(solution)/shard_map/ppermute | solution.py:208
  5.6 8.2 %collective-permute-start = (bf16[256,480]{1,0:T(8,128)(2,1)S(1)}, bf16[256,480]{1,0:T(8,128)(2,1)}, u32[]{:S(2)}, u32[]{:S(2)}) collective-permute-start(bf16[256,480]{1,0:T(8,128)(2,1)S(1)} %bitcast.32), channel_id=1, source_target_pairs={{0,64},{1,0},{16,80},{17,16},{32,96},{33,32},{48,112},{49,48},{64,... | collective-permute-start | bytes 737288 | tf_op jit(solution)/shard_map/ppermute | solution.py:208
  9.0 24.7 %collective-permute-start.6 = (bf16[2,128,1024]{2,1,0:T(8,128)(2,1)}, bf16[2,128,1024]{2,1,0:T(8,128)(2,1)}, u32[]{:S(2)}, u32[]{:S(2)}) collective-permute-start(bf16[2,128,1024]{2,1,0:T(8,128)(2,1)} %pad_maximum_fusion.1), channel_id=1, source_target_pairs={{0,8},{1,9},{8,0},{9,1},{2,10},{3,11},{10,2},{11,3},{4,12},{5,13},... | collective-permute-start | bytes 1572872 | tf_op jit(solution)/shard_map/ppermute | solution.py:192
  12.3 7.9 %copy-start = (bf16[1,1664,480]{1,2,0:T(8,128)(2,1)S(1)}, bf16[1,1664,480]{1,2,0:T(8,128)(2,1)}, u32[]{:S(2)}) copy-start(bf16[1,1664,480]{1,2,0:T(8,128)(2,1)} %param.7) | copy-start | bytes 4792324
  12.3 24.9 %collective-permute-start.7 = (bf16[2,128,1024]{2,1,0:T(8,128)(2,1)}, bf16[2,128,1024]{2,1,0:T(8,128)(2,1)}, u32[]{:S(2)}, u32[]{:S(2)}) collective-permute-start(bf16[2,128,1024]{2,1,0:T(8,128)(2,1)} %pad_maximum_fusion.2), channel_id=1, source_target_pairs={{0,9},{1,8},{8,1},{9,0},{2,11},{3,10},{10,3},{11,2},{4,13},{5,12},... | collective-permute-start | bytes 1572872 | tf_op jit(solution)/shard_map/ppermute | solution.py:192
  13.8 3.0 %copy-start.15 = (bf16[1,128,1024]{2,1,0:T(8,128)(2,1)S(1)}, bf16[1,128,1024]{2,1,0:T(8,128)(2,1)}, u32[]{:S(2)}) copy-start(bf16[1,128,1024]{2,1,0:T(8,128)(2,1)} %get-tuple-element.39) | copy-start | bytes 786436
  15.0 6.3 %copy-start.4 = (bf16[2,256,480]{2,1,0:T(8,128)(2,1)}, bf16[2,256,480]{2,1,0:T(8,128)(2,1)S(1)}, u32[]{:S(2)}) copy-start(bf16[2,256,480]{2,1,0:T(8,128)(2,1)S(1)} %pad_maximum_fusion.w_ref) | copy-start | bytes 1474564
  15.0 16.3 %collective-permute-start.4 = (bf16[2,256,480]{2,1,0:T(8,128)(2,1)S(1)}, bf16[2,256,480]{2,1,0:T(8,128)(2,1)S(1)}, u32[]{:S(2)}, u32[]{:S(2)}) collective-permute-start(bf16[2,256,480]{2,1,0:T(8,128)(2,1)S(1)} %pad_maximum_fusion.w_ref), channel_id=1, source_target_pairs={{0,16},{16,32},{32,48},{48,0},{1,17},{17,33},{33,49},{49,1},{2,18}... | collective-permute-start | bytes 1474568 | tf_op jit(solution)/shard_map/ppermute | solution.py:212
  17.8 19.4 %collective-permute-start.8 = (bf16[2,128,1024]{2,1,0:T(8,128)(2,1)S(1)}, bf16[2,128,1024]{2,1,0:T(8,128)(2,1)S(1)}, u32[]{:S(2)}, u32[]{:S(2)}) collective-permute-start(bf16[2,128,1024]{2,1,0:T(8,128)(2,1)S(1)} %pad_maximum_fusion.3), channel_id=1, source_target_pairs={{0,1},{1,0},{8,9},{9,8},{2,3},{3,2},{10,11},{11,10},{4,5},{5,4},{1... | collective-permute-start | bytes 1572872 | tf_op jit(solution)/shard_map/ppermute | solution.py:192
  18.2 19.9 %collective-permute-start.5 = (bf16[2,256,480]{2,1,0:T(8,128)(2,1)S(1)}, bf16[2,256,480]{2,1,0:T(8,128)(2,1)S(1)}, u32[]{:S(2)}, u32[]{:S(2)}) collective-permute-start(bf16[2,256,480]{2,1,0:T(8,128)(2,1)S(1)} %pad_maximum_fusion.w_ref), channel_id=1, source_target_pairs={{0,48},{16,0},{32,16},{48,32},{1,49},{17,1},{33,17},{49,33},{2,50}... | collective-permute-start | bytes 1474568 | tf_op jit(solution)/shard_map/ppermute | solution.py:213
  32.4 1.2 copy-start.2
  37.2 0.8 copy-start.11
  38.0 0.8 copy-start.9
  38.8 27.2 %all-to-all-start = ((bf16[8,64,1664]{2,1,0:T(8,128)(2,1)}), bf16[8,64,1664]{2,1,0:T(8,128)(2,1)}, u32[]{:S(2)}, u32[]{:S(2)}) async-start(bf16[8,64,1664]{2,1,0:T(8,128)(2,1)} %copy-done.2), calls=%async_computation | async-start | bytes 3407872 | tf_op jit(solution)/shard_map/all_to_all | solution.py:224
  43.7 15.9 %collective-permute-start.2 = (bf16[2,256,480]{2,1,0:T(8,128)(2,1)}, bf16[2,256,480]{2,1,0:T(8,128)(2,1)S(1)}, u32[]{:S(2)}, u32[]{:S(2)}) collective-permute-start(bf16[2,256,480]{2,1,0:T(8,128)(2,1)} %copy-done.4), channel_id=1, source_target_pairs={{0,32},{16,48},{32,0},{48,16},{1,33},{17,49},{33,1},{49,17},{2,34}... | collective-permute-start | bytes 1474568 | tf_op jit(solution)/shard_map/ppermute | solution.py:214
  47.3 1.0 copy-start.10
  60.7 1.2 copy-start.1
  66.0 26.7 %all-to-all-start.1 = ((bf16[8,64,1664]{2,1,0:T(8,128)(2,1)}), bf16[8,64,1664]{2,1,0:T(8,128)(2,1)S(1)}, u32[]{:S(2)}, u32[]{:S(2)}) async-start(bf16[8,64,1664]{2,1,0:T(8,128)(2,1)} %copy-done.1), calls=%async_computation.1 | async-start | bytes 3407872 | tf_op jit(solution)/shard_map/all_to_all | solution.py:228
  92.7 14.4 %all-to-all-start.3 = ((bf16[4,64,1664]{2,1,0:T(8,128)(2,1)}), bf16[4,64,1664]{2,1,0:T(8,128)(2,1)S(1)}, u32[]{:S(2)}, u32[]{:S(2)}) async-start(bf16[4,64,1664]{2,1,0:T(8,128)(2,1)} %sum_parts.2), calls=%async_computation.3 | async-start | bytes 1703936 | tf_op jit(solution)/shard_map/all_to_all | solution.py:231
  96.3 17.0 %copy-start.12 = (bf16[2,128,1024]{2,1,0:T(8,128)(2,1)S(1)}, bf16[2,128,1024]{2,1,0:T(8,128)(2,1)}, u32[]{:S(2)}) copy-start(bf16[2,128,1024]{2,1,0:T(8,128)(2,1)} %copy-done.11) | copy-start | bytes 1572868
  107.1 0.9 copy-start.7
  108.0 32.7 %all-to-all-start.2 = ((bf16[4,64,1664]{2,1,0:T(8,128)(2,1)}), bf16[4,64,1664]{2,1,0:T(8,128)(2,1)S(1)}, u32[]{:S(2)}, u32[]{:S(2)}) async-start(bf16[4,64,1664]{2,1,0:T(8,128)(2,1)} %sum_parts.3), calls=%async_computation.2 | async-start | bytes 1703936 | tf_op jit(solution)/shard_map/all_to_all | solution.py:233
  113.2 1.2 copy-start.8
  114.4 12.5 %copy-start.5 = (bf16[1,128,8192]{2,1,0:T(8,128)(2,1)S(1)}, bf16[1,128,8192]{2,1,0:T(8,128)(2,1)}, u32[]{:S(2)}) copy-start(bf16[1,128,8192]{2,1,0:T(8,128)(2,1)} %param.6) | copy-start | bytes 6291460
  114.4 12.5 %copy-start.13 = (bf16[2,128,1024]{2,1,0:T(8,128)(2,1)S(1)}, bf16[2,128,1024]{2,1,0:T(8,128)(2,1)}, u32[]{:S(2)}) copy-start(bf16[2,128,1024]{2,1,0:T(8,128)(2,1)} %copy-done.11) | copy-start | bytes 1572868
  120.9 12.8 %collective-permute-start.10 = (bf16[128,1024]{1,0:T(8,128)(2,1)S(1)}, bf16[128,1024]{1,0:T(8,128)(2,1)S(1)}, u32[]{:S(2)}, u32[]{:S(2)}) collective-permute-start(bf16[128,1024]{1,0:T(8,128)(2,1)S(1)} %get-tuple-element.32), channel_id=1, source_target_pairs={{0,9},{1,8},{8,1},{9,0},{2,11},{3,10},{10,3},{11,2},{4,13},{5,12},... | collective-permute-start | bytes 786440 | tf_op jit(solution)/shard_map/ppermute | solution.py:192
  126.6 12.7 %collective-permute-start.9 = (bf16[128,1024]{1,0:T(8,128)(2,1)S(1)}, bf16[128,1024]{1,0:T(8,128)(2,1)S(1)}, u32[]{:S(2)}, u32[]{:S(2)}) collective-permute-start(bf16[128,1024]{1,0:T(8,128)(2,1)S(1)} %get-tuple-element.31.held), channel_id=1, source_target_pairs={{0,8},{1,9},{8,0},{9,1},{2,10},{3,11},{10,2},{11,3},{4,12},{5,13},... | collective-permute-start | bytes 786440 | tf_op jit(solution)/shard_map/ppermute | solution.py:192
  132.8 6.5 %collective-permute-start.11 = (bf16[128,1024]{1,0:T(8,128)(2,1)S(1)}, bf16[128,1024]{1,0:T(8,128)(2,1)S(1)}, u32[]{:S(2)}, u32[]{:S(2)}) collective-permute-start(bf16[128,1024]{1,0:T(8,128)(2,1)S(1)} %get-tuple-element.33), channel_id=1, source_target_pairs={{0,1},{1,0},{8,9},{9,8},{2,3},{3,2},{10,11},{11,10},{4,5},{5,4},{1... | collective-permute-start | bytes 786440 | tf_op jit(solution)/shard_map/ppermute | solution.py:192
  140.8 1.6 copy-start.3
  142.4 10.2 %copy-start.6 = (bf16[1,128,8192]{2,1,0:T(8,128)(2,1)S(1)}, bf16[1,128,8192]{2,1,0:T(8,128)(2,1)}, u32[]{:S(2)}) copy-start(bf16[1,128,8192]{2,1,0:T(8,128)(2,1)} %param.6) | copy-start | bytes 6291460
  142.4 10.2 %copy-start.14 = (bf16[2,128,1024]{2,1,0:T(8,128)(2,1)S(1)}, bf16[2,128,1024]{2,1,0:T(8,128)(2,1)}, u32[]{:S(2)}) copy-start(bf16[2,128,1024]{2,1,0:T(8,128)(2,1)} %copy-done.11) | copy-start | bytes 1572868
  148.9 9.6 %collective-permute-start.12 = (bf16[128,1024]{1,0:T(8,128)(2,1)S(1)}, bf16[128,1024]{1,0:T(8,128)(2,1)S(1)}, u32[]{:S(2)}, u32[]{:S(2)}) collective-permute-start(bf16[128,1024]{1,0:T(8,128)(2,1)S(1)} %get-tuple-element.35), channel_id=1, source_target_pairs={{0,8},{1,9},{8,0},{9,1},{2,10},{3,11},{10,2},{11,3},{4,12},{5,13},... | collective-permute-start | bytes 786440 | tf_op jit(solution)/shard_map/ppermute | solution.py:192
  150.4 13.7 %collective-permute-start.13 = (bf16[128,1024]{1,0:T(8,128)(2,1)S(1)}, bf16[128,1024]{1,0:T(8,128)(2,1)S(1)}, u32[]{:S(2)}, u32[]{:S(2)}) collective-permute-start(bf16[128,1024]{1,0:T(8,128)(2,1)S(1)} %get-tuple-element.36), channel_id=1, source_target_pairs={{0,9},{1,8},{8,1},{9,0},{2,11},{3,10},{10,3},{11,2},{4,13},{5,12},... | collective-permute-start | bytes 786440 | tf_op jit(solution)/shard_map/ppermute | solution.py:192
  158.4 5.7 %collective-permute-start.14 = (bf16[128,1024]{1,0:T(8,128)(2,1)S(1)}, bf16[128,1024]{1,0:T(8,128)(2,1)S(1)}, u32[]{:S(2)}, u32[]{:S(2)}) collective-permute-start(bf16[128,1024]{1,0:T(8,128)(2,1)S(1)} %get-tuple-element.37), channel_id=1, source_target_pairs={{0,1},{1,0},{8,9},{9,8},{2,3},{3,2},{10,11},{11,10},{4,5},{5,4},{1... | collective-permute-start | bytes 786440 | tf_op jit(solution)/shard_map/ppermute | solution.py:192

commit v3 on v2

v3 whole, which is shorter than its diff:
```python
import functools

import jax
import jax.numpy as jnp
from jax import lax
from jax.experimental import pallas as pl
from jax.experimental.pallas import tpu as pltpu
from jax.sharding import Mesh
from jax.sharding import PartitionSpec as P

XL, Z, XH, Y, C = "xl", "z", "xh", "y", "c"
CHIPS = (XH, Y)
N_CHIPS = 8
MIB = 1024 * 1024


IN_VMEM = pl.BlockSpec(memory_space=pltpu.VMEM)
IN_SMEM = pl.BlockSpec(memory_space=pltpu.SMEM)
IN_HBM = pl.BlockSpec(memory_space=pltpu.HBM)


def params(mib):
    return pltpu.CompilerParams(vmem_limit_bytes=mib * MIB)


def weight_round(flip):
    pairs = []
    for xl in range(2):
        for z in range(4):
            for b in range(2):
                pairs.append(((xl * 4 + z) * 2 + b, ((b ^ flip) * 4 + z) * 2 + xl))
    return pairs


def ring(size, step):
    return [(i, (i + step) % size) for i in range(size)]


def project_kernel(side, swap_ref, w_ref, own_ref, other_ref, held, out_ref, buffer, sem):
    del held
    swap = swap_ref[0] == 1
    w_0, w_1 = w_ref[0], w_ref[1]
    acc = jnp.dot(jnp.where(swap, w_1, w_0), own_ref[...], preferred_element_type=jnp.float32)
    acc += jnp.dot(jnp.where(swap, w_0, w_1), other_ref[...], preferred_element_type=jnp.float32)
    buffer[...] = acc.astype(jnp.bfloat16).reshape(buffer.shape)
    groups = buffer.shape[0]
    copy = pltpu.make_async_copy(buffer, out_ref.at[pl.ds(side * groups, groups)], sem)
    copy.start()
    copy.wait()


def project(swap, weight, own_image, other_image, side, held):
    kv_rows = weight.shape[1]
    depth, tokens = own_image.shape
    groups = N_CHIPS // 2
    shape = (N_CHIPS, kv_rows // groups, tokens)
    return pl.pallas_call(
        functools.partial(project_kernel, side),
        out_shape=pltpu.HBM(shape, jnp.bfloat16),
        in_specs=[IN_SMEM] + [IN_VMEM] * 3 + [IN_HBM],
        out_specs=IN_HBM,
        scratch_shapes=[pltpu.VMEM((groups,) + shape[1:], jnp.bfloat16), pltpu.SemaphoreType.DMA],
        input_output_aliases={4: 0} if held.shape == shape else {},
        compiler_params=params(20),
        cost_estimate=pl.CostEstimate(
            flops=2 * kv_rows * tokens * depth * 2, bytes_accessed=5 * MIB, transcendentals=0
        ),
        name="project",
    )(swap, weight, own_image, other_image, held)


def sum_kernel(info_ref, parts_ref, out_ref, buffer, sems):
    n = parts_ref.shape[0]
    copies = [pltpu.make_async_copy(parts_ref.at[d], buffer.at[d], sems.at[d]) for d in range(n)]
    for copy in copies:
        copy.start()
    copies[0].wait()
    total = buffer[0].astype(jnp.float32)
    for d in range(1, n):
        copies[d].wait()
        total += buffer[d].astype(jnp.float32)
    first = jnp.where(info_ref[1] == 1, total[:, :1], 0.0)
    slot = lax.broadcasted_iota(jnp.int32, total.shape, 1)
    out_ref[...] = jnp.where(slot < info_ref[0], total, first).astype(jnp.bfloat16)


def sum_parts(info, parts):
    n = parts.shape[0]
    return pl.pallas_call(
        sum_kernel,
        out_shape=jax.ShapeDtypeStruct(parts.shape[1:], jnp.bfloat16),
        in_specs=[IN_SMEM, IN_HBM],
        out_specs=IN_VMEM,
        scratch_shapes=[pltpu.VMEM(parts.shape, jnp.bfloat16), pltpu.SemaphoreType.DMA((n,))],
        compiler_params=params(16),
        cost_estimate=pl.CostEstimate(flops=1 << 20, bytes_accessed=2 * MIB, transcendentals=0),
        name="sum_parts",
    )(info, pltpu.with_memory_space_constraint(parts, pltpu.HBM))


def attend_kernel(head_dim, whole, jobs, scalars, gate_ref, *refs):
    n_jobs, n_groups = len(jobs), len(jobs[0])
    pieces, refs = refs[: 4 * n_jobs], refs[4 * n_jobs :]
    q_refs, refs = refs[: n_jobs * n_groups], refs[n_jobs * n_groups + 1 :]
    outs, (kv, queries, own_out, sems, out_sems) = refs[:-5], refs[-5:]
    rows, width = own_out.shape[1:]
    tokens = kv.shape[2]
    piece_rows = pieces[0].shape[0]
    copies, columns = [], []
    for j in range(n_jobs):
        base = 2 + n_groups + 5 * j
        columns.append(pl.ds(pl.multiple_of(scalars[base] * width, width), width))
        now = []
        for i in range(n_groups):
            ref = q_refs[j * n_groups + i]
            source = ref.at[:, columns[j]] if whole and i == 0 else ref.at[jobs[j][i]]
            now.append((source, queries.at[j, i]))
        for d in range(4):
            to = pl.ds(pl.multiple_of(scalars[base + 1 + d], piece_rows), piece_rows)
            now.append((pieces[4 * j + d], kv.at[j, to]))
        copies.append([pltpu.make_async_copy(*pair, sems.at[j, n]) for n, pair in enumerate(now)])
    for copy in sum(copies, []):
        copy.start()

    slot = lax.broadcasted_iota(jnp.int32, (head_dim, tokens), 1)
    row = lax.broadcasted_iota(jnp.int32, (head_dim, tokens), 0)
    counted = ((slot < scalars[0]) & (row == 0)).astype(jnp.float32).astype(jnp.bfloat16)
    gate = gate_ref[0]
    factor = head_dim**-0.5 * 1.4426950408889634
    heads = 4 // n_groups
    live = []
    for i in range(n_groups):
        live.append(scalars[2 + i] + lax.broadcasted_iota(jnp.int32, (rows, head_dim), 0) < scalars[1])
    live = jnp.concatenate(live * heads, axis=0)
    stores = []
    for j in range(n_jobs):
        for copy in copies[j]:
            copy.wait()
        keys = kv[j, :head_dim]
        values = jnp.concatenate([kv[j, head_dim:], counted], axis=0)
        for h in range(0, width // head_dim, heads):
            parts = [(i, slice(k * head_dim, (k + 1) * head_dim)) for k in range(h, h + heads) for i in range(n_groups)]
            q = jnp.concatenate([queries[j, i, :, cols] for i, cols in parts], axis=0)
            scores = jnp.dot(q, keys, preferred_element_type=jnp.float32)
            top = jnp.max(scores, axis=1, keepdims=True) * factor
            weights = jnp.exp2(scores * factor - top).astype(jnp.bfloat16)
            mixed = lax.dot_general(weights, values, (((1,), (1,)), ((), ())), preferred_element_type=jnp.float32)
            attention = (mixed[:, :head_dim] / mixed[:, head_dim : head_dim + 1]).astype(jnp.bfloat16)
            gated = jnp.where(live, gate * attention.astype(jnp.float32), 0.0).astype(jnp.bfloat16)
            for n, (i, cols) in enumerate(parts):
                value = gated[n * rows : (n + 1) * rows]
                if whole and i == 0:
                    own_out[j, :, cols] = value
                else:
                    outs[i][j, :, cols] = value
        if whole:
            stores.append(pltpu.make_async_copy(own_out.at[j], outs[0].at[:, columns[j]], out_sems.at[j]))
            stores[-1].start()
    for store in stores:
        store.wait()


def attend(scalars, gate, jobs, held, head_dim, whole):
    n_jobs, n = len(jobs), len(jobs[0][1])
    pieces = [x for kv, _ in jobs for x in kv]
    arrays = [x for _, queries in jobs for x, _ in queries]
    places = [[i for _, i in queries] for _, queries in jobs]
    rows, width = arrays[-1].shape[1:]
    tokens = pieces[0].shape[-1]
    shapes = [jax.ShapeDtypeStruct((n_jobs, rows, width), jnp.bfloat16)] * n
    if whole:
        shapes[0] = pltpu.HBM(arrays[0].shape, jnp.bfloat16)
    n_q = n_jobs * n * rows * width // head_dim
    return pl.pallas_call(
        functools.partial(attend_kernel, head_dim, whole, places),
        out_shape=shapes,
        in_specs=[IN_SMEM, IN_SMEM] + [IN_HBM] * (len(pieces) + len(arrays) + 1),
        out_specs=[IN_HBM if whole and i == 0 else IN_VMEM for i in range(n)],
        scratch_shapes=[
            pltpu.VMEM((n_jobs, 2 * head_dim, tokens), jnp.bfloat16),
            pltpu.VMEM((n_jobs, n, rows, width), jnp.bfloat16),
            pltpu.VMEM((n_jobs, rows, width), jnp.bfloat16),
            pltpu.SemaphoreType.DMA((n_jobs, n + 4)),
            pltpu.SemaphoreType.DMA((n_jobs,)),
        ],
        input_output_aliases={2 + len(pieces) + len(arrays): 0} if whole and held.shape == arrays[0].shape else {},
        compiler_params=params(28),
        cost_estimate=pl.CostEstimate(
            flops=4 * n_q * tokens * head_dim, bytes_accessed=4 * MIB, transcendentals=n_q * tokens
        ),
        name="attend",
    )(scalars, gate, *pieces, *arrays, held)


def place_kernel(jobs, scalars, *refs):
    out, sems = refs[-2:]
    copies = []
    for n, (i, part) in enumerate(jobs):
        width = refs[i].shape[2]
        cols = pl.ds(pl.multiple_of(scalars[n] * width, width), width)
        copies.append(pltpu.make_async_copy(refs[i].at[part], out.at[:, cols], sems.at[n]))
    for copy in copies:
        copy.start()
    for copy in copies:
        copy.wait()


def place(columns, received, held):
    n = len(received)
    jobs = [(i, part) for i, x in enumerate(received) for part in range(x.shape[0])]
    return pl.pallas_call(
        functools.partial(place_kernel, jobs),
        out_shape=jax.ShapeDtypeStruct(held.shape, held.dtype),
        in_specs=[IN_SMEM] + [IN_VMEM] * n + [IN_HBM],
        out_specs=IN_HBM,
        scratch_shapes=[pltpu.SemaphoreType.DMA((len(jobs),))],
        input_output_aliases={n + 1: 0},
        compiler_params=params(8),
        cost_estimate=pl.CostEstimate(flops=0, bytes_accessed=1 << 20, transcendentals=0),
        name="place",
    )(jnp.stack(columns).astype(jnp.int32), *received, held)


def on_device(queries, image_tokens, kv_weight, attn_gate, image_counts, response_lengths):
    rows = queries.shape[1]
    head_dim = kv_weight.shape[3]
    width = queries.shape[2] // 8
    z, xh, y, c = (lax.axis_index(a) for a in (Z, XH, Y, C))
    xl = lax.axis_index(XL)
    q = queries[0]
    image = image_tokens[0].T
    w_own = kv_weight[:, 0].transpose(1, 2, 0).reshape(2 * head_dim, -1)

    others = ((1, 0), (1, 1), (0, 1))

    def to_other(value, dx, dc):
        return lax.ppermute(value, (XH, C), [(i, i ^ (dx * 2 + dc)) for i in range(4)])

    def column_of(dx, dc, chunk):
        step = jnp.where((xh ^ dx) == 0, chunk, 3 - chunk)
        return (c ^ dc) * 4 + (z + step) % 4

    def position_of(dx, dc):
        return (((xh ^ dx) * 4 + y) * 2 + (c ^ dc)) * rows

    def query_slice(dx, dc, chunk):
        return lax.dynamic_slice_in_dim(q, column_of(dx, dc, chunk) * width, width, axis=1)[None]

    def exchange(values):
        return [to_other(value, dx, dc) for value, (dx, dc) in zip(values, others)]

    w_here = jnp.stack([lax.ppermute(w_own, (XL, Z, C), weight_round(flip)) for flip in range(2)])
    image_other = lax.ppermute(image, C, ring(2, 1))
    w_prev = lax.ppermute(w_here, Z, ring(4, 1))
    w_next = lax.ppermute(w_here, Z, ring(4, -1))
    w_far = lax.ppermute(w_here, Z, ring(4, 2))
    swap = (xl ^ c).astype(jnp.int32).reshape(1)

    count = image_counts[0]
    sum_info = jnp.stack([count, (y < 2).astype(jnp.int32)])
    gate = jnp.tanh(attn_gate)

    parts_0 = project(swap, w_here, image, image_other, 0, w_own)
    parts_0 = project(swap, w_prev, image, image_other, 1, parts_0)
    here, far, far_other, near = (0, 0), *others

    def in_hbm(x):
        return pltpu.with_memory_space_constraint(x, pltpu.HBM)

    q_far_0 = to_other(query_slice(*far, 0), *far)
    q_near = to_other(jnp.concatenate([query_slice(*near, chunk) for chunk in (0, 1)]), *near)
    parts_0, q_far_0, w_next = lax.optimization_barrier((parts_0, q_far_0, w_next))
    parts_0 = lax.all_to_all(parts_0, CHIPS, 0, 0, tiled=True)
    parts_1 = project(swap, w_next, image, image_other, 0, w_own)
    parts_1 = project(swap, w_far, image, image_other, 1, parts_1)
    parts_1, parts_0, q_near, q_send = lax.optimization_barrier((parts_1, parts_0, q_near, query_slice(*far_other, 0)))
    parts_1 = lax.all_to_all(parts_1, CHIPS, 0, 0, tiled=True)
    sum_0 = sum_parts(sum_info, parts_0)
    kv_0 = [sum_0] + [lax.ppermute(sum_0, Y, ring(4, step)) for step in (1, 3, 2)]
    q_far_other_0 = to_other(q_send, *far_other)
    sum_1 = sum_parts(sum_info, parts_1)
    kv_1 = [sum_1] + [lax.ppermute(sum_1, Y, ring(4, step)) for step in (1, 3, 2)]
    q_send, sum_1 = lax.optimization_barrier(([query_slice(*other, 1) for other in (far, far_other)], sum_1))
    q_far_1, q_far_other_1 = (to_other(x, *other) for x, other in zip(q_send, (far, far_other)))

    pieces_at = [(y - step) % 4 * (2 * head_dim // 4) for step in (0, 1, 3, 2)]

    def scalars_of(chunks, groups):
        values = [count, response_lengths[0]] + [position_of(*g) for g in groups]
        for chunk in chunks:
            values += [column_of(0, 0, chunk)] + pieces_at
        return jnp.stack(values).astype(jnp.int32)

    groups = (far, far_other)
    kv_0 = [in_hbm(x) for x in kv_0]
    q_0 = [(in_hbm(x), 0) for x in (q_far_0, q_far_other_0)]
    gives_0 = attend(scalars_of((0,), groups), gate, [(kv_0, q_0)], w_own, head_dim, False)
    q_1 = [(x, 0) for x in (q_far_1, q_far_other_1)]
    gives_1 = attend(scalars_of((1,), groups), gate, [(kv_1, q_1)], gives_0[0], head_dim, False)
    got = [to_other(value, *other) for gives in (gives_0, gives_1) for value, other in zip(gives, groups)]
    columns = [column_of(*other, chunk) for chunk in (0, 1) for other in groups]
    q_near = in_hbm(q_near)
    out = gives_1[0]
    for chunk, kv in enumerate((kv_0, kv_1)):
        job = (kv, [(q, 0), (q_near, chunk)])
        out, give = attend(scalars_of((chunk,), (here, near)), gate, [job], out, head_dim, True)
        got.append(to_other(give, *near))
        columns.append(column_of(*near, chunk))
    out = place(columns, got, out)
    return out[None]


def solution(mesh):
    fine = Mesh(mesh.devices.reshape(2, 4, 2, 4, 2), (XL, Z, XH, Y, C))
    sample, head = (XL, Z), (XH, Y, C)
    placed = (
        P(sample, head, None),
        P(sample, None, head),
        P(head, sample, None, None),
        P(),
        P(sample),
        P(sample),
    )
    return jax.shard_map(
        on_device, mesh=fine, in_specs=placed, out_specs=P(sample, head, None), check_vma=False
    )
```

time: 166 us -> 140 us (0.84)
  waiting for transfers between devices: 67.1 us -> 33.4 us
  starting transfers between devices: 43 us -> 51.2 us
  Pallas kernels: 36.7 us -> 44.8 us
  local copies, waits for them, and re-layouts: 12.5 us -> 5.26 us
  other arithmetic: 4.08 us -> 2.02 us
    ppermute x9 -> x11, waiting for transfers between devices: 15.2 us -> 1.08 us  [to_other(): lax.ppermute(value, (XH, C), [(i, i ^ dx * 2 + dc) for i in range(4)])]
    all_to_all x2 -> x0, waiting for transfers between devices: 9.04 us -> none  [the longest x1 9.04 us: on_device(): kv_0 = lax.all_to_all(sum_0, Y, 0, 0, tiled=True)]
    ppermute x3 -> x9, waiting for transfers between devices: 20.1 us -> 11.8 us  [the longest x1 9.13 us: on_device(): w_far = lax.ppermute(w_here, Z, ring(4, 2))]
    pallas_call x12 -> x11, Pallas kernels: 36.7 us -> 44.8 us  [the longest x4 27.3 us: attend(): pl.pallas_call(functools.partial(attend_kernel, head_dim, whole, places),...]
    unnamed x32 -> x14, local copies, waits for them, and re-layouts: 8.72 us -> 1.21 us
    ppermute x9 -> x11, starting transfers between devices: 14.1 us -> 21.5 us  [to_other(): lax.ppermute(value, (XH, C), [(i, i ^ dx * 2 + dc) for i in range(4)])]
    all_to_all x2 -> x0, starting transfers between devices: 7.22 us -> none  [the longest x1 3.68 us: on_device(): kv_1 = lax.all_to_all(sum_1, Y, 0, 0, tiled=True)]
    all_to_all x1, waiting for transfers between devices: 18.5 us -> 11.4 us  [on_device(): parts_1 = lax.all_to_all(parts_1, CHIPS, 0, 0, tiled=True)]
  transfers between devices with their start and end apart: 19 -> 25, of which waited for: 9 -> 7; matrix products, arithmetic and copies ran while one was open for 5% -> 4% of each run, Pallas kernels for 17% -> 31%
where the time goes in v3:
time: 140 us; the launch traced here: 139 us
  starting transfers between devices  51.2 us (37%)
  Pallas kernels  44.8 us (32%)
  waiting for transfers between devices  33.4 us (24%)
  local copies, waits for them, and re-layouts  5.26 us (4%)
  between operations  2.44 us (2%)
  other arithmetic  2.02 us (1%)
    pallas_call x4, Pallas kernels, attend(): pl.pallas_call(functools.partial(attend_kernel, head_dim, whole, places),...  27.3 us
    ppermute x11, starting transfers between devices, to_other(): lax.ppermute(value, (XH, C), [(i, i ^ dx * 2 + dc) for i in range(4)])  21.5 us
    all_to_all x1, waiting for transfers between devices, on_device(): parts_1 = lax.all_to_all(parts_1, CHIPS, 0, 0, tiled=True)  11.4 us
    pallas_call x4, Pallas kernels, project(): pl.pallas_call(functools.partial(project_kernel, side), out_shape=pltpu.H...  11.3 us
    ppermute x1, waiting for transfers between devices, on_device(): w_far = lax.ppermute(w_here, Z, ring(4, 2))  9.13 us
    all_to_all x1, starting transfers between devices, on_device(): parts_0 = lax.all_to_all(parts_0, CHIPS, 0, 0, tiled=True)  6.37 us
    all_to_all x1, waiting for transfers between devices, on_device(): parts_0 = lax.all_to_all(parts_0, CHIPS, 0, 0, tiled=True)  4.77 us
    all_to_all x1, starting transfers between devices, on_device(): parts_1 = lax.all_to_all(parts_1, CHIPS, 0, 0, tiled=True)  4.73 us
  transfers between devices with their start and end apart: 25, of which 7 were waited for; matrix products, arithmetic and copies ran while one was open for 4% of the time, Pallas kernels for 31%

profile of v3, /device:TPU:1, one launch (start us, length us, event | category | flops | bytes accessed | tf_op | source)
XLA Modules:
  0.0 139.1 jit_solution(12405943847795315883)
XLA Ops:
  0.0 1.4 %collective-permute-start.3 = (bf16[480,1664]{1,0:T(8,128)(2,1)}, bf16[480,1664]{1,0:T(8,128)(2,1)S(1)}, u32[]{:S(2)}, u32[]{:S(2)}) collective-permute-start(bf16[480,1664]{1,0:T(8,128)(2,1)} %bitcast.29), channel_id=1, source_target_pairs={{0,1},{1,0},{2,3},{3,2},{4,5},{5,4},{6,7},{7,6},{8,9},{9,8},{10,11... | collective-permute-start | bytes 4792328 | tf_op jit(solution)/shard_map/ppermute | solution.py:253
  1.4 1.1 copy.11
  2.6 3.6 %collective-permute-start = (bf16[256,480]{1,0:T(8,128)(2,1)S(1)}, bf16[256,480]{1,0:T(8,128)(2,1)S(1)}, u32[]{:S(2)}, u32[]{:S(2)}) collective-permute-start(bf16[256,480]{1,0:T(8,128)(2,1)S(1)} %bitcast.35), channel_id=1, source_target_pairs={{0,0},{1,64},{16,16},{17,80},{32,32},{33,96},{48,48},{49,112},{64,... | collective-permute-start | bytes 737288 | tf_op jit(solution)/shard_map/ppermute | solution.py:252
  6.2 1.9 %collective-permute-done.1 = bf16[256,480]{1,0:T(8,128)(2,1)S(1)} collective-permute-done((bf16[256,480]{1,0:T(8,128)(2,1)S(1)}, bf16[256,480]{1,0:T(8,128)(2,1)S(1)}, u32[]{:S(2)}, u32[]{:S(2)}) %collective-permute-start.1) | collective-permute-done | bytes 245792 | tf_op jit(solution)/shard_map/ppermute | solution.py:252
  8.1 2.6 %collective-permute-done = bf16[256,480]{1,0:T(8,128)(2,1)S(1)} collective-permute-done((bf16[256,480]{1,0:T(8,128)(2,1)S(1)}, bf16[256,480]{1,0:T(8,128)(2,1)S(1)}, u32[]{:S(2)}, u32[]{:S(2)}) %collective-permute-start) | collective-permute-done | bytes 245792 | tf_op jit(solution)/shard_map/ppermute | solution.py:252
  10.6 0.9 pad_maximum_fusion.w_ref
  11.5 1.7 %collective-permute-start.4 = (bf16[2,256,480]{2,1,0:T(8,128)(2,1)}, bf16[2,256,480]{2,1,0:T(8,128)(2,1)}, u32[]{:S(2)}, u32[]{:S(2)}) collective-permute-start(bf16[2,256,480]{2,1,0:T(8,128)(2,1)} %pad_maximum_fusion.w_ref), channel_id=1, source_target_pairs={{0,16},{16,32},{32,48},{48,0},{1,17},{17,33},{33,49},{49,1},{2,18}... | collective-permute-start | bytes 1474568 | tf_op jit(solution)/shard_map/ppermute | solution.py:254
  13.2 2.1 %collective-permute-start.6 = (bf16[2,256,480]{2,1,0:T(8,128)(2,1)}, bf16[2,256,480]{2,1,0:T(8,128)(2,1)}, u32[]{:S(2)}, u32[]{:S(2)}) collective-permute-start(bf16[2,256,480]{2,1,0:T(8,128)(2,1)} %pad_maximum_fusion.w_ref), channel_id=1, source_target_pairs={{0,48},{16,0},{32,16},{48,32},{1,49},{17,1},{33,17},{49,33},{2,50}... | collective-permute-start | bytes 1474568 | tf_op jit(solution)/shard_map/ppermute | solution.py:255
  15.4 2.5 %constant_dynamic-slice_fusion = (bf16[1,128,1024]{2,1,0:T(8,128)(2,1)}, bf16[1,128,1024]{2,1,0:T(8,128)(2,1)}, bf16[1,128,1024]{2,1,0:T(8,128)(2,1)}, bf16[1,12...) fusion(bf16[1,128,8192]{2,1,0:T(8,128)(2,1)} %param.6, s32[]{:T(128)S(6)} %select_n.119, ...), kind=kLoop, calls=%fused_computation.2 | loop fusion | bytes 3145752 | tf_op jit(solution)/shard_map/dynamic_slice | solution.py:247
  17.9 2.7 %collective-permute-start.5 = (bf16[1,128,1024]{2,1,0:T(8,128)(2,1)}, bf16[1,128,1024]{2,1,0:T(8,128)(2,1)}, u32[]{:S(2)}, u32[]{:S(2)}) collective-permute-start(bf16[1,128,1024]{2,1,0:T(8,128)(2,1)} %get-tuple-element.44), channel_id=1, source_target_pairs={{0,8},{1,9},{8,0},{9,1},{2,10},{3,11},{10,2},{11,3},{4,12},{5,13},... | collective-permute-start | bytes 786440 | tf_op jit(solution)/shard_map/ppermute | solution.py:237
  20.6 3.1 %project.4.held = bf16[8,64,1664]{2,1,0:T(8,128)(2,1)} custom-call(s32[1]{0:T(128)} %bitcast.14.swap_ref, bf16[2,256,480]{2,1,0:T(8,128)(2,1)} %pad_maximum_fusion.w_ref, bf16[480,1664]{1,0:T(8,128)(2,1)S(1)} %bitcast.30, bf16[480,1664]{1,0:T(8,128)(2,1)S(1)} %collective-permute-done.3.other_ref, bf16[256,480]{1,0:T(8,128)(2,1)S(1)} %bitcast.36), custom_call_target="tpu_custom_call" | custom-call | flops 817889280 | bytes 5242880 | tf_op jit(solution)/shard_map/project/pallas_call | solution.py:57
  23.7 2.6 %collective-permute-done.4.w_ref = bf16[2,256,480]{2,1,0:T(8,128)(2,1)} collective-permute-done((bf16[2,256,480]{2,1,0:T(8,128)(2,1)}, bf16[2,256,480]{2,1,0:T(8,128)(2,1)}, u32[]{:S(2)}, u32[]{:S(2)}) %collective-permute-start.4) | collective-permute-done | bytes 491552 | tf_op jit(solution)/shard_map/ppermute | solution.py:254
  26.3 3.1 %project.5 = bf16[8,64,1664]{2,1,0:T(8,128)(2,1)} custom-call(s32[1]{0:T(128)} %bitcast.14.swap_ref, bf16[2,256,480]{2,1,0:T(8,128)(2,1)} %collective-permute-done.4.w_ref, bf16[480,1664]{1,0:T(8,128)(2,1)S(1)} %bitcast.31, bf16[480,1664]{1,0:T(8,128)(2,1)S(1)} %collective-permute-done.3.other_ref, ...), custom_call_target="tpu_custom_call", output_to_operand_aliasing={{}: (4, {})} | custom-call | flops 817889280 | bytes 5242880 | tf_op jit(solution)/shard_map/project/pallas_call | solution.py:57
  29.4 6.4 %all-to-all-start = ((bf16[8,64,1664]{2,1,0:T(8,128)(2,1)}), bf16[8,64,1664]{2,1,0:T(8,128)(2,1)}, u32[]{:S(2)}, u32[]{:S(2)}) async-start(bf16[8,64,1664]{2,1,0:T(8,128)(2,1)} %project.5), calls=%async_computation | async-start | bytes 3407872 | tf_op jit(solution)/shard_map/all_to_all | solution.py:273
  35.8 1.9 %collective-permute-start.2 = (bf16[2,256,480]{2,1,0:T(8,128)(2,1)}, bf16[2,256,480]{2,1,0:T(8,128)(2,1)S(1)}, u32[]{:S(2)}, u32[]{:S(2)}) collective-permute-start(bf16[2,256,480]{2,1,0:T(8,128)(2,1)} %pad_maximum_fusion.w_ref), channel_id=1, source_target_pairs={{0,32},{16,48},{32,0},{48,16},{1,33},{17,49},{33,1},{49,17},{2,34}... | collective-permute-start | bytes 1474568 | tf_op jit(solution)/shard_map/ppermute | solution.py:256
  37.7 1.1 pad_maximum_fusion.1
  38.7 0.1 collective-permute-start.7
  38.8 3.1 %project.6.held = bf16[8,64,1664]{2,1,0:T(8,128)(2,1)} custom-call(s32[1]{0:T(128)} %bitcast.14.swap_ref, bf16[2,256,480]{2,1,0:T(8,128)(2,1)} %collective-permute-done.6.w_ref, bf16[480,1664]{1,0:T(8,128)(2,1)S(1)} %bitcast.32, bf16[480,1664]{1,0:T(8,128)(2,1)S(1)} %collective-permute-done.3.other_ref, bf16[256,480]{1,0:T(8,128)(2,1)S(1)} %bitcast.37), custom_call_target="tpu_custom_call" | custom-call | flops 817889280 | bytes 5242880 | tf_op jit(solution)/shard_map/project/pallas_call | solution.py:57
  42.0 9.1 %collective-permute-done.2.w_ref = bf16[2,256,480]{2,1,0:T(8,128)(2,1)S(1)} collective-permute-done((bf16[2,256,480]{2,1,0:T(8,128)(2,1)}, bf16[2,256,480]{2,1,0:T(8,128)(2,1)S(1)}, u32[]{:S(2)}, u32[]{:S(2)}) %collective-permute-start.2) | collective-permute-done | bytes 491552 | tf_op jit(solution)/shard_map/ppermute | solution.py:256
  51.1 2.0 %project.7 = bf16[8,64,1664]{2,1,0:T(8,128)(2,1)} custom-call(s32[1]{0:T(128)} %bitcast.14.swap_ref, bf16[2,256,480]{2,1,0:T(8,128)(2,1)S(1)} %collective-permute-done.2.w_ref, bf16[480,1664]{1,0:T(8,128)(2,1)S(1)} %bitcast.33, bf16[480,1664]{1,0:T(8,128)(2,1)S(1)} %collective-permute-done.3.other_ref, ...), custom_call_target="tpu_custom_call", output_to_operand_aliasing={{}: (4, {})} | custom-call | flops 817889280 | bytes 5242880 | tf_op jit(solution)/shard_map/project/pallas_call | solution.py:57
  53.1 4.8 %all-to-all-done.parts_ref = bf16[8,64,1664]{2,1,0:T(8,128)(2,1)} async-done(((bf16[8,64,1664]{2,1,0:T(8,128)(2,1)}), bf16[8,64,1664]{2,1,0:T(8,128)(2,1)}, u32[]{:S(2)}, u32[]{:S(2)}) %all-to-all-start) | async-done | bytes 1703968 | tf_op jit(solution)/shard_map/all_to_all | solution.py:273
  57.9 4.7 %all-to-all-start.1 = ((bf16[8,64,1664]{2,1,0:T(8,128)(2,1)}), bf16[8,64,1664]{2,1,0:T(8,128)(2,1)S(1)}, u32[]{:S(2)}, u32[]{:S(2)}) async-start(bf16[8,64,1664]{2,1,0:T(8,128)(2,1)} %project.7), calls=%async_computation.1 | async-start | bytes 3407872 | tf_op jit(solution)/shard_map/all_to_all | solution.py:277
  63.4 3.8 %collective-permute-start.11 = (bf16[1,128,1024]{2,1,0:T(8,128)(2,1)}, bf16[1,128,1024]{2,1,0:T(8,128)(2,1)}, u32[]{:S(2)}, u32[]{:S(2)}) collective-permute-start(bf16[1,128,1024]{2,1,0:T(8,128)(2,1)} %get-tuple-element.26), channel_id=1, source_target_pairs={{0,9},{1,8},{8,1},{9,0},{2,11},{3,10},{10,3},{11,2},{4,13},{5,12},... | collective-permute-start | bytes 786440 | tf_op jit(solution)/shard_map/ppermute | solution.py:237
  67.2 2.2 %sum_parts.2.refs_0_ = bf16[64,1664]{1,0:T(8,128)(2,1)S(1)} custom-call(s32[2]{0:T(128)S(1)} %pad_add_fusion.info_ref, bf16[8,64,1664]{2,1,0:T(8,128)(2,1)} %all-to-all-done.parts_ref), custom_call_target="tpu_custom_call" | custom-call | flops 1048576 | bytes 2097152 | tf_op jit(solution)/shard_map/sum_parts/pallas_call | solution.py:89
  69.4 2.8 %collective-permute-start.10 = (bf16[64,1664]{1,0:T(8,128)(2,1)S(1)}, bf16[64,1664]{1,0:T(8,128)(2,1)S(1)}, u32[]{:S(2)}, u32[]{:S(2)}) collective-permute-start(bf16[64,1664]{1,0:T(8,128)(2,1)S(1)} %sum_parts.2.refs_0_), channel_id=1, source_target_pairs={{0,4},{2,6},{4,0},{6,2},{1,5},{3,7},{5,1},{7,3},{8,12},{10,14},{12... | collective-permute-start | bytes 638984 | tf_op jit(solution)/shard_map/ppermute | solution.py:279
  72.2 0.9 collective-permute-start.9
  73.1 0.6 collective-permute-start.8
  73.7 11.4 %all-to-all-done.1.parts_ref = bf16[8,64,1664]{2,1,0:T(8,128)(2,1)S(1)} async-done(((bf16[8,64,1664]{2,1,0:T(8,128)(2,1)}), bf16[8,64,1664]{2,1,0:T(8,128)(2,1)S(1)}, u32[]{:S(2)}, u32[]{:S(2)}) %all-to-all-start.1) | async-done | bytes 1703968 | tf_op jit(solution)/shard_map/all_to_all | solution.py:277
  85.1 1.2 copy-done.5
  86.2 2.2 %sum_parts.3.refs_0_ = bf16[64,1664]{1,0:T(8,128)(2,1)S(1)} custom-call(s32[2]{0:T(128)S(1)} %pad_add_fusion.info_ref, bf16[8,64,1664]{2,1,0:T(8,128)(2,1)} %copy-done.5), custom_call_target="tpu_custom_call" | custom-call | flops 1048576 | bytes 2097152 | tf_op jit(solution)/shard_map/sum_parts/pallas_call | solution.py:89
  88.5 2.7 %collective-permute-start.17 = (bf16[1,128,1024]{2,1,0:T(8,128)(2,1)}, bf16[1,128,1024]{2,1,0:T(8,128)(2,1)S(1)}, u32[]{:S(2)}, u32[]{:S(2)}) collective-permute-start(bf16[1,128,1024]{2,1,0:T(8,128)(2,1)} %get-tuple-element.30), channel_id=1, source_target_pairs={{0,8},{1,9},{8,0},{9,1},{2,10},{3,11},{10,2},{11,3},{4,12},{5,13},... | collective-permute-start | bytes 786440 | tf_op jit(solution)/shard_map/ppermute | solution.py:237
  91.1 4.8 %collective-permute-start.18 = (bf16[1,128,1024]{2,1,0:T(8,128)(2,1)}, bf16[1,128,1024]{2,1,0:T(8,128)(2,1)S(1)}, u32[]{:S(2)}, u32[]{:S(2)}) collective-permute-start(bf16[1,128,1024]{2,1,0:T(8,128)(2,1)} %get-tuple-element.31), channel_id=1, source_target_pairs={{0,9},{1,8},{8,1},{9,0},{2,11},{3,10},{10,3},{11,2},{4,13},{5,12},... | collective-permute-start | bytes 786440 | tf_op jit(solution)/shard_map/ppermute | solution.py:237
  96.0 0.3 collective-permute-start.16
  96.3 3.2 %collective-permute-start.15 = (bf16[64,1664]{1,0:T(8,128)(2,1)S(1)}, bf16[64,1664]{1,0:T(8,128)(2,1)S(1)}, u32[]{:S(2)}, u32[]{:S(2)}) collective-permute-start(bf16[64,1664]{1,0:T(8,128)(2,1)S(1)} %sum_parts.3.refs_0_), channel_id=1, source_target_pairs={{0,6},{2,0},{4,2},{6,4},{1,7},{3,1},{5,3},{7,5},{8,14},{10,8},{12,... | collective-permute-start | bytes 638984 | tf_op jit(solution)/shard_map/ppermute | solution.py:282
  100.2 0.1 stack.121.scalars
  100.4 0.1 stack.125.scalars
  101.2 6.6 %attend.4 = (bf16[1,128,1024]{2,1,0:T(8,128)(2,1)S(1)}, bf16[1,128,1024]{2,1,0:T(8,128)(2,1)S(1)}) custom-call(s32[9]{0:T(128)S(1)} %stack.113.scalars, f32[1]{0:T(128)S(6)} %tanh.3.gate_ref, bf16[64,1664]{1,0:T(8,128)(2,1)} %copy-done.2, bf16[64,1664]{1,0:T(8,128)(2,1)} %collective-permute-done.8.refs_1_, bf16[64,1664]{1,0:T(8,128)(2,1)} %collective-permute-done.9.refs_2_, ...), custom_call_target="tpu_custom_call" | custom-call | flops 1744830464 | bytes 4194304 | tf_op jit(solution)/shard_map/attend/pallas_call | solution.py:174
  107.8 1.3 collective-permute-start.13
  109.1 0.2 collective-permute-start.12
  109.4 6.4 %attend.5 = (bf16[1,128,1024]{2,1,0:T(8,128)(2,1)S(1)}, bf16[1,128,1024]{2,1,0:T(8,128)(2,1)S(1)}) custom-call(s32[9]{0:T(128)S(1)} %stack.121.scalars, f32[1]{0:T(128)S(6)} %tanh.3.gate_ref, bf16[64,1664]{1,0:T(8,128)(2,1)S(1)} %sum_parts.3.refs_0_, bf16[64,1664]{1,0:T(8,128)(2,1)S(1)} %collective-permute-done.14.refs_1_, ...), custom_call_target="tpu_custom_call" | custom-call | flops 1744830464 | bytes 4194304 | tf_op jit(solution)/shard_map/attend/pallas_call | solution.py:174
  115.9 2.2 %collective-permute-start.20 = (bf16[1,128,1024]{2,1,0:T(8,128)(2,1)S(1)}, bf16[1,128,1024]{2,1,0:T(8,128)(2,1)S(1)}, u32[]{:S(2)}, u32[]{:S(2)}) collective-permute-start(bf16[1,128,1024]{2,1,0:T(8,128)(2,1)S(1)} %get-tuple-element.33), channel_id=1, source_target_pairs={{0,9},{1,8},{8,1},{9,0},{2,11},{3,10},{10,3},{11,2},{4,13},{5,12},... | collective-permute-start | bytes 786440 | tf_op jit(solution)/shard_map/ppermute | solution.py:237
  118.0 2.9 %collective-permute-start.19 = (bf16[1,128,1024]{2,1,0:T(8,128)(2,1)S(1)}, bf16[1,128,1024]{2,1,0:T(8,128)(2,1)S(1)}, u32[]{:S(2)}, u32[]{:S(2)}) collective-permute-start(bf16[1,128,1024]{2,1,0:T(8,128)(2,1)S(1)} %get-tuple-element.32.refs_6_), channel_id=1, source_target_pairs={{0,8},{1,9},{8,0},{9,1},{2,10},{3,11},{10,2},{11,3},{4,12},{5,13},... | collective-permute-start | bytes 786440 | tf_op jit(solution)/shard_map/ppermute | solution.py:237
  121.0 7.2 %attend.6 = (bf16[128,8192]{1,0:T(8,128)(2,1)}, bf16[1,128,1024]{2,1,0:T(8,128)(2,1)S(1)}) custom-call(s32[9]{0:T(128)S(1)} %stack.124.scalars, f32[1]{0:T(128)S(6)} %tanh.3.gate_ref, bf16[64,1664]{1,0:T(8,128)(2,1)} %copy-done.2, bf16[64,1664]{1,0:T(8,128)(2,1)} %collective-permute-done.8.refs_1_, bf16[64,1664]{1,0:T(8,128)(2,1)} %collective-permute-done.9.refs_2_, ...), custom_call_target="tpu_custom_call" | custom-call | flops 1744830464 | bytes 4194304 | tf_op jit(solution)/shard_map/attend/pallas_call | solution.py:174
  128.2 0.1 collective-permute-start.21
  128.3 7.1 %attend.7 = (bf16[128,8192]{1,0:T(8,128)(2,1)}, bf16[1,128,1024]{2,1,0:T(8,128)(2,1)S(1)}) custom-call(s32[9]{0:T(128)S(1)} %stack.125.scalars, f32[1]{0:T(128)S(6)} %tanh.3.gate_ref, bf16[64,1664]{1,0:T(8,128)(2,1)S(1)} %sum_parts.3.refs_0_, bf16[64,1664]{1,0:T(8,128)(2,1)S(1)} %copy-done.4, ...), custom_call_target="tpu_custom_call", output_to_operand_aliasing={{0}: (8, {})} | custom-call | flops 1744830464 | bytes 4194304 | tf_op jit(solution)/shard_map/attend/pallas_call | solution.py:174
  135.4 0.6 collective-permute-start.22
  136.1 1.1 collective-permute-done.22.refs_5_
  137.2 1.7 %place.1 = bf16[128,8192]{1,0:T(8,128)(2,1)} custom-call(s32[6]{0:T(128)S(1)} %stack.105.scalars, bf16[1,128,1024]{2,1,0:T(8,128)(2,1)S(1)} %collective-permute-done.12.refs_0_, bf16[1,128,1024]{2,1,0:T(8,128)(2,1)S(1)} %collective-permute-done.13.refs_1_, bf16[1,128,1024]{2,1,0:T(8,128)(2,1)S(1)} %collective-permute-done.19.refs_2_, ...), custom_call_target="tpu_custom_call", output_to_operand_aliasing={{}: (7, {})} | custom-call | bytes 1048576 | tf_op jit(solution)/shard_map/place/pallas_call | solution.py:211
  (37 shorter events, 0.5 us)
Async XLA Ops:
  0.0 20.6 %collective-permute-start.3 = (bf16[480,1664]{1,0:T(8,128)(2,1)}, bf16[480,1664]{1,0:T(8,128)(2,1)S(1)}, u32[]{:S(2)}, u32[]{:S(2)}) collective-permute-start(bf16[480,1664]{1,0:T(8,128)(2,1)} %bitcast.29), channel_id=1, source_target_pairs={{0,1},{1,0},{2,3},{3,2},{4,5},{5,4},{6,7},{7,6},{8,9},{9,8},{10,11... | collective-permute-start | bytes 4792328 | tf_op jit(solution)/shard_map/ppermute | solution.py:253
  2.5 5.6 %collective-permute-start.1 = (bf16[256,480]{1,0:T(8,128)(2,1)S(1)}, bf16[256,480]{1,0:T(8,128)(2,1)S(1)}, u32[]{:S(2)}, u32[]{:S(2)}) collective-permute-start(bf16[256,480]{1,0:T(8,128)(2,1)S(1)} %bitcast.34), channel_id=1, source_target_pairs={{0,64},{1,0},{16,80},{17,16},{32,96},{33,32},{48,112},{49,48},{64,... | collective-permute-start | bytes 737288 | tf_op jit(solution)/shard_map/ppermute | solution.py:252
  2.6 8.0 %collective-permute-start = (bf16[256,480]{1,0:T(8,128)(2,1)S(1)}, bf16[256,480]{1,0:T(8,128)(2,1)S(1)}, u32[]{:S(2)}, u32[]{:S(2)}) collective-permute-start(bf16[256,480]{1,0:T(8,128)(2,1)S(1)} %bitcast.35), channel_id=1, source_target_pairs={{0,0},{1,64},{16,16},{17,80},{32,32},{33,96},{48,48},{49,112},{64,... | collective-permute-start | bytes 737288 | tf_op jit(solution)/shard_map/ppermute | solution.py:252
  11.5 9.1 %copy-start = (bf16[1,1664,480]{1,2,0:T(8,128)(2,1)S(1)}, bf16[1,1664,480]{1,2,0:T(8,128)(2,1)}, u32[]{:S(2)}) copy-start(bf16[1,1664,480]{1,2,0:T(8,128)(2,1)} %param.7) | copy-start | bytes 4792324
  11.5 14.8 %collective-permute-start.4 = (bf16[2,256,480]{2,1,0:T(8,128)(2,1)}, bf16[2,256,480]{2,1,0:T(8,128)(2,1)}, u32[]{:S(2)}, u32[]{:S(2)}) collective-permute-start(bf16[2,256,480]{2,1,0:T(8,128)(2,1)} %pad_maximum_fusion.w_ref), channel_id=1, source_target_pairs={{0,16},{16,32},{32,48},{48,0},{1,17},{17,33},{33,49},{49,1},{2,18}... | collective-permute-start | bytes 1474568 | tf_op jit(solution)/shard_map/ppermute | solution.py:254
  13.2 16.2 %collective-permute-start.6 = (bf16[2,256,480]{2,1,0:T(8,128)(2,1)}, bf16[2,256,480]{2,1,0:T(8,128)(2,1)}, u32[]{:S(2)}, u32[]{:S(2)}) collective-permute-start(bf16[2,256,480]{2,1,0:T(8,128)(2,1)} %pad_maximum_fusion.w_ref), channel_id=1, source_target_pairs={{0,48},{16,0},{32,16},{48,32},{1,49},{17,1},{33,17},{49,33},{2,50}... | collective-permute-start | bytes 1474568 | tf_op jit(solution)/shard_map/ppermute | solution.py:255
  17.9 11.5 %collective-permute-start.5 = (bf16[1,128,1024]{2,1,0:T(8,128)(2,1)}, bf16[1,128,1024]{2,1,0:T(8,128)(2,1)}, u32[]{:S(2)}, u32[]{:S(2)}) collective-permute-start(bf16[1,128,1024]{2,1,0:T(8,128)(2,1)} %get-tuple-element.44), channel_id=1, source_target_pairs={{0,8},{1,9},{8,0},{9,1},{2,10},{3,11},{10,2},{11,3},{4,12},{5,13},... | collective-permute-start | bytes 786440 | tf_op jit(solution)/shard_map/ppermute | solution.py:237
  29.4 28.5 %all-to-all-start = ((bf16[8,64,1664]{2,1,0:T(8,128)(2,1)}), bf16[8,64,1664]{2,1,0:T(8,128)(2,1)}, u32[]{:S(2)}, u32[]{:S(2)}) async-start(bf16[8,64,1664]{2,1,0:T(8,128)(2,1)} %project.5), calls=%async_computation | async-start | bytes 3407872 | tf_op jit(solution)/shard_map/all_to_all | solution.py:273
  35.8 15.3 %collective-permute-start.2 = (bf16[2,256,480]{2,1,0:T(8,128)(2,1)}, bf16[2,256,480]{2,1,0:T(8,128)(2,1)S(1)}, u32[]{:S(2)}, u32[]{:S(2)}) collective-permute-start(bf16[2,256,480]{2,1,0:T(8,128)(2,1)} %pad_maximum_fusion.w_ref), channel_id=1, source_target_pairs={{0,32},{16,48},{32,0},{48,16},{1,33},{17,49},{33,1},{49,17},{2,34}... | collective-permute-start | bytes 1474568 | tf_op jit(solution)/shard_map/ppermute | solution.py:256
  38.7 14.4 %collective-permute-start.7 = (bf16[2,128,1024]{2,1,0:T(8,128)(2,1)S(1)}, bf16[2,128,1024]{2,1,0:T(8,128)(2,1)}, u32[]{:S(2)}, u32[]{:S(2)}) collective-permute-start(bf16[2,128,1024]{2,1,0:T(8,128)(2,1)S(1)} %pad_maximum_fusion.1), channel_id=1, source_target_pairs={{0,1},{1,0},{8,9},{9,8},{2,3},{3,2},{10,11},{11,10},{4,5},{5,4},{1... | collective-permute-start | bytes 1572872 | tf_op jit(solution)/shard_map/ppermute | solution.py:237
  57.9 27.2 %all-to-all-start.1 = ((bf16[8,64,1664]{2,1,0:T(8,128)(2,1)}), bf16[8,64,1664]{2,1,0:T(8,128)(2,1)S(1)}, u32[]{:S(2)}, u32[]{:S(2)}) async-start(bf16[8,64,1664]{2,1,0:T(8,128)(2,1)} %project.7), calls=%async_computation.1 | async-start | bytes 3407872 | tf_op jit(solution)/shard_map/all_to_all | solution.py:277
  63.4 36.2 %collective-permute-start.11 = (bf16[1,128,1024]{2,1,0:T(8,128)(2,1)}, bf16[1,128,1024]{2,1,0:T(8,128)(2,1)}, u32[]{:S(2)}, u32[]{:S(2)}) collective-permute-start(bf16[1,128,1024]{2,1,0:T(8,128)(2,1)} %get-tuple-element.26), channel_id=1, source_target_pairs={{0,9},{1,8},{8,1},{9,0},{2,11},{3,10},{10,3},{11,2},{4,13},{5,12},... | collective-permute-start | bytes 786440 | tf_op jit(solution)/shard_map/ppermute | solution.py:237
  69.4 31.8 %copy-start.2 = (bf16[64,1664]{1,0:T(8,128)(2,1)}, bf16[64,1664]{1,0:T(8,128)(2,1)S(1)}, u32[]{:S(2)}) copy-start(bf16[64,1664]{1,0:T(8,128)(2,1)S(1)} %sum_parts.2.refs_0_) | copy-start | bytes 638980
  69.4 21.7 %collective-permute-start.10 = (bf16[64,1664]{1,0:T(8,128)(2,1)S(1)}, bf16[64,1664]{1,0:T(8,128)(2,1)S(1)}, u32[]{:S(2)}, u32[]{:S(2)}) collective-permute-start(bf16[64,1664]{1,0:T(8,128)(2,1)S(1)} %sum_parts.2.refs_0_), channel_id=1, source_target_pairs={{0,4},{2,6},{4,0},{6,2},{1,5},{3,7},{5,1},{7,3},{8,12},{10,14},{12... | collective-permute-start | bytes 638984 | tf_op jit(solution)/shard_map/ppermute | solution.py:279
  72.2 23.8 %collective-permute-start.9 = (bf16[64,1664]{1,0:T(8,128)(2,1)S(1)}, bf16[64,1664]{1,0:T(8,128)(2,1)}, u32[]{:S(2)}, u32[]{:S(2)}) collective-permute-start(bf16[64,1664]{1,0:T(8,128)(2,1)S(1)} %sum_parts.2.refs_0_), channel_id=1, source_target_pairs={{0,6},{2,0},{4,2},{6,4},{1,7},{3,1},{5,3},{7,5},{8,14},{10,8},{12,... | collective-permute-start | bytes 638984 | tf_op jit(solution)/shard_map/ppermute | solution.py:279
  73.1 23.2 %collective-permute-start.8 = (bf16[64,1664]{1,0:T(8,128)(2,1)S(1)}, bf16[64,1664]{1,0:T(8,128)(2,1)}, u32[]{:S(2)}, u32[]{:S(2)}) collective-permute-start(bf16[64,1664]{1,0:T(8,128)(2,1)S(1)} %sum_parts.2.refs_0_), channel_id=1, source_target_pairs={{0,2},{2,4},{4,6},{6,0},{1,3},{3,5},{5,7},{7,1},{8,10},{10,12},{12... | collective-permute-start | bytes 638984 | tf_op jit(solution)/shard_map/ppermute | solution.py:279
  85.1 1.2 copy-start.5
  88.5 20.9 %collective-permute-start.17 = (bf16[1,128,1024]{2,1,0:T(8,128)(2,1)}, bf16[1,128,1024]{2,1,0:T(8,128)(2,1)S(1)}, u32[]{:S(2)}, u32[]{:S(2)}) collective-permute-start(bf16[1,128,1024]{2,1,0:T(8,128)(2,1)} %get-tuple-element.30), channel_id=1, source_target_pairs={{0,8},{1,9},{8,0},{9,1},{2,10},{3,11},{10,2},{11,3},{4,12},{5,13},... | collective-permute-start | bytes 786440 | tf_op jit(solution)/shard_map/ppermute | solution.py:237
  91.1 10.1 %copy-start.6 = (bf16[64,1664]{1,0:T(8,128)(2,1)}, bf16[64,1664]{1,0:T(8,128)(2,1)S(1)}, u32[]{:S(2)}) copy-start(bf16[64,1664]{1,0:T(8,128)(2,1)S(1)} %collective-permute-done.10.refs_3_) | copy-start | bytes 638980
  91.1 18.2 %collective-permute-start.18 = (bf16[1,128,1024]{2,1,0:T(8,128)(2,1)}, bf16[1,128,1024]{2,1,0:T(8,128)(2,1)S(1)}, u32[]{:S(2)}, u32[]{:S(2)}) collective-permute-start(bf16[1,128,1024]{2,1,0:T(8,128)(2,1)} %get-tuple-element.31), channel_id=1, source_target_pairs={{0,9},{1,8},{8,1},{9,0},{2,11},{3,10},{10,3},{11,2},{4,13},{5,12},... | collective-permute-start | bytes 786440 | tf_op jit(solution)/shard_map/ppermute | solution.py:237
  96.0 11.8 %collective-permute-start.16 = (bf16[64,1664]{1,0:T(8,128)(2,1)S(1)}, bf16[64,1664]{1,0:T(8,128)(2,1)S(1)}, u32[]{:S(2)}, u32[]{:S(2)}) collective-permute-start(bf16[64,1664]{1,0:T(8,128)(2,1)S(1)} %sum_parts.3.refs_0_), channel_id=1, source_target_pairs={{0,4},{2,6},{4,0},{6,2},{1,5},{3,7},{5,1},{7,3},{8,12},{10,14},{12... | collective-permute-start | bytes 638984 | tf_op jit(solution)/shard_map/ppermute | solution.py:282
  96.3 12.8 %collective-permute-start.15 = (bf16[64,1664]{1,0:T(8,128)(2,1)S(1)}, bf16[64,1664]{1,0:T(8,128)(2,1)S(1)}, u32[]{:S(2)}, u32[]{:S(2)}) collective-permute-start(bf16[64,1664]{1,0:T(8,128)(2,1)S(1)} %sum_parts.3.refs_0_), channel_id=1, source_target_pairs={{0,6},{2,0},{4,2},{6,4},{1,7},{3,1},{5,3},{7,5},{8,14},{10,8},{12,... | collective-permute-start | bytes 638984 | tf_op jit(solution)/shard_map/ppermute | solution.py:282
  99.5 9.9 %collective-permute-start.14 = (bf16[64,1664]{1,0:T(8,128)(2,1)S(1)}, bf16[64,1664]{1,0:T(8,128)(2,1)S(1)}, u32[]{:S(2)}, u32[]{:S(2)}) collective-permute-start(bf16[64,1664]{1,0:T(8,128)(2,1)S(1)} %sum_parts.3.refs_0_), channel_id=1, source_target_pairs={{0,2},{2,4},{4,6},{6,0},{1,3},{3,5},{5,7},{7,1},{8,10},{10,12},{12... | collective-permute-start | bytes 638984 | tf_op jit(solution)/shard_map/ppermute | solution.py:282
  107.8 27.6 %collective-permute-start.13 = (bf16[1,128,1024]{2,1,0:T(8,128)(2,1)S(1)}, bf16[1,128,1024]{2,1,0:T(8,128)(2,1)S(1)}, u32[]{:S(2)}, u32[]{:S(2)}) collective-permute-start(bf16[1,128,1024]{2,1,0:T(8,128)(2,1)S(1)} %get-tuple-element.28), channel_id=1, source_target_pairs={{0,9},{1,8},{8,1},{9,0},{2,11},{3,10},{10,3},{11,2},{4,13},{5,12},... | collective-permute-start | bytes 786440 | tf_op jit(solution)/shard_map/ppermute | solution.py:237
  109.1 11.8 %copy-start.1 = (bf16[1,128,8192]{2,1,0:T(8,128)(2,1)S(1)}, bf16[1,128,8192]{2,1,0:T(8,128)(2,1)}, u32[]{:S(2)}) copy-start(bf16[1,128,8192]{2,1,0:T(8,128)(2,1)} %param.6) | copy-start | bytes 6291460
  109.1 27.0 %collective-permute-start.12 = (bf16[1,128,1024]{2,1,0:T(8,128)(2,1)S(1)}, bf16[1,128,1024]{2,1,0:T(8,128)(2,1)S(1)}, u32[]{:S(2)}, u32[]{:S(2)}) collective-permute-start(bf16[1,128,1024]{2,1,0:T(8,128)(2,1)S(1)} %get-tuple-element.27.refs_6_), channel_id=1, source_target_pairs={{0,8},{1,9},{8,0},{9,1},{2,10},{3,11},{10,2},{11,3},{4,12},{5,13},... | collective-permute-start | bytes 786440 | tf_op jit(solution)/shard_map/ppermute | solution.py:237
  109.4 6.5 %copy-start.3 = (bf16[64,1664]{1,0:T(8,128)(2,1)}, bf16[64,1664]{1,0:T(8,128)(2,1)S(1)}, u32[]{:S(2)}) copy-start(bf16[64,1664]{1,0:T(8,128)(2,1)S(1)} %collective-permute-done.14.refs_1_) | copy-start | bytes 638980
  115.9 20.2 %collective-permute-start.20 = (bf16[1,128,1024]{2,1,0:T(8,128)(2,1)S(1)}, bf16[1,128,1024]{2,1,0:T(8,128)(2,1)S(1)}, u32[]{:S(2)}, u32[]{:S(2)}) collective-permute-start(bf16[1,128,1024]{2,1,0:T(8,128)(2,1)S(1)} %get-tuple-element.33), channel_id=1, source_target_pairs={{0,9},{1,8},{8,1},{9,0},{2,11},{3,10},{10,3},{11,2},{4,13},{5,12},... | collective-permute-start | bytes 786440 | tf_op jit(solution)/shard_map/ppermute | solution.py:237
  118.0 18.1 %collective-permute-start.19 = (bf16[1,128,1024]{2,1,0:T(8,128)(2,1)S(1)}, bf16[1,128,1024]{2,1,0:T(8,128)(2,1)S(1)}, u32[]{:S(2)}, u32[]{:S(2)}) collective-permute-start(bf16[1,128,1024]{2,1,0:T(8,128)(2,1)S(1)} %get-tuple-element.32.refs_6_), channel_id=1, source_target_pairs={{0,8},{1,9},{8,0},{9,1},{2,10},{3,11},{10,2},{11,3},{4,12},{5,13},... | collective-permute-start | bytes 786440 | tf_op jit(solution)/shard_map/ppermute | solution.py:237
  121.0 7.3 %copy-start.4 = (bf16[64,1664]{1,0:T(8,128)(2,1)S(1)}, bf16[64,1664]{1,0:T(8,128)(2,1)}, u32[]{:S(2)}) copy-start(bf16[64,1664]{1,0:T(8,128)(2,1)} %copy-done.3) | copy-start | bytes 638980
  128.2 7.9 %collective-permute-start.21 = (bf16[1,128,1024]{2,1,0:T(8,128)(2,1)S(1)}, bf16[1,128,1024]{2,1,0:T(8,128)(2,1)S(1)}, u32[]{:S(2)}, u32[]{:S(2)}) collective-permute-start(bf16[1,128,1024]{2,1,0:T(8,128)(2,1)S(1)} %get-tuple-element.35), channel_id=1, source_target_pairs={{0,1},{1,0},{8,9},{9,8},{2,3},{3,2},{10,11},{11,10},{4,5},{5,4},{1... | collective-permute-start | bytes 786440 | tf_op jit(solution)/shard_map/ppermute | solution.py:237
  135.4 1.7 %collective-permute-start.22 = (bf16[1,128,1024]{2,1,0:T(8,128)(2,1)S(1)}, bf16[1,128,1024]{2,1,0:T(8,128)(2,1)S(1)}, u32[]{:S(2)}, u32[]{:S(2)}) collective-permute-start(bf16[1,128,1024]{2,1,0:T(8,128)(2,1)S(1)} %get-tuple-element.37), channel_id=1, source_target_pairs={{0,1},{1,0},{8,9},{9,8},{2,3},{3,2},{10,11},{11,10},{4,5},{5,4},{1... | collective-permute-start | bytes 786440 | tf_op jit(solution)/shard_map/ppermute | solution.py:237

commit v4 on v3

--- a/solution.py
+++ b/solution.py
@@ -69,36 +69,28 @@
     )(swap, weight, own_image, other_image, held)
 
 
-def sum_kernel(info_ref, parts_ref, out_ref, buffer, sems):
-    n = parts_ref.shape[0]
-    copies = [pltpu.make_async_copy(parts_ref.at[d], buffer.at[d], sems.at[d]) for d in range(n)]
-    for copy in copies:
-        copy.start()
-    copies[0].wait()
-    total = buffer[0].astype(jnp.float32)
-    for d in range(1, n):
-        copies[d].wait()
-        total += buffer[d].astype(jnp.float32)
+def sum_kernel(info_ref, parts_ref, out_ref):
+    total = parts_ref[0].astype(jnp.float32)
+    for d in range(1, parts_ref.shape[0]):
+        total += parts_ref[d].astype(jnp.float32)
     first = jnp.where(info_ref[1] == 1, total[:, :1], 0.0)
     slot = lax.broadcasted_iota(jnp.int32, total.shape, 1)
     out_ref[...] = jnp.where(slot < info_ref[0], total, first).astype(jnp.bfloat16)
 
 
 def sum_parts(info, parts):
-    n = parts.shape[0]
     return pl.pallas_call(
         sum_kernel,
         out_shape=jax.ShapeDtypeStruct(parts.shape[1:], jnp.bfloat16),
-        in_specs=[IN_SMEM, IN_HBM],
+        in_specs=[IN_SMEM, IN_VMEM],
         out_specs=IN_VMEM,
-        scratch_shapes=[pltpu.VMEM(parts.shape, jnp.bfloat16), pltpu.SemaphoreType.DMA((n,))],
         compiler_params=params(16),
         cost_estimate=pl.CostEstimate(flops=1 << 20, bytes_accessed=2 * MIB, transcendentals=0),
         name="sum_parts",
-    )(info, pltpu.with_memory_space_constraint(parts, pltpu.HBM))
-
-
-def attend_kernel(head_dim, whole, jobs, scalars, gate_ref, *refs):
+    )(info, parts)
+
+
+def attend_kernel(head_dim, whole, jobs, base, scalars, gate_ref, *refs):
     n_jobs, n_groups = len(jobs), len(jobs[0])
     pieces, refs = refs[: 4 * n_jobs], refs[4 * n_jobs :]
     q_refs, refs = refs[: n_jobs * n_groups], refs[n_jobs * n_groups + 1 :]
@@ -108,15 +100,15 @@
     piece_rows = pieces[0].shape[0]
     copies, columns = [], []
     for j in range(n_jobs):
-        base = 2 + n_groups + 5 * j
-        columns.append(pl.ds(pl.multiple_of(scalars[base] * width, width), width))
+        at = base + 2 + n_groups + 5 * j
+        columns.append(pl.ds(pl.multiple_of(scalars[at] * width, width), width))
         now = []
         for i in range(n_groups):
             ref = q_refs[j * n_groups + i]
             source = ref.at[:, columns[j]] if whole and i == 0 else ref.at[jobs[j][i]]
             now.append((source, queries.at[j, i]))
         for d in range(4):
-            to = pl.ds(pl.multiple_of(scalars[base + 1 + d], piece_rows), piece_rows)
+            to = pl.ds(pl.multiple_of(scalars[at + 1 + d], piece_rows), piece_rows)
             now.append((pieces[4 * j + d], kv.at[j, to]))
         copies.append([pltpu.make_async_copy(*pair, sems.at[j, n]) for n, pair in enumerate(now)])
     for copy in sum(copies, []):
@@ -124,13 +116,13 @@
 
     slot = lax.broadcasted_iota(jnp.int32, (head_dim, tokens), 1)
     row = lax.broadcasted_iota(jnp.int32, (head_dim, tokens), 0)
-    counted = ((slot < scalars[0]) & (row == 0)).astype(jnp.float32).astype(jnp.bfloat16)
+    counted = ((slot < scalars[base]) & (row == 0)).astype(jnp.float32).astype(jnp.bfloat16)
     gate = gate_ref[0]
     factor = head_dim**-0.5 * 1.4426950408889634
     heads = 4 // n_groups
     live = []
     for i in range(n_groups):
-        live.append(scalars[2 + i] + lax.broadcasted_iota(jnp.int32, (rows, head_dim), 0) < scalars[1])
+        live.append(scalars[base + 2 + i] + lax.broadcasted_iota(jnp.int32, (rows, head_dim), 0) < scalars[base + 1])
     live = jnp.concatenate(live * heads, axis=0)
     stores = []
     for j in range(n_jobs):
@@ -152,7 +144,7 @@
                 if whole and i == 0:
                     own_out[j, :, cols] = value
                 else:
-                    outs[i][j, :, cols] = value
+                    outs[i][:, cols] = value
         if whole:
             stores.append(pltpu.make_async_copy(own_out.at[j], outs[0].at[:, columns[j]], out_sems.at[j]))
             stores[-1].start()
@@ -160,22 +152,22 @@
         store.wait()
 
 
-def attend(scalars, gate, jobs, held, head_dim, whole):
+def attend(scalars, base, gate, jobs, held, head_dim, whole):
     n_jobs, n = len(jobs), len(jobs[0][1])
     pieces = [x for kv, _ in jobs for x in kv]
     arrays = [x for _, queries in jobs for x, _ in queries]
     places = [[i for _, i in queries] for _, queries in jobs]
     rows, width = arrays[-1].shape[1:]
     tokens = pieces[0].shape[-1]
-    shapes = [jax.ShapeDtypeStruct((n_jobs, rows, width), jnp.bfloat16)] * n
+    shapes = [jax.ShapeDtypeStruct((rows, width), jnp.bfloat16)] * n
     if whole:
         shapes[0] = pltpu.HBM(arrays[0].shape, jnp.bfloat16)
     n_q = n_jobs * n * rows * width // head_dim
     return pl.pallas_call(
-        functools.partial(attend_kernel, head_dim, whole, places),
+        functools.partial(attend_kernel, head_dim, whole, places, base),
         out_shape=shapes,
         in_specs=[IN_SMEM, IN_SMEM] + [IN_HBM] * (len(pieces) + len(arrays) + 1),
-        out_specs=[IN_HBM if whole and i == 0 else IN_VMEM for i in range(n)],
+        out_specs=[IN_HBM if whole and i == 0 else IN_VMEM for i in range(len(shapes))],
         scratch_shapes=[
             pltpu.VMEM((n_jobs, 2 * head_dim, tokens), jnp.bfloat16),
             pltpu.VMEM((n_jobs, n, rows, width), jnp.bfloat16),
@@ -192,33 +184,32 @@
     )(scalars, gate, *pieces, *arrays, held)
 
 
-def place_kernel(jobs, scalars, *refs):
-    out, sems = refs[-2:]
+def place_kernel(base, scalars, *refs):
+    *received, _, out, sems = refs
     copies = []
-    for n, (i, part) in enumerate(jobs):
-        width = refs[i].shape[2]
-        cols = pl.ds(pl.multiple_of(scalars[n] * width, width), width)
-        copies.append(pltpu.make_async_copy(refs[i].at[part], out.at[:, cols], sems.at[n]))
+    for n, ref in enumerate(received):
+        width = ref.shape[1]
+        cols = pl.ds(pl.multiple_of(scalars[base + n] * width, width), width)
+        copies.append(pltpu.make_async_copy(ref, out.at[:, cols], sems.at[n]))
     for copy in copies:
         copy.start()
     for copy in copies:
         copy.wait()
 
 
-def place(columns, received, held):
+def place(scalars, base, received, held):
     n = len(received)
-    jobs = [(i, part) for i, x in enumerate(received) for part in range(x.shape[0])]
     return pl.pallas_call(
-        functools.partial(place_kernel, jobs),
+        functools.partial(place_kernel, base),
         out_shape=jax.ShapeDtypeStruct(held.shape, held.dtype),
         in_specs=[IN_SMEM] + [IN_VMEM] * n + [IN_HBM],
         out_specs=IN_HBM,
-        scratch_shapes=[pltpu.SemaphoreType.DMA((len(jobs),))],
+        scratch_shapes=[pltpu.SemaphoreType.DMA((n,))],
         input_output_aliases={n + 1: 0},
         compiler_params=params(8),
         cost_estimate=pl.CostEstimate(flops=0, bytes_accessed=1 << 20, transcendentals=0),
         name="place",
-    )(jnp.stack(columns).astype(jnp.int32), *received, held)
+    )(scalars, *received, held)
 
 
 def on_device(queries, image_tokens, kv_weight, attn_gate, image_counts, response_lengths):
@@ -267,46 +258,49 @@
     def in_hbm(x):
         return pltpu.with_memory_space_constraint(x, pltpu.HBM)
 
+    pieces_at = [(y - step) % 4 * (2 * head_dim // 4) for step in (0, 1, 3, 2)]
+    groups = (far, far_other)
+    values, base = [], {}
+    for chunk in (0, 1):
+        for name, now in (("far", groups), ("near", (here, near))):
+            base[name, chunk] = len(values)
+            values += [count, response_lengths[0]] + [position_of(*g) for g in now]
+            values += [column_of(0, 0, chunk)] + pieces_at
+    base["place"] = len(values)
+    values += [column_of(*g, chunk) for chunk in (0, 1) for g in groups]
+    values += [column_of(*near, chunk) for chunk in (0, 1)]
+    scalars = jnp.stack(values).astype(jnp.int32)
+
     q_far_0 = to_other(query_slice(*far, 0), *far)
     q_near = to_other(jnp.concatenate([query_slice(*near, chunk) for chunk in (0, 1)]), *near)
-    parts_0, q_far_0, w_next = lax.optimization_barrier((parts_0, q_far_0, w_next))
+    parts_0, q_far_0, w_next, scalars, sum_info, gate = lax.optimization_barrier(
+        (parts_0, q_far_0, w_next, scalars, sum_info, gate)
+    )
     parts_0 = lax.all_to_all(parts_0, CHIPS, 0, 0, tiled=True)
     parts_1 = project(swap, w_next, image, image_other, 0, w_own)
     parts_1 = project(swap, w_far, image, image_other, 1, parts_1)
     parts_1, parts_0, q_near, q_send = lax.optimization_barrier((parts_1, parts_0, q_near, query_slice(*far_other, 0)))
     parts_1 = lax.all_to_all(parts_1, CHIPS, 0, 0, tiled=True)
     sum_0 = sum_parts(sum_info, parts_0)
-    kv_0 = [sum_0] + [lax.ppermute(sum_0, Y, ring(4, step)) for step in (1, 3, 2)]
+    kv_0 = [in_hbm(x) for x in [sum_0] + [lax.ppermute(sum_0, Y, ring(4, step)) for step in (1, 3, 2)]]
     q_far_other_0 = to_other(q_send, *far_other)
+
     sum_1 = sum_parts(sum_info, parts_1)
     kv_1 = [sum_1] + [lax.ppermute(sum_1, Y, ring(4, step)) for step in (1, 3, 2)]
-    q_send, sum_1 = lax.optimization_barrier(([query_slice(*other, 1) for other in (far, far_other)], sum_1))
-    q_far_1, q_far_other_1 = (to_other(x, *other) for x, other in zip(q_send, (far, far_other)))
-
-    pieces_at = [(y - step) % 4 * (2 * head_dim // 4) for step in (0, 1, 3, 2)]
-
-    def scalars_of(chunks, groups):
-        values = [count, response_lengths[0]] + [position_of(*g) for g in groups]
-        for chunk in chunks:
-            values += [column_of(0, 0, chunk)] + pieces_at
-        return jnp.stack(values).astype(jnp.int32)
-
-    groups = (far, far_other)
-    kv_0 = [in_hbm(x) for x in kv_0]
+    q_send, sum_1 = lax.optimization_barrier(([query_slice(*other, 1) for other in groups], sum_1))
+    q_1 = [(to_other(x, *other), 0) for x, other in zip(q_send, groups)]
+
+    q_near = in_hbm(q_near)
     q_0 = [(in_hbm(x), 0) for x in (q_far_0, q_far_other_0)]
-    gives_0 = attend(scalars_of((0,), groups), gate, [(kv_0, q_0)], w_own, head_dim, False)
-    q_1 = [(x, 0) for x in (q_far_1, q_far_other_1)]
-    gives_1 = attend(scalars_of((1,), groups), gate, [(kv_1, q_1)], gives_0[0], head_dim, False)
+    gives_0 = attend(scalars, base["far", 0], gate, [(kv_0, q_0)], w_own, head_dim, False)
+    gives_1 = attend(scalars, base["far", 1], gate, [(kv_1, q_1)], gives_0[0], head_dim, False)
     got = [to_other(value, *other) for gives in (gives_0, gives_1) for value, other in zip(gives, groups)]
-    columns = [column_of(*other, chunk) for chunk in (0, 1) for other in groups]
-    q_near = in_hbm(q_near)
     out = gives_1[0]
     for chunk, kv in enumerate((kv_0, kv_1)):
         job = (kv, [(q, 0), (q_near, chunk)])
-        out, give = attend(scalars_of((chunk,), (here, near)), gate, [job], out, head_dim, True)
+        out, give = attend(scalars, base["near", chunk], gate, [job], out, head_dim, True)
         got.append(to_other(give, *near))
-        columns.append(column_of(*near, chunk))
-    out = place(columns, got, out)
+    out = place(scalars, base["place"], got, out)
     return out[None]
 
 

time: 140 us -> 137 us (0.979)
  Pallas kernels: 44.8 us -> 43 us
    ppermute x1, waiting for transfers between devices: 2.61 us -> 0.33 us  [on_device(): w_prev = lax.ppermute(w_here, Z, ring(4, 1))]
    pallas_call x2, Pallas kernels: 4.43 us -> 2.63 us  [sum_parts(): pl.pallas_call(sum_kernel, out_shape=jax.ShapeDtypeStruct(parts.shape[1:]...]
  transfers between devices with their start and end apart: 25 -> 25, of which waited for: 7 -> 8; matrix products, arithmetic and copies ran while one was open for 4% -> 4% of each run, Pallas kernels for 31% -> 30%
where the time goes in v4:
time: 137 us
  starting transfers between devices  51.9 us (38%)
  Pallas kernels  43 us (31%)
  waiting for transfers between devices  32.8 us (24%)
  local copies, waits for them, and re-layouts  4.56 us (3%)
  between operations  2.39 us (2%)
  other arithmetic  2.01 us (1%)
    pallas_call x4, Pallas kernels, attend(): pl.pallas_call(functools.partial(attend_kernel, head_dim, whole, places,...  27.3 us
    ppermute x11, starting transfers between devices, to_other(): lax.ppermute(value, (XH, C), [(i, i ^ dx * 2 + dc) for i in range(4)])  22.6 us
    all_to_all x1, waiting for transfers between devices, on_device(): parts_1 = lax.all_to_all(parts_1, CHIPS, 0, 0, tiled=True)  12.4 us
    pallas_call x4, Pallas kernels, project(): pl.pallas_call(functools.partial(project_kernel, side), out_shape=pltpu.H...  11.3 us
    ppermute x1, waiting for transfers between devices, on_device(): w_far = lax.ppermute(w_here, Z, ring(4, 2))  9.13 us
    all_to_all x1, starting transfers between devices, on_device(): parts_0 = lax.all_to_all(parts_0, CHIPS, 0, 0, tiled=True)  6.37 us
    all_to_all x1, starting transfers between devices, on_device(): parts_1 = lax.all_to_all(parts_1, CHIPS, 0, 0, tiled=True)  4.86 us
    all_to_all x1, waiting for transfers between devices, on_device(): parts_0 = lax.all_to_all(parts_0, CHIPS, 0, 0, tiled=True)  4.76 us
  transfers between devices with their start and end apart: 25, of which 8 were waited for; matrix products, arithmetic and copies ran while one was open for 4% of the time, Pallas kernels for 30%

profile of v4, /device:TPU:1, one launch (start us, length us, event | category | flops | bytes accessed | tf_op | source)
XLA Modules:
  0.0 136.6 jit_solution(17055521873712611328)
XLA Ops:
  0.0 1.4 %collective-permute-start.3 = (bf16[480,1664]{1,0:T(8,128)(2,1)}, bf16[480,1664]{1,0:T(8,128)(2,1)S(1)}, u32[]{:S(2)}, u32[]{:S(2)}) collective-permute-start(bf16[480,1664]{1,0:T(8,128)(2,1)} %bitcast.29), channel_id=1, source_target_pairs={{0,1},{1,0},{2,3},{3,2},{4,5},{5,4},{6,7},{7,6},{8,9},{9,8},{10,11... | collective-permute-start | bytes 4792328 | tf_op jit(solution)/shard_map/ppermute | solution.py:244
  1.4 1.1 copy.11
  2.6 3.6 %collective-permute-start = (bf16[256,480]{1,0:T(8,128)(2,1)S(1)}, bf16[256,480]{1,0:T(8,128)(2,1)S(1)}, u32[]{:S(2)}, u32[]{:S(2)}) collective-permute-start(bf16[256,480]{1,0:T(8,128)(2,1)S(1)} %bitcast.35), channel_id=1, source_target_pairs={{0,0},{1,64},{16,16},{17,80},{32,32},{33,96},{48,48},{49,112},{64,... | collective-permute-start | bytes 737288 | tf_op jit(solution)/shard_map/ppermute | solution.py:243
  6.2 1.9 %collective-permute-done.1 = bf16[256,480]{1,0:T(8,128)(2,1)S(1)} collective-permute-done((bf16[256,480]{1,0:T(8,128)(2,1)S(1)}, bf16[256,480]{1,0:T(8,128)(2,1)S(1)}, u32[]{:S(2)}, u32[]{:S(2)}) %collective-permute-start.1) | collective-permute-done | bytes 245792 | tf_op jit(solution)/shard_map/ppermute | solution.py:243
  8.1 2.6 %collective-permute-done = bf16[256,480]{1,0:T(8,128)(2,1)S(1)} collective-permute-done((bf16[256,480]{1,0:T(8,128)(2,1)S(1)}, bf16[256,480]{1,0:T(8,128)(2,1)S(1)}, u32[]{:S(2)}, u32[]{:S(2)}) %collective-permute-start) | collective-permute-done | bytes 245792 | tf_op jit(solution)/shard_map/ppermute | solution.py:243
  10.6 0.9 pad_maximum_fusion.w_ref
  11.5 1.7 %collective-permute-start.2 = (bf16[2,256,480]{2,1,0:T(8,128)(2,1)}, bf16[2,256,480]{2,1,0:T(8,128)(2,1)}, u32[]{:S(2)}, u32[]{:S(2)}) collective-permute-start(bf16[2,256,480]{2,1,0:T(8,128)(2,1)} %pad_maximum_fusion.w_ref), channel_id=1, source_target_pairs={{0,16},{16,32},{32,48},{48,0},{1,17},{17,33},{33,49},{49,1},{2,18}... | collective-permute-start | bytes 1474568 | tf_op jit(solution)/shard_map/ppermute | solution.py:245
  13.2 2.1 %collective-permute-start.5 = (bf16[2,256,480]{2,1,0:T(8,128)(2,1)}, bf16[2,256,480]{2,1,0:T(8,128)(2,1)}, u32[]{:S(2)}, u32[]{:S(2)}) collective-permute-start(bf16[2,256,480]{2,1,0:T(8,128)(2,1)} %pad_maximum_fusion.w_ref), channel_id=1, source_target_pairs={{0,48},{16,0},{32,16},{48,32},{1,49},{17,1},{33,17},{49,33},{2,50}... | collective-permute-start | bytes 1474568 | tf_op jit(solution)/shard_map/ppermute | solution.py:246
  15.3 2.6 %constant_dynamic-slice_fusion = (bf16[1,128,1024]{2,1,0:T(8,128)(2,1)}, bf16[1,128,1024]{2,1,0:T(8,128)(2,1)}, bf16[1,128,1024]{2,1,0:T(8,128)(2,1)}, bf16[1,12...) fusion(bf16[1,128,8192]{2,1,0:T(8,128)(2,1)} %param.6, s32[]{:T(128)S(6)} %select_n.119, ...), kind=kLoop, calls=%fused_computation.2 | loop fusion | bytes 3145752 | tf_op jit(solution)/shard_map/dynamic_slice | solution.py:238
  18.0 2.7 %collective-permute-start.4 = (bf16[1,128,1024]{2,1,0:T(8,128)(2,1)}, bf16[1,128,1024]{2,1,0:T(8,128)(2,1)}, u32[]{:S(2)}, u32[]{:S(2)}) collective-permute-start(bf16[1,128,1024]{2,1,0:T(8,128)(2,1)} %get-tuple-element.50), channel_id=1, source_target_pairs={{0,8},{1,9},{8,0},{9,1},{2,10},{3,11},{10,2},{11,3},{4,12},{5,13},... | collective-permute-start | bytes 786440 | tf_op jit(solution)/shard_map/ppermute | solution.py:228
  22.7 0.1 stack.106.scalars
  22.9 3.1 %project.4.held = bf16[8,64,1664]{2,1,0:T(8,128)(2,1)} custom-call(s32[1]{0:T(128)} %bitcast.swap_ref, bf16[2,256,480]{2,1,0:T(8,128)(2,1)} %pad_maximum_fusion.w_ref, bf16[480,1664]{1,0:T(8,128)(2,1)S(1)} %bitcast.30, bf16[480,1664]{1,0:T(8,128)(2,1)S(1)} %collective-permute-done.3.other_ref, bf16[256,480]{1,0:T(8,128)(2,1)S(1)} %bitcast.36), custom_call_target="tpu_custom_call" | custom-call | flops 817889280 | bytes 5242880 | tf_op jit(solution)/shard_map/project/pallas_call | solution.py:57
  26.0 0.3 collective-permute-done.2.w_ref
  26.3 3.1 %project.5 = bf16[8,64,1664]{2,1,0:T(8,128)(2,1)} custom-call(s32[1]{0:T(128)} %bitcast.swap_ref, bf16[2,256,480]{2,1,0:T(8,128)(2,1)} %collective-permute-done.2.w_ref, bf16[480,1664]{1,0:T(8,128)(2,1)S(1)} %bitcast.31, bf16[480,1664]{1,0:T(8,128)(2,1)S(1)} %collective-permute-done.3.other_ref, ...), custom_call_target="tpu_custom_call", output_to_operand_aliasing={{}: (4, {})} | custom-call | flops 817889280 | bytes 5242880 | tf_op jit(solution)/shard_map/project/pallas_call | solution.py:57
  29.4 6.4 %all-to-all-start = ((bf16[8,64,1664]{2,1,0:T(8,128)(2,1)}), bf16[8,64,1664]{2,1,0:T(8,128)(2,1)}, u32[]{:S(2)}, u32[]{:S(2)}) async-start(bf16[8,64,1664]{2,1,0:T(8,128)(2,1)} %project.5), calls=%async_computation | async-start | bytes 3407872 | tf_op jit(solution)/shard_map/all_to_all | solution.py:279
  35.8 1.9 %collective-permute-start.6 = (bf16[2,256,480]{2,1,0:T(8,128)(2,1)}, bf16[2,256,480]{2,1,0:T(8,128)(2,1)S(1)}, u32[]{:S(2)}, u32[]{:S(2)}) collective-permute-start(bf16[2,256,480]{2,1,0:T(8,128)(2,1)} %pad_maximum_fusion.w_ref), channel_id=1, source_target_pairs={{0,32},{16,48},{32,0},{48,16},{1,33},{17,49},{33,1},{49,17},{2,34}... | collective-permute-start | bytes 1474568 | tf_op jit(solution)/shard_map/ppermute | solution.py:247
  37.7 1.1 pad_maximum_fusion.1
  38.7 0.1 collective-permute-start.7
  38.8 3.1 %project.6.held = bf16[8,64,1664]{2,1,0:T(8,128)(2,1)} custom-call(s32[1]{0:T(128)} %bitcast.swap_ref, bf16[2,256,480]{2,1,0:T(8,128)(2,1)} %collective-permute-done.5.w_ref, bf16[480,1664]{1,0:T(8,128)(2,1)S(1)} %bitcast.32, bf16[480,1664]{1,0:T(8,128)(2,1)S(1)} %collective-permute-done.3.other_ref, bf16[256,480]{1,0:T(8,128)(2,1)S(1)} %bitcast.37), custom_call_target="tpu_custom_call" | custom-call | flops 817889280 | bytes 5242880 | tf_op jit(solution)/shard_map/project/pallas_call | solution.py:57
  41.9 9.1 %collective-permute-done.6.w_ref = bf16[2,256,480]{2,1,0:T(8,128)(2,1)S(1)} collective-permute-done((bf16[2,256,480]{2,1,0:T(8,128)(2,1)}, bf16[2,256,480]{2,1,0:T(8,128)(2,1)S(1)}, u32[]{:S(2)}, u32[]{:S(2)}) %collective-permute-start.6) | collective-permute-done | bytes 491552 | tf_op jit(solution)/shard_map/ppermute | solution.py:247
  51.1 2.0 %project.7 = bf16[8,64,1664]{2,1,0:T(8,128)(2,1)} custom-call(s32[1]{0:T(128)} %bitcast.swap_ref, bf16[2,256,480]{2,1,0:T(8,128)(2,1)S(1)} %collective-permute-done.6.w_ref, bf16[480,1664]{1,0:T(8,128)(2,1)S(1)} %bitcast.33, bf16[480,1664]{1,0:T(8,128)(2,1)S(1)} %collective-permute-done.3.other_ref, ...), custom_call_target="tpu_custom_call", output_to_operand_aliasing={{}: (4, {})} | custom-call | flops 817889280 | bytes 5242880 | tf_op jit(solution)/shard_map/project/pallas_call | solution.py:57
  53.1 4.8 %all-to-all-done.parts_ref = bf16[8,64,1664]{2,1,0:T(8,128)(2,1)} async-done(((bf16[8,64,1664]{2,1,0:T(8,128)(2,1)}), bf16[8,64,1664]{2,1,0:T(8,128)(2,1)}, u32[]{:S(2)}, u32[]{:S(2)}) %all-to-all-start) | async-done | bytes 1703968 | tf_op jit(solution)/shard_map/all_to_all | solution.py:279
  57.9 4.9 %all-to-all-start.1 = ((bf16[8,64,1664]{2,1,0:T(8,128)(2,1)}), bf16[8,64,1664]{2,1,0:T(8,128)(2,1)S(1)}, u32[]{:S(2)}, u32[]{:S(2)}) async-start(bf16[8,64,1664]{2,1,0:T(8,128)(2,1)} %project.7), calls=%async_computation.1 | async-start | bytes 3407872 | tf_op jit(solution)/shard_map/all_to_all | solution.py:283
  62.8 3.9 %collective-permute-start.11 = (bf16[1,128,1024]{2,1,0:T(8,128)(2,1)S(1)}, bf16[1,128,1024]{2,1,0:T(8,128)(2,1)S(1)}, u32[]{:S(2)}, u32[]{:S(2)}) collective-permute-start(bf16[1,128,1024]{2,1,0:T(8,128)(2,1)S(1)} %copy-done.4), channel_id=1, source_target_pairs={{0,9},{1,8},{8,1},{9,0},{2,11},{3,10},{10,3},{11,2},{4,13},{5,12},... | collective-permute-start | bytes 786440 | tf_op jit(solution)/shard_map/ppermute | solution.py:228
  66.6 1.8 %sum_parts.2.refs_0_ = bf16[64,1664]{1,0:T(8,128)(2,1)S(1)} custom-call(s32[2]{0:T(128)S(1)} %pad_add_fusion.info_ref, bf16[8,64,1664]{2,1,0:T(8,128)(2,1)} %all-to-all-done.parts_ref), custom_call_target="tpu_custom_call" | custom-call | flops 1048576 | bytes 2097152 | tf_op jit(solution)/shard_map/sum_parts/pallas_call | solution.py:82
  68.4 2.8 %collective-permute-start.10 = (bf16[64,1664]{1,0:T(8,128)(2,1)S(1)}, bf16[64,1664]{1,0:T(8,128)(2,1)S(1)}, u32[]{:S(2)}, u32[]{:S(2)}) collective-permute-start(bf16[64,1664]{1,0:T(8,128)(2,1)S(1)} %sum_parts.2.refs_0_), channel_id=1, source_target_pairs={{0,4},{2,6},{4,0},{6,2},{1,5},{3,7},{5,1},{7,3},{8,12},{10,14},{12... | collective-permute-start | bytes 638984 | tf_op jit(solution)/shard_map/ppermute | solution.py:285
  71.2 0.9 collective-permute-start.9
  72.1 0.6 collective-permute-start.8
  72.7 12.4 %all-to-all-done.1.parts_ref = bf16[8,64,1664]{2,1,0:T(8,128)(2,1)S(1)} async-done(((bf16[8,64,1664]{2,1,0:T(8,128)(2,1)}), bf16[8,64,1664]{2,1,0:T(8,128)(2,1)S(1)}, u32[]{:S(2)}, u32[]{:S(2)}) %all-to-all-start.1) | async-done | bytes 1703968 | tf_op jit(solution)/shard_map/all_to_all | solution.py:283
  85.1 0.9 sum_parts.3.refs_0_
  85.9 2.8 %collective-permute-start.17 = (bf16[1,128,1024]{2,1,0:T(8,128)(2,1)}, bf16[1,128,1024]{2,1,0:T(8,128)(2,1)S(1)}, u32[]{:S(2)}, u32[]{:S(2)}) collective-permute-start(bf16[1,128,1024]{2,1,0:T(8,128)(2,1)} %get-tuple-element.36), channel_id=1, source_target_pairs={{0,8},{1,9},{8,0},{9,1},{2,10},{3,11},{10,2},{11,3},{4,12},{5,13},... | collective-permute-start | bytes 786440 | tf_op jit(solution)/shard_map/ppermute | solution.py:228
  88.7 0.2 collective-permute-done.10.refs_3_
  88.9 5.2 %collective-permute-start.18 = (bf16[1,128,1024]{2,1,0:T(8,128)(2,1)S(1)}, bf16[1,128,1024]{2,1,0:T(8,128)(2,1)S(1)}, u32[]{:S(2)}, u32[]{:S(2)}) collective-permute-start(bf16[1,128,1024]{2,1,0:T(8,128)(2,1)S(1)} %copy-done.3), channel_id=1, source_target_pairs={{0,9},{1,8},{8,1},{9,0},{2,11},{3,10},{10,3},{11,2},{4,13},{5,12},... | collective-permute-start | bytes 786440 | tf_op jit(solution)/shard_map/ppermute | solution.py:228
  94.2 0.3 collective-permute-start.16
  94.5 2.7 %collective-permute-start.15 = (bf16[64,1664]{1,0:T(8,128)(2,1)S(1)}, bf16[64,1664]{1,0:T(8,128)(2,1)S(1)}, u32[]{:S(2)}, u32[]{:S(2)}) collective-permute-start(bf16[64,1664]{1,0:T(8,128)(2,1)S(1)} %sum_parts.3.refs_0_), channel_id=1, source_target_pairs={{0,6},{2,0},{4,2},{6,4},{1,7},{3,1},{5,3},{7,5},{8,14},{10,8},{12,... | collective-permute-start | bytes 638984 | tf_op jit(solution)/shard_map/ppermute | solution.py:289
  97.2 0.7 copy-done.5
  97.9 6.6 %attend.4 = (bf16[128,1024]{1,0:T(8,128)(2,1)S(1)}, bf16[128,1024]{1,0:T(8,128)(2,1)S(1)}) custom-call(s32[42]{0:T(128)S(1)} %stack.106.scalars, f32[1]{0:T(128)S(6)} %tanh.3.gate_ref, bf16[64,1664]{1,0:T(8,128)(2,1)} %copy-done.2, bf16[64,1664]{1,0:T(8,128)(2,1)} %collective-permute-done.8.refs_1_, bf16[64,1664]{1,0:T(8,128)(2,1)} %collective-permute-done.9.refs_2_, ...), custom_call_target="tpu_custom_call" | custom-call | flops 1744830464 | bytes 4194304 | tf_op jit(solution)/shard_map/attend/pallas_call | solution.py:166
  104.4 3.8 %collective-permute-start.13 = (bf16[128,1024]{1,0:T(8,128)(2,1)S(1)}, bf16[128,1024]{1,0:T(8,128)(2,1)S(1)}, u32[]{:S(2)}, u32[]{:S(2)}) collective-permute-start(bf16[128,1024]{1,0:T(8,128)(2,1)S(1)} %get-tuple-element.34), channel_id=1, source_target_pairs={{0,9},{1,8},{8,1},{9,0},{2,11},{3,10},{10,3},{11,2},{4,13},{5,12},... | collective-permute-start | bytes 786440 | tf_op jit(solution)/shard_map/ppermute | solution.py:228
  108.2 0.2 collective-permute-start.12
  108.5 6.5 %attend.5 = (bf16[128,1024]{1,0:T(8,128)(2,1)S(1)}, bf16[128,1024]{1,0:T(8,128)(2,1)S(1)}) custom-call(s32[42]{0:T(128)S(1)} %stack.106.scalars, f32[1]{0:T(128)S(6)} %tanh.3.gate_ref, bf16[64,1664]{1,0:T(8,128)(2,1)S(1)} %sum_parts.3.refs_0_, bf16[64,1664]{1,0:T(8,128)(2,1)S(1)} %collective-permute-done.14.refs_1_, ...), custom_call_target="tpu_custom_call" | custom-call | flops 1744830464 | bytes 4194304 | tf_op jit(solution)/shard_map/attend/pallas_call | solution.py:166
  114.9 2.2 %collective-permute-start.20 = (bf16[128,1024]{1,0:T(8,128)(2,1)S(1)}, bf16[128,1024]{1,0:T(8,128)(2,1)S(1)}, u32[]{:S(2)}, u32[]{:S(2)}) collective-permute-start(bf16[128,1024]{1,0:T(8,128)(2,1)S(1)} %get-tuple-element.39), channel_id=1, source_target_pairs={{0,9},{1,8},{8,1},{9,0},{2,11},{3,10},{10,3},{11,2},{4,13},{5,12},... | collective-permute-start | bytes 786440 | tf_op jit(solution)/shard_map/ppermute | solution.py:228
  117.1 1.1 collective-permute-start.19
  118.2 7.2 %attend.6 = (bf16[128,8192]{1,0:T(8,128)(2,1)}, bf16[128,1024]{1,0:T(8,128)(2,1)S(1)}) custom-call(s32[42]{0:T(128)S(1)} %stack.106.scalars, f32[1]{0:T(128)S(6)} %tanh.3.gate_ref, bf16[64,1664]{1,0:T(8,128)(2,1)} %copy-done.2, bf16[64,1664]{1,0:T(8,128)(2,1)} %collective-permute-done.8.refs_1_, bf16[64,1664]{1,0:T(8,128)(2,1)} %collective-permute-done.9.refs_2_, ...), custom_call_target="tpu_custom_call" | custom-call | flops 1744830464 | bytes 4194304 | tf_op jit(solution)/shard_map/attend/pallas_call | solution.py:166
  125.4 0.6 collective-permute-start.21
  126.0 7.1 %attend.7 = (bf16[128,8192]{1,0:T(8,128)(2,1)}, bf16[128,1024]{1,0:T(8,128)(2,1)S(1)}) custom-call(s32[42]{0:T(128)S(1)} %stack.106.scalars, f32[1]{0:T(128)S(6)} %tanh.3.gate_ref, bf16[64,1664]{1,0:T(8,128)(2,1)S(1)} %sum_parts.3.refs_0_, bf16[64,1664]{1,0:T(8,128)(2,1)S(1)} %collective-permute-done.14.refs_1_, ...), custom_call_target="tpu_custom_call", output_to_operand_aliasing={{0}: (8, {})} | custom-call | flops 1744830464 | bytes 4194304 | tf_op jit(solution)/shard_map/attend/pallas_call | solution.py:166
  133.1 0.1 collective-permute-start.22
  133.2 1.5 %collective-permute-done.22.refs_5_ = bf16[128,1024]{1,0:T(8,128)(2,1)S(1)} collective-permute-done((bf16[128,1024]{1,0:T(8,128)(2,1)S(1)}, bf16[128,1024]{1,0:T(8,128)(2,1)S(1)}, u32[]{:S(2)}, u32[]{:S(2)}) %collective-permute-start.22) | collective-permute-done | bytes 262176 | tf_op jit(solution)/shard_map/ppermute | solution.py:228
  134.7 1.7 %place.1 = bf16[128,8192]{1,0:T(8,128)(2,1)} custom-call(s32[42]{0:T(128)S(1)} %stack.106.scalars, bf16[128,1024]{1,0:T(8,128)(2,1)S(1)} %collective-permute-done.12.refs_0_, bf16[128,1024]{1,0:T(8,128)(2,1)S(1)} %collective-permute-done.13.refs_1_, bf16[128,1024]{1,0:T(8,128)(2,1)S(1)} %collective-permute-done.19.refs_2_, ...), custom_call_target="tpu_custom_call", output_to_operand_aliasing={{}: (7, {})} | custom-call | bytes 1048576 | tf_op jit(solution)/shard_map/place/pallas_call | solution.py:202
  (33 shorter events, 0.2 us)
Async XLA Ops:
  0.0 22.9 %collective-permute-start.3 = (bf16[480,1664]{1,0:T(8,128)(2,1)}, bf16[480,1664]{1,0:T(8,128)(2,1)S(1)}, u32[]{:S(2)}, u32[]{:S(2)}) collective-permute-start(bf16[480,1664]{1,0:T(8,128)(2,1)} %bitcast.29), channel_id=1, source_target_pairs={{0,1},{1,0},{2,3},{3,2},{4,5},{5,4},{6,7},{7,6},{8,9},{9,8},{10,11... | collective-permute-start | bytes 4792328 | tf_op jit(solution)/shard_map/ppermute | solution.py:244
  2.5 5.6 %collective-permute-start.1 = (bf16[256,480]{1,0:T(8,128)(2,1)S(1)}, bf16[256,480]{1,0:T(8,128)(2,1)S(1)}, u32[]{:S(2)}, u32[]{:S(2)}) collective-permute-start(bf16[256,480]{1,0:T(8,128)(2,1)S(1)} %bitcast.34), channel_id=1, source_target_pairs={{0,64},{1,0},{16,80},{17,16},{32,96},{33,32},{48,112},{49,48},{64,... | collective-permute-start | bytes 737288 | tf_op jit(solution)/shard_map/ppermute | solution.py:243
  2.6 8.0 %collective-permute-start = (bf16[256,480]{1,0:T(8,128)(2,1)S(1)}, bf16[256,480]{1,0:T(8,128)(2,1)S(1)}, u32[]{:S(2)}, u32[]{:S(2)}) collective-permute-start(bf16[256,480]{1,0:T(8,128)(2,1)S(1)} %bitcast.35), channel_id=1, source_target_pairs={{0,0},{1,64},{16,16},{17,80},{32,32},{33,96},{48,48},{49,112},{64,... | collective-permute-start | bytes 737288 | tf_op jit(solution)/shard_map/ppermute | solution.py:243
  11.5 14.8 %collective-permute-start.2 = (bf16[2,256,480]{2,1,0:T(8,128)(2,1)}, bf16[2,256,480]{2,1,0:T(8,128)(2,1)}, u32[]{:S(2)}, u32[]{:S(2)}) collective-permute-start(bf16[2,256,480]{2,1,0:T(8,128)(2,1)} %pad_maximum_fusion.w_ref), channel_id=1, source_target_pairs={{0,16},{16,32},{32,48},{48,0},{1,17},{17,33},{33,49},{49,1},{2,18}... | collective-permute-start | bytes 1474568 | tf_op jit(solution)/shard_map/ppermute | solution.py:245
  13.2 16.2 %collective-permute-start.5 = (bf16[2,256,480]{2,1,0:T(8,128)(2,1)}, bf16[2,256,480]{2,1,0:T(8,128)(2,1)}, u32[]{:S(2)}, u32[]{:S(2)}) collective-permute-start(bf16[2,256,480]{2,1,0:T(8,128)(2,1)} %pad_maximum_fusion.w_ref), channel_id=1, source_target_pairs={{0,48},{16,0},{32,16},{48,32},{1,49},{17,1},{33,17},{49,33},{2,50}... | collective-permute-start | bytes 1474568 | tf_op jit(solution)/shard_map/ppermute | solution.py:246
  15.3 7.6 %copy-start = (bf16[1,1664,480]{1,2,0:T(8,128)(2,1)S(1)}, bf16[1,1664,480]{1,2,0:T(8,128)(2,1)}, u32[]{:S(2)}) copy-start(bf16[1,1664,480]{1,2,0:T(8,128)(2,1)} %param.7) | copy-start | bytes 4792324
  18.0 11.4 %collective-permute-start.4 = (bf16[1,128,1024]{2,1,0:T(8,128)(2,1)}, bf16[1,128,1024]{2,1,0:T(8,128)(2,1)}, u32[]{:S(2)}, u32[]{:S(2)}) collective-permute-start(bf16[1,128,1024]{2,1,0:T(8,128)(2,1)} %get-tuple-element.50), channel_id=1, source_target_pairs={{0,8},{1,9},{8,0},{9,1},{2,10},{3,11},{10,2},{11,3},{4,12},{5,13},... | collective-permute-start | bytes 786440 | tf_op jit(solution)/shard_map/ppermute | solution.py:228
  29.4 28.5 %all-to-all-start = ((bf16[8,64,1664]{2,1,0:T(8,128)(2,1)}), bf16[8,64,1664]{2,1,0:T(8,128)(2,1)}, u32[]{:S(2)}, u32[]{:S(2)}) async-start(bf16[8,64,1664]{2,1,0:T(8,128)(2,1)} %project.5), calls=%async_computation | async-start | bytes 3407872 | tf_op jit(solution)/shard_map/all_to_all | solution.py:279
  35.8 15.3 %collective-permute-start.6 = (bf16[2,256,480]{2,1,0:T(8,128)(2,1)}, bf16[2,256,480]{2,1,0:T(8,128)(2,1)S(1)}, u32[]{:S(2)}, u32[]{:S(2)}) collective-permute-start(bf16[2,256,480]{2,1,0:T(8,128)(2,1)} %pad_maximum_fusion.w_ref), channel_id=1, source_target_pairs={{0,32},{16,48},{32,0},{48,16},{1,33},{17,49},{33,1},{49,17},{2,34}... | collective-permute-start | bytes 1474568 | tf_op jit(solution)/shard_map/ppermute | solution.py:247
  38.7 14.4 %collective-permute-start.7 = (bf16[2,128,1024]{2,1,0:T(8,128)(2,1)S(1)}, bf16[2,128,1024]{2,1,0:T(8,128)(2,1)}, u32[]{:S(2)}, u32[]{:S(2)}) collective-permute-start(bf16[2,128,1024]{2,1,0:T(8,128)(2,1)S(1)} %pad_maximum_fusion.1), channel_id=1, source_target_pairs={{0,1},{1,0},{8,9},{9,8},{2,3},{3,2},{10,11},{11,10},{4,5},{5,4},{1... | collective-permute-start | bytes 1572872 | tf_op jit(solution)/shard_map/ppermute | solution.py:228
  57.9 4.9 %copy-start.4 = (bf16[1,128,1024]{2,1,0:T(8,128)(2,1)S(1)}, bf16[1,128,1024]{2,1,0:T(8,128)(2,1)}, u32[]{:S(2)}) copy-start(bf16[1,128,1024]{2,1,0:T(8,128)(2,1)} %get-tuple-element.32) | copy-start | bytes 786436
  57.9 27.2 %all-to-all-start.1 = ((bf16[8,64,1664]{2,1,0:T(8,128)(2,1)}), bf16[8,64,1664]{2,1,0:T(8,128)(2,1)S(1)}, u32[]{:S(2)}, u32[]{:S(2)}) async-start(bf16[8,64,1664]{2,1,0:T(8,128)(2,1)} %project.7), calls=%async_computation.1 | async-start | bytes 3407872 | tf_op jit(solution)/shard_map/all_to_all | solution.py:283
  62.8 26.2 %copy-start.3 = (bf16[1,128,1024]{2,1,0:T(8,128)(2,1)S(1)}, bf16[1,128,1024]{2,1,0:T(8,128)(2,1)}, u32[]{:S(2)}) copy-start(bf16[1,128,1024]{2,1,0:T(8,128)(2,1)} %get-tuple-element.37) | copy-start | bytes 786436
  62.8 34.4 %collective-permute-start.11 = (bf16[1,128,1024]{2,1,0:T(8,128)(2,1)S(1)}, bf16[1,128,1024]{2,1,0:T(8,128)(2,1)S(1)}, u32[]{:S(2)}, u32[]{:S(2)}) collective-permute-start(bf16[1,128,1024]{2,1,0:T(8,128)(2,1)S(1)} %copy-done.4), channel_id=1, source_target_pairs={{0,9},{1,8},{8,1},{9,0},{2,11},{3,10},{10,3},{11,2},{4,13},{5,12},... | collective-permute-start | bytes 786440 | tf_op jit(solution)/shard_map/ppermute | solution.py:228
  68.4 29.5 %copy-start.2 = (bf16[64,1664]{1,0:T(8,128)(2,1)}, bf16[64,1664]{1,0:T(8,128)(2,1)S(1)}, u32[]{:S(2)}) copy-start(bf16[64,1664]{1,0:T(8,128)(2,1)S(1)} %sum_parts.2.refs_0_) | copy-start | bytes 638980
  68.4 20.5 %collective-permute-start.10 = (bf16[64,1664]{1,0:T(8,128)(2,1)S(1)}, bf16[64,1664]{1,0:T(8,128)(2,1)S(1)}, u32[]{:S(2)}, u32[]{:S(2)}) collective-permute-start(bf16[64,1664]{1,0:T(8,128)(2,1)S(1)} %sum_parts.2.refs_0_), channel_id=1, source_target_pairs={{0,4},{2,6},{4,0},{6,2},{1,5},{3,7},{5,1},{7,3},{8,12},{10,14},{12... | collective-permute-start | bytes 638984 | tf_op jit(solution)/shard_map/ppermute | solution.py:285
  71.2 23.0 %collective-permute-start.9 = (bf16[64,1664]{1,0:T(8,128)(2,1)S(1)}, bf16[64,1664]{1,0:T(8,128)(2,1)}, u32[]{:S(2)}, u32[]{:S(2)}) collective-permute-start(bf16[64,1664]{1,0:T(8,128)(2,1)S(1)} %sum_parts.2.refs_0_), channel_id=1, source_target_pairs={{0,6},{2,0},{4,2},{6,4},{1,7},{3,1},{5,3},{7,5},{8,14},{10,8},{12,... | collective-permute-start | bytes 638984 | tf_op jit(solution)/shard_map/ppermute | solution.py:285
  72.1 22.4 %collective-permute-start.8 = (bf16[64,1664]{1,0:T(8,128)(2,1)S(1)}, bf16[64,1664]{1,0:T(8,128)(2,1)}, u32[]{:S(2)}, u32[]{:S(2)}) collective-permute-start(bf16[64,1664]{1,0:T(8,128)(2,1)S(1)} %sum_parts.2.refs_0_), channel_id=1, source_target_pairs={{0,2},{2,4},{4,6},{6,0},{1,3},{3,5},{5,7},{7,1},{8,10},{10,12},{12... | collective-permute-start | bytes 638984 | tf_op jit(solution)/shard_map/ppermute | solution.py:285
  85.9 22.6 %collective-permute-start.17 = (bf16[1,128,1024]{2,1,0:T(8,128)(2,1)}, bf16[1,128,1024]{2,1,0:T(8,128)(2,1)S(1)}, u32[]{:S(2)}, u32[]{:S(2)}) collective-permute-start(bf16[1,128,1024]{2,1,0:T(8,128)(2,1)} %get-tuple-element.36), channel_id=1, source_target_pairs={{0,8},{1,9},{8,0},{9,1},{2,10},{3,11},{10,2},{11,3},{4,12},{5,13},... | collective-permute-start | bytes 786440 | tf_op jit(solution)/shard_map/ppermute | solution.py:228
  88.9 8.2 %copy-start.6 = (bf16[64,1664]{1,0:T(8,128)(2,1)}, bf16[64,1664]{1,0:T(8,128)(2,1)S(1)}, u32[]{:S(2)}) copy-start(bf16[64,1664]{1,0:T(8,128)(2,1)S(1)} %collective-permute-done.10.refs_3_) | copy-start | bytes 638980
  88.9 19.6 %collective-permute-start.18 = (bf16[1,128,1024]{2,1,0:T(8,128)(2,1)S(1)}, bf16[1,128,1024]{2,1,0:T(8,128)(2,1)S(1)}, u32[]{:S(2)}, u32[]{:S(2)}) collective-permute-start(bf16[1,128,1024]{2,1,0:T(8,128)(2,1)S(1)} %copy-done.3), channel_id=1, source_target_pairs={{0,9},{1,8},{8,1},{9,0},{2,11},{3,10},{10,3},{11,2},{4,13},{5,12},... | collective-permute-start | bytes 786440 | tf_op jit(solution)/shard_map/ppermute | solution.py:228
  94.2 10.3 %collective-permute-start.16 = (bf16[64,1664]{1,0:T(8,128)(2,1)S(1)}, bf16[64,1664]{1,0:T(8,128)(2,1)S(1)}, u32[]{:S(2)}, u32[]{:S(2)}) collective-permute-start(bf16[64,1664]{1,0:T(8,128)(2,1)S(1)} %sum_parts.3.refs_0_), channel_id=1, source_target_pairs={{0,4},{2,6},{4,0},{6,2},{1,5},{3,7},{5,1},{7,3},{8,12},{10,14},{12... | collective-permute-start | bytes 638984 | tf_op jit(solution)/shard_map/ppermute | solution.py:289
  94.5 13.8 %collective-permute-start.15 = (bf16[64,1664]{1,0:T(8,128)(2,1)S(1)}, bf16[64,1664]{1,0:T(8,128)(2,1)S(1)}, u32[]{:S(2)}, u32[]{:S(2)}) collective-permute-start(bf16[64,1664]{1,0:T(8,128)(2,1)S(1)} %sum_parts.3.refs_0_), channel_id=1, source_target_pairs={{0,6},{2,0},{4,2},{6,4},{1,7},{3,1},{5,3},{7,5},{8,14},{10,8},{12,... | collective-permute-start | bytes 638984 | tf_op jit(solution)/shard_map/ppermute | solution.py:289
  97.2 0.7 copy-start.5
  97.9 10.6 %collective-permute-start.14 = (bf16[64,1664]{1,0:T(8,128)(2,1)S(1)}, bf16[64,1664]{1,0:T(8,128)(2,1)S(1)}, u32[]{:S(2)}, u32[]{:S(2)}) collective-permute-start(bf16[64,1664]{1,0:T(8,128)(2,1)S(1)} %sum_parts.3.refs_0_), channel_id=1, source_target_pairs={{0,2},{2,4},{4,6},{6,0},{1,3},{3,5},{5,7},{7,1},{8,10},{10,12},{12... | collective-permute-start | bytes 638984 | tf_op jit(solution)/shard_map/ppermute | solution.py:289
  104.4 28.7 %collective-permute-start.13 = (bf16[128,1024]{1,0:T(8,128)(2,1)S(1)}, bf16[128,1024]{1,0:T(8,128)(2,1)S(1)}, u32[]{:S(2)}, u32[]{:S(2)}) collective-permute-start(bf16[128,1024]{1,0:T(8,128)(2,1)S(1)} %get-tuple-element.34), channel_id=1, source_target_pairs={{0,9},{1,8},{8,1},{9,0},{2,11},{3,10},{10,3},{11,2},{4,13},{5,12},... | collective-permute-start | bytes 786440 | tf_op jit(solution)/shard_map/ppermute | solution.py:228
  108.2 9.9 %copy-start.1 = (bf16[1,128,8192]{2,1,0:T(8,128)(2,1)S(1)}, bf16[1,128,8192]{2,1,0:T(8,128)(2,1)}, u32[]{:S(2)}) copy-start(bf16[1,128,8192]{2,1,0:T(8,128)(2,1)} %param.6) | copy-start | bytes 6291460
  108.2 25.0 %collective-permute-start.12 = (bf16[128,1024]{1,0:T(8,128)(2,1)S(1)}, bf16[128,1024]{1,0:T(8,128)(2,1)S(1)}, u32[]{:S(2)}, u32[]{:S(2)}) collective-permute-start(bf16[128,1024]{1,0:T(8,128)(2,1)S(1)} %get-tuple-element.33.refs_6_), channel_id=1, source_target_pairs={{0,8},{1,9},{8,0},{9,1},{2,10},{3,11},{10,2},{11,3},{4,12},{5,13},... | collective-permute-start | bytes 786440 | tf_op jit(solution)/shard_map/ppermute | solution.py:228
  114.9 18.3 %collective-permute-start.20 = (bf16[128,1024]{1,0:T(8,128)(2,1)S(1)}, bf16[128,1024]{1,0:T(8,128)(2,1)S(1)}, u32[]{:S(2)}, u32[]{:S(2)}) collective-permute-start(bf16[128,1024]{1,0:T(8,128)(2,1)S(1)} %get-tuple-element.39), channel_id=1, source_target_pairs={{0,9},{1,8},{8,1},{9,0},{2,11},{3,10},{10,3},{11,2},{4,13},{5,12},... | collective-permute-start | bytes 786440 | tf_op jit(solution)/shard_map/ppermute | solution.py:228
  117.1 16.1 %collective-permute-start.19 = (bf16[128,1024]{1,0:T(8,128)(2,1)S(1)}, bf16[128,1024]{1,0:T(8,128)(2,1)S(1)}, u32[]{:S(2)}, u32[]{:S(2)}) collective-permute-start(bf16[128,1024]{1,0:T(8,128)(2,1)S(1)} %get-tuple-element.38.refs_6_), channel_id=1, source_target_pairs={{0,8},{1,9},{8,0},{9,1},{2,10},{3,11},{10,2},{11,3},{4,12},{5,13},... | collective-permute-start | bytes 786440 | tf_op jit(solution)/shard_map/ppermute | solution.py:228
  125.4 7.8 %collective-permute-start.21 = (bf16[128,1024]{1,0:T(8,128)(2,1)S(1)}, bf16[128,1024]{1,0:T(8,128)(2,1)S(1)}, u32[]{:S(2)}, u32[]{:S(2)}) collective-permute-start(bf16[128,1024]{1,0:T(8,128)(2,1)S(1)} %get-tuple-element.41), channel_id=1, source_target_pairs={{0,1},{1,0},{8,9},{9,8},{2,3},{3,2},{10,11},{11,10},{4,5},{5,4},{1... | collective-permute-start | bytes 786440 | tf_op jit(solution)/shard_map/ppermute | solution.py:228
  133.1 1.6 %collective-permute-start.22 = (bf16[128,1024]{1,0:T(8,128)(2,1)S(1)}, bf16[128,1024]{1,0:T(8,128)(2,1)S(1)}, u32[]{:S(2)}, u32[]{:S(2)}) collective-permute-start(bf16[128,1024]{1,0:T(8,128)(2,1)S(1)} %get-tuple-element.43), channel_id=1, source_target_pairs={{0,1},{1,0},{8,9},{9,8},{2,3},{3,2},{10,11},{11,10},{4,5},{5,4},{1... | collective-permute-start | bytes 786440 | tf_op jit(solution)/shard_map/ppermute | solution.py:228

commit v5 on v4

--- a/solution.py
+++ b/solution.py
@@ -90,7 +90,7 @@
     )(info, parts)
 
 
-def attend_kernel(head_dim, whole, jobs, base, scalars, gate_ref, *refs):
+def attend_kernel(head_dim, whole, direct, jobs, base, scalars, gate_ref, *refs):
     n_jobs, n_groups = len(jobs), len(jobs[0])
     pieces, refs = refs[: 4 * n_jobs], refs[4 * n_jobs :]
     q_refs, refs = refs[: n_jobs * n_groups], refs[n_jobs * n_groups + 1 :]
@@ -105,21 +105,32 @@
         now = []
         for i in range(n_groups):
             ref = q_refs[j * n_groups + i]
-            source = ref.at[:, columns[j]] if whole and i == 0 else ref.at[jobs[j][i]]
-            now.append((source, queries.at[j, i]))
+            if not direct:
+                now.append((ref.at[jobs[j][i]], queries.at[j, i]))
         for d in range(4):
             to = pl.ds(pl.multiple_of(scalars[at + 1 + d], piece_rows), piece_rows)
-            now.append((pieces[4 * j + d], kv.at[j, to]))
+            if not direct:
+                now.append((pieces[4 * j + d], kv.at[j, to]))
         copies.append([pltpu.make_async_copy(*pair, sems.at[j, n]) for n, pair in enumerate(now)])
     for copy in sum(copies, []):
         copy.start()
+    if direct:
+        for j in range(n_jobs):
+            for d in range(4):
+                to = pl.ds(pl.multiple_of(scalars[base + 3 + n_groups + 5 * j + d], piece_rows), piece_rows)
+                kv[j, to] = pieces[4 * j + d][...]
+
+    def query(j, i, cols):
+        if direct:
+            return q_refs[j * n_groups + i][jobs[j][i], :, cols]
+        return queries[j, i, :, cols]
 
     slot = lax.broadcasted_iota(jnp.int32, (head_dim, tokens), 1)
     row = lax.broadcasted_iota(jnp.int32, (head_dim, tokens), 0)
     counted = ((slot < scalars[base]) & (row == 0)).astype(jnp.float32).astype(jnp.bfloat16)
     gate = gate_ref[0]
     factor = head_dim**-0.5 * 1.4426950408889634
-    heads = 4 // n_groups
+    heads = 8 // n_groups
     live = []
     for i in range(n_groups):
         live.append(scalars[base + 2 + i] + lax.broadcasted_iota(jnp.int32, (rows, head_dim), 0) < scalars[base + 1])
@@ -132,7 +143,7 @@
         values = jnp.concatenate([kv[j, head_dim:], counted], axis=0)
         for h in range(0, width // head_dim, heads):
             parts = [(i, slice(k * head_dim, (k + 1) * head_dim)) for k in range(h, h + heads) for i in range(n_groups)]
-            q = jnp.concatenate([queries[j, i, :, cols] for i, cols in parts], axis=0)
+            q = jnp.concatenate([query(j, i, cols) for i, cols in parts], axis=0)
             scores = jnp.dot(q, keys, preferred_element_type=jnp.float32)
             top = jnp.max(scores, axis=1, keepdims=True) * factor
             weights = jnp.exp2(scores * factor - top).astype(jnp.bfloat16)
@@ -152,7 +163,7 @@
         store.wait()
 
 
-def attend(scalars, base, gate, jobs, held, head_dim, whole):
+def attend(scalars, base, gate, jobs, held, head_dim, whole, direct):
     n_jobs, n = len(jobs), len(jobs[0][1])
     pieces = [x for kv, _ in jobs for x in kv]
     arrays = [x for _, queries in jobs for x, _ in queries]
@@ -161,12 +172,15 @@
     tokens = pieces[0].shape[-1]
     shapes = [jax.ShapeDtypeStruct((rows, width), jnp.bfloat16)] * n
     if whole:
-        shapes[0] = pltpu.HBM(arrays[0].shape, jnp.bfloat16)
+        shapes[0] = pltpu.HBM(whole, jnp.bfloat16)
     n_q = n_jobs * n * rows * width // head_dim
     return pl.pallas_call(
-        functools.partial(attend_kernel, head_dim, whole, places, base),
+        functools.partial(attend_kernel, head_dim, whole is not None, direct, places, base),
         out_shape=shapes,
-        in_specs=[IN_SMEM, IN_SMEM] + [IN_HBM] * (len(pieces) + len(arrays) + 1),
+        in_specs=[IN_SMEM, IN_SMEM]
+        + [IN_VMEM if direct else IN_HBM] * len(pieces)
+        + [IN_VMEM if direct else IN_HBM] * len(arrays)
+        + [IN_HBM],
         out_specs=[IN_HBM if whole and i == 0 else IN_VMEM for i in range(len(shapes))],
         scratch_shapes=[
             pltpu.VMEM((n_jobs, 2 * head_dim, tokens), jnp.bfloat16),
@@ -175,7 +189,7 @@
             pltpu.SemaphoreType.DMA((n_jobs, n + 4)),
             pltpu.SemaphoreType.DMA((n_jobs,)),
         ],
-        input_output_aliases={2 + len(pieces) + len(arrays): 0} if whole and held.shape == arrays[0].shape else {},
+        input_output_aliases={2 + len(pieces) + len(arrays): 0} if held.shape == whole else {},
         compiler_params=params(28),
         cost_estimate=pl.CostEstimate(
             flops=4 * n_q * tokens * head_dim, bytes_accessed=4 * MIB, transcendentals=n_q * tokens
@@ -272,6 +286,7 @@
     scalars = jnp.stack(values).astype(jnp.int32)
 
     q_far_0 = to_other(query_slice(*far, 0), *far)
+    q_own = jnp.concatenate([query_slice(0, 0, chunk) for chunk in (0, 1)])
     q_near = to_other(jnp.concatenate([query_slice(*near, chunk) for chunk in (0, 1)]), *near)
     parts_0, q_far_0, w_next, scalars, sum_info, gate = lax.optimization_barrier(
         (parts_0, q_far_0, w_next, scalars, sum_info, gate)
@@ -279,10 +294,11 @@
     parts_0 = lax.all_to_all(parts_0, CHIPS, 0, 0, tiled=True)
     parts_1 = project(swap, w_next, image, image_other, 0, w_own)
     parts_1 = project(swap, w_far, image, image_other, 1, parts_1)
-    parts_1, parts_0, q_near, q_send = lax.optimization_barrier((parts_1, parts_0, q_near, query_slice(*far_other, 0)))
+    parts_1, parts_0, q_near, q_own = lax.optimization_barrier((parts_1, parts_0, q_near, q_own))
     parts_1 = lax.all_to_all(parts_1, CHIPS, 0, 0, tiled=True)
     sum_0 = sum_parts(sum_info, parts_0)
     kv_0 = [in_hbm(x) for x in [sum_0] + [lax.ppermute(sum_0, Y, ring(4, step)) for step in (1, 3, 2)]]
+    q_send, _ = lax.optimization_barrier((query_slice(*far_other, 0), sum_0))
     q_far_other_0 = to_other(q_send, *far_other)
 
     sum_1 = sum_parts(sum_info, parts_1)
@@ -290,15 +306,14 @@
     q_send, sum_1 = lax.optimization_barrier(([query_slice(*other, 1) for other in groups], sum_1))
     q_1 = [(to_other(x, *other), 0) for x, other in zip(q_send, groups)]
 
-    q_near = in_hbm(q_near)
-    q_0 = [(in_hbm(x), 0) for x in (q_far_0, q_far_other_0)]
-    gives_0 = attend(scalars, base["far", 0], gate, [(kv_0, q_0)], w_own, head_dim, False)
-    gives_1 = attend(scalars, base["far", 1], gate, [(kv_1, q_1)], gives_0[0], head_dim, False)
+    q_0 = [(x, 0) for x in (q_far_0, q_far_other_0)]
+    gives_0 = attend(scalars, base["far", 0], gate, [(kv_0, q_0)], w_own, head_dim, None, True)
+    gives_1 = attend(scalars, base["far", 1], gate, [(kv_1, q_1)], gives_0[0], head_dim, None, True)
     got = [to_other(value, *other) for gives in (gives_0, gives_1) for value, other in zip(gives, groups)]
     out = gives_1[0]
     for chunk, kv in enumerate((kv_0, kv_1)):
-        job = (kv, [(q, 0), (q_near, chunk)])
-        out, give = attend(scalars, base["near", chunk], gate, [job], out, head_dim, True)
+        job = (kv, [(q_own, chunk), (q_near, chunk)])
+        out, give = attend(scalars, base["near", chunk], gate, [job], out, head_dim, q.shape, True)
         got.append(to_other(give, *near))
     out = place(scalars, base["place"], got, out)
     return out[None]

time: 137 us -> 133 us (0.971)
  Pallas kernels: 43 us -> 38.2 us
  waiting for transfers between devices: 32.8 us -> 30.3 us
  other arithmetic: 2.01 us -> 3.87 us
    pallas_call x4, Pallas kernels: 27.3 us -> 22.6 us  [attend(): pl.pallas_call(functools.partial(attend_kernel, head_dim, whole is not No...]
    concatenate x0 -> x1, other arithmetic: none -> 1.86 us  [on_device(): q_own = jnp.concatenate([query_slice(0, 0, chunk) for chunk in (0, 1)])]
    ppermute x1, waiting for transfers between devices: 9.13 us -> 7.28 us  [on_device(): w_far = lax.ppermute(w_here, Z, ring(4, 2))]
  transfers between devices with their start and end apart: 25 -> 25, of which waited for: 8 -> 9; matrix products, arithmetic and copies ran while one was open for 4% -> 6% of each run, Pallas kernels for 30% -> 28%
where the time goes in v5:
time: 133 us
  starting transfers between devices  52.6 us (40%)
  Pallas kernels  38.2 us (29%)
  waiting for transfers between devices  30.3 us (23%)
  local copies, waits for them, and re-layouts  5.01 us (4%)
  other arithmetic  3.87 us (3%)
  between operations  2.4 us (2%)
    ppermute x11, starting transfers between devices, to_other(): lax.ppermute(value, (XH, C), [(i, i ^ dx * 2 + dc) for i in range(4)])  23.6 us
    pallas_call x4, Pallas kernels, attend(): pl.pallas_call(functools.partial(attend_kernel, head_dim, whole is not No...  22.6 us
    all_to_all x1, waiting for transfers between devices, on_device(): parts_1 = lax.all_to_all(parts_1, CHIPS, 0, 0, tiled=True)  12.4 us
    pallas_call x4, Pallas kernels, project(): pl.pallas_call(functools.partial(project_kernel, side), out_shape=pltpu.H...  11.3 us
    ppermute x1, waiting for transfers between devices, on_device(): w_far = lax.ppermute(w_here, Z, ring(4, 2))  7.28 us
    all_to_all x1, starting transfers between devices, on_device(): parts_0 = lax.all_to_all(parts_0, CHIPS, 0, 0, tiled=True)  6.15 us
    all_to_all x1, starting transfers between devices, on_device(): parts_1 = lax.all_to_all(parts_1, CHIPS, 0, 0, tiled=True)  4.73 us
    ppermute x2, waiting for transfers between devices, on_device(): lax.ppermute(w_own, (XL, Z, C), weight_round(flip))  4.44 us
  transfers between devices with their start and end apart: 25, of which 9 were waited for; matrix products, arithmetic and copies ran while one was open for 6% of the time, Pallas kernels for 28%

profile of v5, /device:TPU:1, one launch (start us, length us, event | category | flops | bytes accessed | tf_op | source)
XLA Modules:
  0.0 132.5 jit_solution(4150180266179218305)
XLA Ops:
  0.0 1.4 %collective-permute-start.3 = (bf16[480,1664]{1,0:T(8,128)(2,1)}, bf16[480,1664]{1,0:T(8,128)(2,1)S(1)}, u32[]{:S(2)}, u32[]{:S(2)}) collective-permute-start(bf16[480,1664]{1,0:T(8,128)(2,1)} %bitcast.28), channel_id=1, source_target_pairs={{0,1},{1,0},{2,3},{3,2},{4,5},{5,4},{6,7},{7,6},{8,9},{9,8},{10,11... | collective-permute-start | bytes 4792328 | tf_op jit(solution)/shard_map/ppermute | solution.py:258
  1.4 1.1 copy.11
  2.6 3.6 %collective-permute-start = (bf16[256,480]{1,0:T(8,128)(2,1)S(1)}, bf16[256,480]{1,0:T(8,128)(2,1)S(1)}, u32[]{:S(2)}, u32[]{:S(2)}) collective-permute-start(bf16[256,480]{1,0:T(8,128)(2,1)S(1)} %bitcast.34), channel_id=1, source_target_pairs={{0,0},{1,64},{16,16},{17,80},{32,32},{33,96},{48,48},{49,112},{64,... | collective-permute-start | bytes 737288 | tf_op jit(solution)/shard_map/ppermute | solution.py:257
  6.2 1.9 %collective-permute-done.1 = bf16[256,480]{1,0:T(8,128)(2,1)S(1)} collective-permute-done((bf16[256,480]{1,0:T(8,128)(2,1)S(1)}, bf16[256,480]{1,0:T(8,128)(2,1)S(1)}, u32[]{:S(2)}, u32[]{:S(2)}) %collective-permute-start.1) | collective-permute-done | bytes 245792 | tf_op jit(solution)/shard_map/ppermute | solution.py:257
  8.1 2.6 %collective-permute-done = bf16[256,480]{1,0:T(8,128)(2,1)S(1)} collective-permute-done((bf16[256,480]{1,0:T(8,128)(2,1)S(1)}, bf16[256,480]{1,0:T(8,128)(2,1)S(1)}, u32[]{:S(2)}, u32[]{:S(2)}) %collective-permute-start) | collective-permute-done | bytes 245792 | tf_op jit(solution)/shard_map/ppermute | solution.py:257
  10.6 0.9 pad_maximum_fusion.w_ref
  11.5 1.7 %collective-permute-start.2 = (bf16[2,256,480]{2,1,0:T(8,128)(2,1)}, bf16[2,256,480]{2,1,0:T(8,128)(2,1)}, u32[]{:S(2)}, u32[]{:S(2)}) collective-permute-start(bf16[2,256,480]{2,1,0:T(8,128)(2,1)} %pad_maximum_fusion.w_ref), channel_id=1, source_target_pairs={{0,16},{16,32},{32,48},{48,0},{1,17},{17,33},{33,49},{49,1},{2,18}... | collective-permute-start | bytes 1474568 | tf_op jit(solution)/shard_map/ppermute | solution.py:259
  13.2 2.1 %collective-permute-start.5 = (bf16[2,256,480]{2,1,0:T(8,128)(2,1)}, bf16[2,256,480]{2,1,0:T(8,128)(2,1)}, u32[]{:S(2)}, u32[]{:S(2)}) collective-permute-start(bf16[2,256,480]{2,1,0:T(8,128)(2,1)} %pad_maximum_fusion.w_ref), channel_id=1, source_target_pairs={{0,48},{16,0},{32,16},{48,32},{1,49},{17,1},{33,17},{49,33},{2,50}... | collective-permute-start | bytes 1474568 | tf_op jit(solution)/shard_map/ppermute | solution.py:260
  15.3 3.0 %constant_dynamic-slice_fusion = (bf16[1,128,1024]{2,1,0:T(8,128)(2,1)}, bf16[1,128,1024]{2,1,0:T(8,128)(2,1)}, bf16[1,128,1024]{2,1,0:T(8,128)(2,1)}, bf16[1,12...) fusion(bf16[1,128,8192]{2,1,0:T(8,128)(2,1)} %param.6, ...), kind=kLoop, calls=%fused_computation.3 | loop fusion | bytes 4194336 | tf_op jit(solution)/shard_map/dynamic_slice | solution.py:252
  18.3 2.7 %collective-permute-start.4 = (bf16[1,128,1024]{2,1,0:T(8,128)(2,1)}, bf16[1,128,1024]{2,1,0:T(8,128)(2,1)}, u32[]{:S(2)}, u32[]{:S(2)}) collective-permute-start(bf16[1,128,1024]{2,1,0:T(8,128)(2,1)} %get-tuple-element.53), channel_id=1, source_target_pairs={{0,8},{1,9},{8,0},{9,1},{2,10},{3,11},{10,2},{11,3},{4,12},{5,13},... | collective-permute-start | bytes 786440 | tf_op jit(solution)/shard_map/ppermute | solution.py:242
  23.0 0.1 stack.106.scalars
  23.3 3.1 %project.4.held = bf16[8,64,1664]{2,1,0:T(8,128)(2,1)} custom-call(s32[1]{0:T(128)} %bitcast.swap_ref, bf16[2,256,480]{2,1,0:T(8,128)(2,1)} %pad_maximum_fusion.w_ref, bf16[480,1664]{1,0:T(8,128)(2,1)S(1)} %bitcast.29, bf16[480,1664]{1,0:T(8,128)(2,1)S(1)} %collective-permute-done.3.other_ref, bf16[256,480]{1,0:T(8,128)(2,1)S(1)} %bitcast.35), custom_call_target="tpu_custom_call" | custom-call | flops 817889280 | bytes 5242880 | tf_op jit(solution)/shard_map/project/pallas_call | solution.py:57
  26.3 0.2 collective-permute-done.2.w_ref
  26.5 3.1 %project.5 = bf16[8,64,1664]{2,1,0:T(8,128)(2,1)} custom-call(s32[1]{0:T(128)} %bitcast.swap_ref, bf16[2,256,480]{2,1,0:T(8,128)(2,1)} %collective-permute-done.2.w_ref, bf16[480,1664]{1,0:T(8,128)(2,1)S(1)} %bitcast.30, bf16[480,1664]{1,0:T(8,128)(2,1)S(1)} %collective-permute-done.3.other_ref, ...), custom_call_target="tpu_custom_call", output_to_operand_aliasing={{}: (4, {})} | custom-call | flops 817889280 | bytes 5242880 | tf_op jit(solution)/shard_map/project/pallas_call | solution.py:57
  29.6 6.2 %all-to-all-start = ((bf16[8,64,1664]{2,1,0:T(8,128)(2,1)}), bf16[8,64,1664]{2,1,0:T(8,128)(2,1)}, u32[]{:S(2)}, u32[]{:S(2)}) async-start(bf16[8,64,1664]{2,1,0:T(8,128)(2,1)} %project.5), calls=%async_computation | async-start | bytes 3407872 | tf_op jit(solution)/shard_map/all_to_all | solution.py:294
  35.8 1.9 %collective-permute-start.6 = (bf16[2,256,480]{2,1,0:T(8,128)(2,1)}, bf16[2,256,480]{2,1,0:T(8,128)(2,1)S(1)}, u32[]{:S(2)}, u32[]{:S(2)}) collective-permute-start(bf16[2,256,480]{2,1,0:T(8,128)(2,1)} %pad_maximum_fusion.w_ref), channel_id=1, source_target_pairs={{0,32},{16,48},{32,0},{48,16},{1,33},{17,49},{33,1},{49,17},{2,34}... | collective-permute-start | bytes 1474568 | tf_op jit(solution)/shard_map/ppermute | solution.py:261
  37.7 1.1 pad_maximum_fusion.1
  38.8 1.9 %pad_maximum_fusion.2.refs_4_ = bf16[2,128,1024]{2,1,0:T(8,128)(2,1)} fusion(bf16[1,128,1024]{2,1,0:T(8,128)(2,1)} %get-tuple-element.49, bf16[1,128,1024]{2,1,0:T(8,128)(2,1)} %get-tuple-element.50), kind=kLoop, calls=%fused_computation.2 | loop fusion | flops 262144 | bytes 1048576 | tf_op jit(solution)/shard_map/concatenate | solution.py:289
  40.7 3.1 %project.6.held = bf16[8,64,1664]{2,1,0:T(8,128)(2,1)} custom-call(s32[1]{0:T(128)} %bitcast.swap_ref, bf16[2,256,480]{2,1,0:T(8,128)(2,1)} %collective-permute-done.5.w_ref, bf16[480,1664]{1,0:T(8,128)(2,1)S(1)} %bitcast.31, bf16[480,1664]{1,0:T(8,128)(2,1)S(1)} %collective-permute-done.3.other_ref, bf16[256,480]{1,0:T(8,128)(2,1)S(1)} %bitcast.36), custom_call_target="tpu_custom_call" | custom-call | flops 817889280 | bytes 5242880 | tf_op jit(solution)/shard_map/project/pallas_call | solution.py:57
  43.8 7.3 %collective-permute-done.6.w_ref = bf16[2,256,480]{2,1,0:T(8,128)(2,1)S(1)} collective-permute-done((bf16[2,256,480]{2,1,0:T(8,128)(2,1)}, bf16[2,256,480]{2,1,0:T(8,128)(2,1)S(1)}, u32[]{:S(2)}, u32[]{:S(2)}) %collective-permute-start.6) | collective-permute-done | bytes 491552 | tf_op jit(solution)/shard_map/ppermute | solution.py:261
  51.1 2.0 %project.7 = bf16[8,64,1664]{2,1,0:T(8,128)(2,1)} custom-call(s32[1]{0:T(128)} %bitcast.swap_ref, bf16[2,256,480]{2,1,0:T(8,128)(2,1)S(1)} %collective-permute-done.6.w_ref, bf16[480,1664]{1,0:T(8,128)(2,1)S(1)} %bitcast.32, bf16[480,1664]{1,0:T(8,128)(2,1)S(1)} %collective-permute-done.3.other_ref, ...), custom_call_target="tpu_custom_call", output_to_operand_aliasing={{}: (4, {})} | custom-call | flops 817889280 | bytes 5242880 | tf_op jit(solution)/shard_map/project/pallas_call | solution.py:57
  53.1 0.8 copy-done.3
  53.9 4.0 %all-to-all-done.parts_ref = bf16[8,64,1664]{2,1,0:T(8,128)(2,1)} async-done(((bf16[8,64,1664]{2,1,0:T(8,128)(2,1)}), bf16[8,64,1664]{2,1,0:T(8,128)(2,1)}, u32[]{:S(2)}, u32[]{:S(2)}) %all-to-all-start) | async-done | bytes 1703968 | tf_op jit(solution)/shard_map/all_to_all | solution.py:294
  57.9 4.7 %all-to-all-start.1 = ((bf16[8,64,1664]{2,1,0:T(8,128)(2,1)}), bf16[8,64,1664]{2,1,0:T(8,128)(2,1)S(1)}, u32[]{:S(2)}, u32[]{:S(2)}) async-start(bf16[8,64,1664]{2,1,0:T(8,128)(2,1)} %project.7), calls=%async_computation.1 | async-start | bytes 3407872 | tf_op jit(solution)/shard_map/all_to_all | solution.py:298
  62.6 1.8 %sum_parts.2.refs_0_ = bf16[64,1664]{1,0:T(8,128)(2,1)S(1)} custom-call(s32[2]{0:T(128)S(1)} %pad_add_fusion.info_ref, bf16[8,64,1664]{2,1,0:T(8,128)(2,1)} %all-to-all-done.parts_ref), custom_call_target="tpu_custom_call" | custom-call | flops 1048576 | bytes 2097152 | tf_op jit(solution)/shard_map/sum_parts/pallas_call | solution.py:82
  64.5 3.9 %collective-permute-start.11 = (bf16[1,128,1024]{2,1,0:T(8,128)(2,1)S(1)}, bf16[1,128,1024]{2,1,0:T(8,128)(2,1)S(1)}, u32[]{:S(2)}, u32[]{:S(2)}) collective-permute-start(bf16[1,128,1024]{2,1,0:T(8,128)(2,1)S(1)} %copy-done.5), channel_id=1, source_target_pairs={{0,9},{1,8},{8,1},{9,0},{2,11},{3,10},{10,3},{11,2},{4,13},{5,12},... | collective-permute-start | bytes 786440 | tf_op jit(solution)/shard_map/ppermute | solution.py:242
  68.3 2.7 %collective-permute-start.10 = (bf16[64,1664]{1,0:T(8,128)(2,1)S(1)}, bf16[64,1664]{1,0:T(8,128)(2,1)S(1)}, u32[]{:S(2)}, u32[]{:S(2)}) collective-permute-start(bf16[64,1664]{1,0:T(8,128)(2,1)S(1)} %sum_parts.2.refs_0_), channel_id=1, source_target_pairs={{0,4},{2,6},{4,0},{6,2},{1,5},{3,7},{5,1},{7,3},{8,12},{10,14},{12... | collective-permute-start | bytes 638984 | tf_op jit(solution)/shard_map/ppermute | solution.py:300
  71.0 0.9 collective-permute-start.9
  71.9 0.6 collective-permute-start.8
  72.5 12.4 %all-to-all-done.1.parts_ref = bf16[8,64,1664]{2,1,0:T(8,128)(2,1)S(1)} async-done(((bf16[8,64,1664]{2,1,0:T(8,128)(2,1)}), bf16[8,64,1664]{2,1,0:T(8,128)(2,1)S(1)}, u32[]{:S(2)}, u32[]{:S(2)}) %all-to-all-start.1) | async-done | bytes 1703968 | tf_op jit(solution)/shard_map/all_to_all | solution.py:298
  84.9 0.9 sum_parts.3.refs_0_
  85.8 2.8 %collective-permute-start.17 = (bf16[1,128,1024]{2,1,0:T(8,128)(2,1)}, bf16[1,128,1024]{2,1,0:T(8,128)(2,1)S(1)}, u32[]{:S(2)}, u32[]{:S(2)}) collective-permute-start(bf16[1,128,1024]{2,1,0:T(8,128)(2,1)} %get-tuple-element.37), channel_id=1, source_target_pairs={{0,8},{1,9},{8,0},{9,1},{2,10},{3,11},{10,2},{11,3},{4,12},{5,13},... | collective-permute-start | bytes 786440 | tf_op jit(solution)/shard_map/ppermute | solution.py:242
  88.6 0.2 collective-permute-done.10.refs_3_
  88.8 5.2 %collective-permute-start.18 = (bf16[1,128,1024]{2,1,0:T(8,128)(2,1)}, bf16[1,128,1024]{2,1,0:T(8,128)(2,1)S(1)}, u32[]{:S(2)}, u32[]{:S(2)}) collective-permute-start(bf16[1,128,1024]{2,1,0:T(8,128)(2,1)} %get-tuple-element.38), channel_id=1, source_target_pairs={{0,9},{1,8},{8,1},{9,0},{2,11},{3,10},{10,3},{11,2},{4,13},{5,12},... | collective-permute-start | bytes 786440 | tf_op jit(solution)/shard_map/ppermute | solution.py:242
  94.0 0.3 collective-permute-start.16
  94.3 2.6 %collective-permute-start.15 = (bf16[64,1664]{1,0:T(8,128)(2,1)S(1)}, bf16[64,1664]{1,0:T(8,128)(2,1)S(1)}, u32[]{:S(2)}, u32[]{:S(2)}) collective-permute-start(bf16[64,1664]{1,0:T(8,128)(2,1)S(1)} %sum_parts.3.refs_0_), channel_id=1, source_target_pairs={{0,6},{2,0},{4,2},{6,4},{1,7},{3,1},{5,3},{7,5},{8,14},{10,8},{12,... | collective-permute-start | bytes 638984 | tf_op jit(solution)/shard_map/ppermute | solution.py:305
  96.9 0.3 collective-permute-start.14
  97.2 5.7 %attend.4 = (bf16[128,1024]{1,0:T(8,128)(2,1)S(1)}, bf16[128,1024]{1,0:T(8,128)(2,1)S(1)}) custom-call(s32[42]{0:T(128)S(1)} %stack.106.scalars, f32[1]{0:T(128)S(6)} %tanh.3.gate_ref, bf16[64,1664]{1,0:T(8,128)(2,1)} %copy-done.2, bf16[64,1664]{1,0:T(8,128)(2,1)} %collective-permute-done.8.refs_1_, bf16[64,1664]{1,0:T(8,128)(2,1)} %copy-done.7, ...), custom_call_target="tpu_custom_call" | custom-call | flops 1744830464 | bytes 4194304 | tf_op jit(solution)/shard_map/attend/pallas_call | solution.py:177
  103.0 3.7 %collective-permute-start.13 = (bf16[128,1024]{1,0:T(8,128)(2,1)S(1)}, bf16[128,1024]{1,0:T(8,128)(2,1)S(1)}, u32[]{:S(2)}, u32[]{:S(2)}) collective-permute-start(bf16[128,1024]{1,0:T(8,128)(2,1)S(1)} %get-tuple-element.35), channel_id=1, source_target_pairs={{0,9},{1,8},{8,1},{9,0},{2,11},{3,10},{10,3},{11,2},{4,13},{5,12},... | collective-permute-start | bytes 786440 | tf_op jit(solution)/shard_map/ppermute | solution.py:242
  106.7 0.2 collective-permute-start.12
  107.0 4.9 %attend.5 = (bf16[128,1024]{1,0:T(8,128)(2,1)S(1)}, bf16[128,1024]{1,0:T(8,128)(2,1)S(1)}) custom-call(s32[42]{0:T(128)S(1)} %stack.106.scalars, f32[1]{0:T(128)S(6)} %tanh.3.gate_ref, bf16[64,1664]{1,0:T(8,128)(2,1)S(1)} %sum_parts.3.refs_0_, bf16[64,1664]{1,0:T(8,128)(2,1)S(1)} %collective-permute-done.14.refs_1_, ...), custom_call_target="tpu_custom_call" | custom-call | flops 1744830464 | bytes 4194304 | tf_op jit(solution)/shard_map/attend/pallas_call | solution.py:177
  112.0 2.3 %collective-permute-start.20 = (bf16[128,1024]{1,0:T(8,128)(2,1)S(1)}, bf16[128,1024]{1,0:T(8,128)(2,1)S(1)}, u32[]{:S(2)}, u32[]{:S(2)}) collective-permute-start(bf16[128,1024]{1,0:T(8,128)(2,1)S(1)} %get-tuple-element.40), channel_id=1, source_target_pairs={{0,9},{1,8},{8,1},{9,0},{2,11},{3,10},{10,3},{11,2},{4,13},{5,12},... | collective-permute-start | bytes 786440 | tf_op jit(solution)/shard_map/ppermute | solution.py:242
  114.3 1.9 %collective-permute-start.19 = (bf16[128,1024]{1,0:T(8,128)(2,1)S(1)}, bf16[128,1024]{1,0:T(8,128)(2,1)S(1)}, u32[]{:S(2)}, u32[]{:S(2)}) collective-permute-start(bf16[128,1024]{1,0:T(8,128)(2,1)S(1)} %get-tuple-element.39.refs_6_), channel_id=1, source_target_pairs={{0,8},{1,9},{8,0},{9,1},{2,10},{3,11},{10,2},{11,3},{4,12},{5,13},... | collective-permute-start | bytes 786440 | tf_op jit(solution)/shard_map/ppermute | solution.py:242
  116.2 6.3 %attend.6 = (bf16[128,8192]{1,0:T(8,128)(2,1)}, bf16[128,1024]{1,0:T(8,128)(2,1)S(1)}) custom-call(s32[42]{0:T(128)S(1)} %stack.106.scalars, f32[1]{0:T(128)S(6)} %tanh.3.gate_ref, bf16[64,1664]{1,0:T(8,128)(2,1)} %copy-done.2, bf16[64,1664]{1,0:T(8,128)(2,1)} %collective-permute-done.8.refs_1_, bf16[64,1664]{1,0:T(8,128)(2,1)} %copy-done.7, ...), custom_call_target="tpu_custom_call" | custom-call | flops 1744830464 | bytes 4194304 | tf_op jit(solution)/shard_map/attend/pallas_call | solution.py:177
  122.6 5.6 %attend.7 = (bf16[128,8192]{1,0:T(8,128)(2,1)}, bf16[128,1024]{1,0:T(8,128)(2,1)S(1)}) custom-call(s32[42]{0:T(128)S(1)} %stack.106.scalars, f32[1]{0:T(128)S(6)} %tanh.3.gate_ref, bf16[64,1664]{1,0:T(8,128)(2,1)S(1)} %sum_parts.3.refs_0_, bf16[64,1664]{1,0:T(8,128)(2,1)S(1)} %collective-permute-done.14.refs_1_, ...), custom_call_target="tpu_custom_call", output_to_operand_aliasing={{0}: (8, {})} | custom-call | flops 1744830464 | bytes 4194304 | tf_op jit(solution)/shard_map/attend/pallas_call | solution.py:177
  128.3 0.6 collective-permute-start.22
  128.8 1.7 %collective-permute-done.19.refs_2_ = bf16[128,1024]{1,0:T(8,128)(2,1)S(1)} collective-permute-done((bf16[128,1024]{1,0:T(8,128)(2,1)S(1)}, bf16[128,1024]{1,0:T(8,128)(2,1)S(1)}, u32[]{:S(2)}, u32[]{:S(2)}) %collective-permute-start.19) | collective-permute-done | bytes 262176 | tf_op jit(solution)/shard_map/ppermute | solution.py:242
  130.6 1.7 %place.1 = bf16[128,8192]{1,0:T(8,128)(2,1)} custom-call(s32[42]{0:T(128)S(1)} %stack.106.scalars, bf16[128,1024]{1,0:T(8,128)(2,1)S(1)} %collective-permute-done.12.refs_0_, bf16[128,1024]{1,0:T(8,128)(2,1)S(1)} %collective-permute-done.13.refs_1_, bf16[128,1024]{1,0:T(8,128)(2,1)S(1)} %collective-permute-done.19.refs_2_, ...), custom_call_target="tpu_custom_call", output_to_operand_aliasing={{}: (7, {})} | custom-call | bytes 1048576 | tf_op jit(solution)/shard_map/place/pallas_call | solution.py:216
  (36 shorter events, 0.5 us)
Async XLA Ops:
  0.0 23.2 %collective-permute-start.3 = (bf16[480,1664]{1,0:T(8,128)(2,1)}, bf16[480,1664]{1,0:T(8,128)(2,1)S(1)}, u32[]{:S(2)}, u32[]{:S(2)}) collective-permute-start(bf16[480,1664]{1,0:T(8,128)(2,1)} %bitcast.28), channel_id=1, source_target_pairs={{0,1},{1,0},{2,3},{3,2},{4,5},{5,4},{6,7},{7,6},{8,9},{9,8},{10,11... | collective-permute-start | bytes 4792328 | tf_op jit(solution)/shard_map/ppermute | solution.py:258
  2.5 5.6 %collective-permute-start.1 = (bf16[256,480]{1,0:T(8,128)(2,1)S(1)}, bf16[256,480]{1,0:T(8,128)(2,1)S(1)}, u32[]{:S(2)}, u32[]{:S(2)}) collective-permute-start(bf16[256,480]{1,0:T(8,128)(2,1)S(1)} %bitcast.33), channel_id=1, source_target_pairs={{0,64},{1,0},{16,80},{17,16},{32,96},{33,32},{48,112},{49,48},{64,... | collective-permute-start | bytes 737288 | tf_op jit(solution)/shard_map/ppermute | solution.py:257
  2.6 8.0 %collective-permute-start = (bf16[256,480]{1,0:T(8,128)(2,1)S(1)}, bf16[256,480]{1,0:T(8,128)(2,1)S(1)}, u32[]{:S(2)}, u32[]{:S(2)}) collective-permute-start(bf16[256,480]{1,0:T(8,128)(2,1)S(1)} %bitcast.34), channel_id=1, source_target_pairs={{0,0},{1,64},{16,16},{17,80},{32,32},{33,96},{48,48},{49,112},{64,... | collective-permute-start | bytes 737288 | tf_op jit(solution)/shard_map/ppermute | solution.py:257
  11.5 15.0 %collective-permute-start.2 = (bf16[2,256,480]{2,1,0:T(8,128)(2,1)}, bf16[2,256,480]{2,1,0:T(8,128)(2,1)}, u32[]{:S(2)}, u32[]{:S(2)}) collective-permute-start(bf16[2,256,480]{2,1,0:T(8,128)(2,1)} %pad_maximum_fusion.w_ref), channel_id=1, source_target_pairs={{0,16},{16,32},{32,48},{48,0},{1,17},{17,33},{33,49},{49,1},{2,18}... | collective-permute-start | bytes 1474568 | tf_op jit(solution)/shard_map/ppermute | solution.py:259
  13.2 16.4 %collective-permute-start.5 = (bf16[2,256,480]{2,1,0:T(8,128)(2,1)}, bf16[2,256,480]{2,1,0:T(8,128)(2,1)}, u32[]{:S(2)}, u32[]{:S(2)}) collective-permute-start(bf16[2,256,480]{2,1,0:T(8,128)(2,1)} %pad_maximum_fusion.w_ref), channel_id=1, source_target_pairs={{0,48},{16,0},{32,16},{48,32},{1,49},{17,1},{33,17},{49,33},{2,50}... | collective-permute-start | bytes 1474568 | tf_op jit(solution)/shard_map/ppermute | solution.py:260
  15.3 7.9 %copy-start = (bf16[1,1664,480]{1,2,0:T(8,128)(2,1)S(1)}, bf16[1,1664,480]{1,2,0:T(8,128)(2,1)}, u32[]{:S(2)}) copy-start(bf16[1,1664,480]{1,2,0:T(8,128)(2,1)} %param.7) | copy-start | bytes 4792324
  18.3 11.3 %collective-permute-start.4 = (bf16[1,128,1024]{2,1,0:T(8,128)(2,1)}, bf16[1,128,1024]{2,1,0:T(8,128)(2,1)}, u32[]{:S(2)}, u32[]{:S(2)}) collective-permute-start(bf16[1,128,1024]{2,1,0:T(8,128)(2,1)} %get-tuple-element.53), channel_id=1, source_target_pairs={{0,8},{1,9},{8,0},{9,1},{2,10},{3,11},{10,2},{11,3},{4,12},{5,13},... | collective-permute-start | bytes 786440 | tf_op jit(solution)/shard_map/ppermute | solution.py:242
  29.6 28.3 %all-to-all-start = ((bf16[8,64,1664]{2,1,0:T(8,128)(2,1)}), bf16[8,64,1664]{2,1,0:T(8,128)(2,1)}, u32[]{:S(2)}, u32[]{:S(2)}) async-start(bf16[8,64,1664]{2,1,0:T(8,128)(2,1)} %project.5), calls=%async_computation | async-start | bytes 3407872 | tf_op jit(solution)/shard_map/all_to_all | solution.py:294
  35.8 15.3 %collective-permute-start.6 = (bf16[2,256,480]{2,1,0:T(8,128)(2,1)}, bf16[2,256,480]{2,1,0:T(8,128)(2,1)S(1)}, u32[]{:S(2)}, u32[]{:S(2)}) collective-permute-start(bf16[2,256,480]{2,1,0:T(8,128)(2,1)} %pad_maximum_fusion.w_ref), channel_id=1, source_target_pairs={{0,32},{16,48},{32,0},{48,16},{1,33},{17,49},{33,1},{49,17},{2,34}... | collective-permute-start | bytes 1474568 | tf_op jit(solution)/shard_map/ppermute | solution.py:261
  38.7 14.4 %collective-permute-start.7 = (bf16[2,128,1024]{2,1,0:T(8,128)(2,1)S(1)}, bf16[2,128,1024]{2,1,0:T(8,128)(2,1)S(1)}, u32[]{:S(2)}, u32[]{:S(2)}) collective-permute-start(bf16[2,128,1024]{2,1,0:T(8,128)(2,1)S(1)} %pad_maximum_fusion.1), channel_id=1, source_target_pairs={{0,1},{1,0},{8,9},{9,8},{2,3},{3,2},{10,11},{11,10},{4,5},{5,4},{1... | collective-permute-start | bytes 1572872 | tf_op jit(solution)/shard_map/ppermute | solution.py:242
  53.1 0.8 copy-start.3
  57.9 27.0 %all-to-all-start.1 = ((bf16[8,64,1664]{2,1,0:T(8,128)(2,1)}), bf16[8,64,1664]{2,1,0:T(8,128)(2,1)S(1)}, u32[]{:S(2)}, u32[]{:S(2)}) async-start(bf16[8,64,1664]{2,1,0:T(8,128)(2,1)} %project.7), calls=%async_computation.1 | async-start | bytes 3407872 | tf_op jit(solution)/shard_map/all_to_all | solution.py:298
  62.6 1.8 %copy-start.5 = (bf16[1,128,1024]{2,1,0:T(8,128)(2,1)S(1)}, bf16[1,128,1024]{2,1,0:T(8,128)(2,1)}, u32[]{:S(2)}) copy-start(bf16[1,128,1024]{2,1,0:T(8,128)(2,1)} %get-tuple-element.33) | copy-start | bytes 786436
  64.4 32.8 %copy-start.2 = (bf16[64,1664]{1,0:T(8,128)(2,1)}, bf16[64,1664]{1,0:T(8,128)(2,1)S(1)}, u32[]{:S(2)}) copy-start(bf16[64,1664]{1,0:T(8,128)(2,1)S(1)} %sum_parts.2.refs_0_) | copy-start | bytes 638980
  64.5 32.5 %collective-permute-start.11 = (bf16[1,128,1024]{2,1,0:T(8,128)(2,1)S(1)}, bf16[1,128,1024]{2,1,0:T(8,128)(2,1)S(1)}, u32[]{:S(2)}, u32[]{:S(2)}) collective-permute-start(bf16[1,128,1024]{2,1,0:T(8,128)(2,1)S(1)} %copy-done.5), channel_id=1, source_target_pairs={{0,9},{1,8},{8,1},{9,0},{2,11},{3,10},{10,3},{11,2},{4,13},{5,12},... | collective-permute-start | bytes 786440 | tf_op jit(solution)/shard_map/ppermute | solution.py:242
  68.3 20.4 %collective-permute-start.10 = (bf16[64,1664]{1,0:T(8,128)(2,1)S(1)}, bf16[64,1664]{1,0:T(8,128)(2,1)S(1)}, u32[]{:S(2)}, u32[]{:S(2)}) collective-permute-start(bf16[64,1664]{1,0:T(8,128)(2,1)S(1)} %sum_parts.2.refs_0_), channel_id=1, source_target_pairs={{0,4},{2,6},{4,0},{6,2},{1,5},{3,7},{5,1},{7,3},{8,12},{10,14},{12... | collective-permute-start | bytes 638984 | tf_op jit(solution)/shard_map/ppermute | solution.py:300
  71.0 23.0 %collective-permute-start.9 = (bf16[64,1664]{1,0:T(8,128)(2,1)S(1)}, bf16[64,1664]{1,0:T(8,128)(2,1)S(1)}, u32[]{:S(2)}, u32[]{:S(2)}) collective-permute-start(bf16[64,1664]{1,0:T(8,128)(2,1)S(1)} %sum_parts.2.refs_0_), channel_id=1, source_target_pairs={{0,6},{2,0},{4,2},{6,4},{1,7},{3,1},{5,3},{7,5},{8,14},{10,8},{12,... | collective-permute-start | bytes 638984 | tf_op jit(solution)/shard_map/ppermute | solution.py:300
  71.9 22.4 %collective-permute-start.8 = (bf16[64,1664]{1,0:T(8,128)(2,1)S(1)}, bf16[64,1664]{1,0:T(8,128)(2,1)}, u32[]{:S(2)}, u32[]{:S(2)}) collective-permute-start(bf16[64,1664]{1,0:T(8,128)(2,1)S(1)} %sum_parts.2.refs_0_), channel_id=1, source_target_pairs={{0,2},{2,4},{4,6},{6,0},{1,3},{3,5},{5,7},{7,1},{8,10},{10,12},{12... | collective-permute-start | bytes 638984 | tf_op jit(solution)/shard_map/ppermute | solution.py:300
  85.8 21.2 %collective-permute-start.17 = (bf16[1,128,1024]{2,1,0:T(8,128)(2,1)}, bf16[1,128,1024]{2,1,0:T(8,128)(2,1)S(1)}, u32[]{:S(2)}, u32[]{:S(2)}) collective-permute-start(bf16[1,128,1024]{2,1,0:T(8,128)(2,1)} %get-tuple-element.37), channel_id=1, source_target_pairs={{0,8},{1,9},{8,0},{9,1},{2,10},{3,11},{10,2},{11,3},{4,12},{5,13},... | collective-permute-start | bytes 786440 | tf_op jit(solution)/shard_map/ppermute | solution.py:242
  88.8 8.2 %copy-start.6 = (bf16[64,1664]{1,0:T(8,128)(2,1)}, bf16[64,1664]{1,0:T(8,128)(2,1)S(1)}, u32[]{:S(2)}) copy-start(bf16[64,1664]{1,0:T(8,128)(2,1)S(1)} %collective-permute-done.10.refs_3_) | copy-start | bytes 638980
  88.8 18.2 %collective-permute-start.18 = (bf16[1,128,1024]{2,1,0:T(8,128)(2,1)}, bf16[1,128,1024]{2,1,0:T(8,128)(2,1)S(1)}, u32[]{:S(2)}, u32[]{:S(2)}) collective-permute-start(bf16[1,128,1024]{2,1,0:T(8,128)(2,1)} %get-tuple-element.38), channel_id=1, source_target_pairs={{0,9},{1,8},{8,1},{9,0},{2,11},{3,10},{10,3},{11,2},{4,13},{5,12},... | collective-permute-start | bytes 786440 | tf_op jit(solution)/shard_map/ppermute | solution.py:242
  94.0 2.9 %copy-start.7 = (bf16[64,1664]{1,0:T(8,128)(2,1)}, bf16[64,1664]{1,0:T(8,128)(2,1)S(1)}, u32[]{:S(2)}) copy-start(bf16[64,1664]{1,0:T(8,128)(2,1)S(1)} %collective-permute-done.9.refs_2_) | copy-start | bytes 638980
  94.0 8.9 %collective-permute-start.16 = (bf16[64,1664]{1,0:T(8,128)(2,1)S(1)}, bf16[64,1664]{1,0:T(8,128)(2,1)S(1)}, u32[]{:S(2)}, u32[]{:S(2)}) collective-permute-start(bf16[64,1664]{1,0:T(8,128)(2,1)S(1)} %sum_parts.3.refs_0_), channel_id=1, source_target_pairs={{0,4},{2,6},{4,0},{6,2},{1,5},{3,7},{5,1},{7,3},{8,12},{10,14},{12... | collective-permute-start | bytes 638984 | tf_op jit(solution)/shard_map/ppermute | solution.py:305
  94.3 12.4 %collective-permute-start.15 = (bf16[64,1664]{1,0:T(8,128)(2,1)S(1)}, bf16[64,1664]{1,0:T(8,128)(2,1)S(1)}, u32[]{:S(2)}, u32[]{:S(2)}) collective-permute-start(bf16[64,1664]{1,0:T(8,128)(2,1)S(1)} %sum_parts.3.refs_0_), channel_id=1, source_target_pairs={{0,6},{2,0},{4,2},{6,4},{1,7},{3,1},{5,3},{7,5},{8,14},{10,8},{12,... | collective-permute-start | bytes 638984 | tf_op jit(solution)/shard_map/ppermute | solution.py:305
  96.9 10.1 %collective-permute-start.14 = (bf16[64,1664]{1,0:T(8,128)(2,1)S(1)}, bf16[64,1664]{1,0:T(8,128)(2,1)S(1)}, u32[]{:S(2)}, u32[]{:S(2)}) collective-permute-start(bf16[64,1664]{1,0:T(8,128)(2,1)S(1)} %sum_parts.3.refs_0_), channel_id=1, source_target_pairs={{0,2},{2,4},{4,6},{6,0},{1,3},{3,5},{5,7},{7,1},{8,10},{10,12},{12... | collective-permute-start | bytes 638984 | tf_op jit(solution)/shard_map/ppermute | solution.py:305
  103.0 25.3 %collective-permute-start.13 = (bf16[128,1024]{1,0:T(8,128)(2,1)S(1)}, bf16[128,1024]{1,0:T(8,128)(2,1)S(1)}, u32[]{:S(2)}, u32[]{:S(2)}) collective-permute-start(bf16[128,1024]{1,0:T(8,128)(2,1)S(1)} %get-tuple-element.35), channel_id=1, source_target_pairs={{0,9},{1,8},{8,1},{9,0},{2,11},{3,10},{10,3},{11,2},{4,13},{5,12},... | collective-permute-start | bytes 786440 | tf_op jit(solution)/shard_map/ppermute | solution.py:242
  106.7 9.5 %copy-start.1 = (bf16[2,128,1024]{2,1,0:T(8,128)(2,1)S(1)}, bf16[2,128,1024]{2,1,0:T(8,128)(2,1)}, u32[]{:S(2)}) copy-start(bf16[2,128,1024]{2,1,0:T(8,128)(2,1)} %pad_maximum_fusion.2.refs_4_) | copy-start | bytes 1572868
  106.7 9.5 %copy-start.4 = (bf16[2,128,1024]{2,1,0:T(8,128)(2,1)S(1)}, bf16[2,128,1024]{2,1,0:T(8,128)(2,1)}, u32[]{:S(2)}) copy-start(bf16[2,128,1024]{2,1,0:T(8,128)(2,1)} %copy-done.3) | copy-start | bytes 1572868
  106.7 22.1 %collective-permute-start.12 = (bf16[128,1024]{1,0:T(8,128)(2,1)S(1)}, bf16[128,1024]{1,0:T(8,128)(2,1)S(1)}, u32[]{:S(2)}, u32[]{:S(2)}) collective-permute-start(bf16[128,1024]{1,0:T(8,128)(2,1)S(1)} %get-tuple-element.34.refs_6_), channel_id=1, source_target_pairs={{0,8},{1,9},{8,0},{9,1},{2,10},{3,11},{10,2},{11,3},{4,12},{5,13},... | collective-permute-start | bytes 786440 | tf_op jit(solution)/shard_map/ppermute | solution.py:242
  112.0 16.9 %collective-permute-start.20 = (bf16[128,1024]{1,0:T(8,128)(2,1)S(1)}, bf16[128,1024]{1,0:T(8,128)(2,1)S(1)}, u32[]{:S(2)}, u32[]{:S(2)}) collective-permute-start(bf16[128,1024]{1,0:T(8,128)(2,1)S(1)} %get-tuple-element.40), channel_id=1, source_target_pairs={{0,9},{1,8},{8,1},{9,0},{2,11},{3,10},{10,3},{11,2},{4,13},{5,12},... | collective-permute-start | bytes 786440 | tf_op jit(solution)/shard_map/ppermute | solution.py:242
  114.3 16.3 %collective-permute-start.19 = (bf16[128,1024]{1,0:T(8,128)(2,1)S(1)}, bf16[128,1024]{1,0:T(8,128)(2,1)S(1)}, u32[]{:S(2)}, u32[]{:S(2)}) collective-permute-start(bf16[128,1024]{1,0:T(8,128)(2,1)S(1)} %get-tuple-element.39.refs_6_), channel_id=1, source_target_pairs={{0,8},{1,9},{8,0},{9,1},{2,10},{3,11},{10,2},{11,3},{4,12},{5,13},... | collective-permute-start | bytes 786440 | tf_op jit(solution)/shard_map/ppermute | solution.py:242
  122.6 8.0 %collective-permute-start.21 = (bf16[128,1024]{1,0:T(8,128)(2,1)S(1)}, bf16[128,1024]{1,0:T(8,128)(2,1)S(1)}, u32[]{:S(2)}, u32[]{:S(2)}) collective-permute-start(bf16[128,1024]{1,0:T(8,128)(2,1)S(1)} %get-tuple-element.43), channel_id=1, source_target_pairs={{0,1},{1,0},{8,9},{9,8},{2,3},{3,2},{10,11},{11,10},{4,5},{5,4},{1... | collective-permute-start | bytes 786440 | tf_op jit(solution)/shard_map/ppermute | solution.py:242
  128.3 2.3 %collective-permute-start.22 = (bf16[128,1024]{1,0:T(8,128)(2,1)S(1)}, bf16[128,1024]{1,0:T(8,128)(2,1)S(1)}, u32[]{:S(2)}, u32[]{:S(2)}) collective-permute-start(bf16[128,1024]{1,0:T(8,128)(2,1)S(1)} %get-tuple-element.45), channel_id=1, source_target_pairs={{0,1},{1,0},{8,9},{9,8},{2,3},{3,2},{10,11},{11,10},{4,5},{5,4},{1... | collective-permute-start | bytes 786440 | tf_op jit(solution)/shard_map/ppermute | solution.py:242
